TPU v7x, 128 devices: a whole 4x4x4 slice. The times are simulated.
128 devices in a mesh: tm: 4 (over y), space: 32 (over z, x, core).
Axes of the slice: x: 4, y: 4, z: 4, core: 2. Of those that a mesh axis runs over, the one named last changes fastest.
Arguments:
- spectra: bfloat16 [2, 8, 4, 64, 4, 4096], P(None, 'tm', None, None, None, 'space'), may hold values from -6 to 6
- weights: float32 [4, 4096], P(None, 'space'), may hold values from 0.25 to 4
Outputs:
- modes: bfloat16 [2, 8, 4, 64, 4, 4096], P(None, None, 'tm', None, None, 'space')
- upper: float32 [2, 8, 4, 64, 64], P(None, None, 'tm')
All inputs are finite; a program needn't handle non-finite values.
Results may differ from a plain program's by a relative error of at most 0.009.
Values may be sent and summed in bfloat16 or wider, within the bound.
No kernel may reach another device: no remote copies, remote signals or barrier semaphores. Data moves between devices by JAX's collectives and lax.ppermute only.
A program may use at most 128 MiB of HBM per device.

v0:
```python
import math

import jax
import jax.numpy as jnp
from jax import lax
from jax.sharding import PartitionSpec as P

HIGHEST = lax.Precision.HIGHEST
TWO_PI = 2.0 * math.pi


def partner_2(value, axis, distance):
    return lax.ppermute(value, axis, [(i, i ^ 1 << distance) for i in range(lax.axis_size(axis))])


def cholesky_upper(gram_real, gram_imag):
    width = gram_real.shape[0]
    counter = jnp.arange(width, dtype=jnp.int32)

    def cholesky_advance(column, carry):
        work_real, work_imag, upper_real, upper_imag = carry
        row_real = lax.dynamic_index_in_dim(work_real, column, 0, keepdims=False)
        row_imag = lax.dynamic_index_in_dim(work_imag, column, 0, keepdims=False)
        on_diag = (counter == column)[:, None]
        pivot = jnp.sqrt(jnp.sum(jnp.where(on_diag, row_real, 0.0), axis=0))
        row_real = jnp.where((counter >= column)[:, None], row_real, 0.0) / pivot
        row_imag = jnp.where((counter > column)[:, None], row_imag, 0.0) / pivot
        work_real = work_real - (
            row_real[:, None] * row_real[None] + row_imag[:, None] * row_imag[None]
        )
        work_imag = work_imag - (
            row_real[:, None] * row_imag[None] - row_imag[:, None] * row_real[None]
        )
        on_row = (counter == column)[:, None, None]
        upper_real = upper_real + jnp.where(on_row, row_real[None], 0.0)
        upper_imag = upper_imag + jnp.where(on_row, row_imag[None], 0.0)
        return (work_real, work_imag, upper_real, upper_imag)

    zeros = jnp.zeros_like(gram_real)
    result = lax.fori_loop(
        0, width, cholesky_advance, (gram_real, gram_imag, zeros, zeros), unroll=16
    )
    return (result[2], result[3])


def upper_inverse(upper_real, upper_imag):
    width = upper_real.shape[0]
    counter = jnp.arange(width, dtype=jnp.int32)

    def upper_advance(offset, carry):
        inverse_real, inverse_imag = carry
        column = width - 1 - offset
        row_real = lax.dynamic_index_in_dim(upper_real, column, 0, keepdims=False)
        row_imag = lax.dynamic_index_in_dim(upper_imag, column, 0, keepdims=False)
        on_diag = (counter == column)[:, None]
        pivot = jnp.sum(jnp.where(on_diag, row_real, 0.0), axis=0)
        sum_real = jnp.sum(
            row_real[:, None] * inverse_real - row_imag[:, None] * inverse_imag, axis=0
        )
        sum_imag = jnp.sum(
            row_real[:, None] * inverse_imag + row_imag[:, None] * inverse_real, axis=0
        )
        unit = jnp.where(on_diag, 1.0, 0.0).astype(upper_real.dtype)
        new_real = (unit - sum_real) / pivot
        new_imag = -sum_imag / pivot
        on_row = (counter == column)[:, None, None]
        inverse_real = inverse_real + jnp.where(on_row, new_real[None], 0.0)
        inverse_imag = inverse_imag + jnp.where(on_row, new_imag[None], 0.0)
        return (inverse_real, inverse_imag)

    zeros = jnp.zeros_like(upper_real)
    return lax.fori_loop(0, width, upper_advance, (zeros, zeros), unroll=16)


def data_gram(data_real, data_imag, row_weight):
    weighted_real = data_real * row_weight
    weighted_imag = data_imag * row_weight
    gram_real = jnp.einsum(
        "bcs,bds->cdb", weighted_real, data_real, precision=HIGHEST
    ) + jnp.einsum("bcs,bds->cdb", weighted_imag, data_imag, precision=HIGHEST)
    gram_imag = jnp.einsum(
        "bcs,bds->cdb", weighted_real, data_imag, precision=HIGHEST
    ) - jnp.einsum("bcs,bds->cdb", weighted_imag, data_real, precision=HIGHEST)
    return (gram_real, gram_imag)


def gram_of_upper(upper_real, upper_imag):
    gram_real = jnp.einsum("jab,jcb->acb", upper_real, upper_real, precision=HIGHEST) + jnp.einsum(
        "jab,jcb->acb", upper_imag, upper_imag, precision=HIGHEST
    )
    gram_imag = jnp.einsum("jab,jcb->acb", upper_real, upper_imag, precision=HIGHEST) - jnp.einsum(
        "jab,jcb->acb", upper_imag, upper_real, precision=HIGHEST
    )
    return (gram_real, gram_imag)


def apply_inverse(data_real, data_imag, inverse_real, inverse_imag):
    mode_real = jnp.einsum("bcs,clb->bls", data_real, inverse_real, precision=HIGHEST) - jnp.einsum(
        "bcs,clb->bls", data_imag, inverse_imag, precision=HIGHEST
    )
    mode_imag = jnp.einsum("bcs,clb->bls", data_real, inverse_imag, precision=HIGHEST) + jnp.einsum(
        "bcs,clb->bls", data_imag, inverse_real, precision=HIGHEST
    )
    return jnp.stack([mode_real, mode_imag]).astype(jnp.bfloat16)


def on_device(spectra, weights):
    tm_index = lax.axis_index("tm")
    tm_count = lax.axis_size("tm")
    local_subs = spectra.shape[1]
    sub_count = local_subs * tm_count
    bins_all = spectra.shape[2]
    bins_local = bins_all // tm_count
    width = spectra.shape[3]
    fields = spectra.shape[4]
    freq_total = sub_count * bins_all
    sub_index = jnp.arange(sub_count, dtype=jnp.int32)
    received = lax.all_to_all(spectra, "tm", split_axis=2, concat_axis=1, tiled=True)
    items = received.shape[3]
    bin_global = tm_index * bins_local + jnp.arange(bins_local, dtype=jnp.int32)
    phase = (
        sub_index[None, :, None]
        * (bin_global[None, None, :] + bins_all * sub_index[:, None, None])
        % freq_total
    )
    angle = -TWO_PI / freq_total * phase.astype(jnp.float32)
    kernel_real = jnp.cos(angle)
    kernel_imag = jnp.sin(angle)
    flat = received.reshape(2, sub_count, bins_local, -1).astype(jnp.float32)
    data_real = jnp.einsum("qrm,rmx->qmx", kernel_real, flat[0], precision=HIGHEST) - jnp.einsum(
        "qrm,rmx->qmx", kernel_imag, flat[1], precision=HIGHEST
    )
    data_imag = jnp.einsum("qrm,rmx->qmx", kernel_real, flat[1], precision=HIGHEST) + jnp.einsum(
        "qrm,rmx->qmx", kernel_imag, flat[0], precision=HIGHEST
    )
    spectrum = jnp.stack([data_real, data_imag]).reshape(
        2, sub_count, bins_local, items, fields, -1
    )
    batch = sub_count * bins_local
    flat_data = spectrum.reshape(2, batch, width, -1)
    row_weight = weights.reshape(-1)
    gram_real, gram_imag = data_gram(flat_data[0], flat_data[1], row_weight)
    upper_real, upper_imag = cholesky_upper(gram_real, gram_imag)
    space_bits = lax.axis_size("space").bit_length() - 1
    for level_bit in range(space_bits):
        partner = partner_2(jnp.stack([upper_real, upper_imag]), "space", level_bit)
        own_real, own_imag = gram_of_upper(upper_real, upper_imag)
        far_real, far_imag = gram_of_upper(partner[0], partner[1])
        upper_real, upper_imag = cholesky_upper(own_real + far_real, own_imag + far_imag)
    inverse_real, inverse_imag = upper_inverse(upper_real, upper_imag)
    modes = apply_inverse(flat_data[0], flat_data[1], inverse_real, inverse_imag).reshape(
        spectrum.shape
    )
    upper = jnp.stack([jnp.transpose(upper_real, (2, 0, 1)), jnp.transpose(upper_imag, (2, 0, 1))])
    upper = upper.reshape(2, sub_count, bins_local, width, width)
    return (modes, upper)


def solution(mesh):
    placed = (P(None, "tm", None, None, None, "space"), P(None, "space"))
    return jax.shard_map(
        on_device,
        mesh=mesh,
        in_specs=placed,
        out_specs=(P(None, None, "tm", None, None, "space"), P(None, None, "tm", None, None)),
        check_vma=False,
    )
```

profile of v0, /device:TPU:0, one launch (start us, length us, event | category | flops | bytes accessed | tf_op | source)
XLA Modules:
  0.0 539.5 jit_solution(458820778013208920)
XLA Ops:
  0.6 2.6 copy.594
  3.2 4.5 all-to-all-start
  7.9 15.0 %all-to-all-done = bf16[2,2,4,64,4,128]{5,4,3,1,0,2:T(4,128)(2,1)S(1)} async-done(((bf16[2,2,4,64,4,128]{5,4,3,1,0,2:T(4,128)(2,1)}), bf16[2,2,4,64,4,128]{5,4,3,1,0,2:T(4,128)(2,1)S(1)}, u32[]{:S(2)}, u32[]{:S(2)}) %all-to-all-start) | async-done | bytes 1048608 | tf_op jit(solution)/shard_map/all_to_all | solution.py:118
  22.9 1.3 fusion.614
  24.1 1.4 reshape.13271
  29.2 2.2 fusion.484
  31.4 2.9 fusion.482
  34.4 3.0 fusion.515
  37.3 1.8 copy.601
  39.1 4.1 fusion.521
  44.3 71.7 %while.185 = (s32[]{:T(128)}, f32[64,64,8]{1,2,0:T(8,128)}, f32[64,64,8]{1,2,0:T(8,128)S(1)}, f32[64,64,8]{1,2,0:T(8,128)}, f32[64,64,8]{1,2,0:T(8,128)}, /*inde...) while((s32[]{:T(128)}, f32[64,64,8]{1,2,0:T(8,128)}, ...), condition=%wide.region_17.18_spmd.clone.clone.clone.clone, body=%wide.region_0.17_spmd.clone.clone.clone.clone.clone.sunk | while | flops 6441923 | bytes 11646952 | solution.py:40
  125.0 54.6 %while.186 = (s32[]{:T(128)}, f32[64,64,8]{1,2,0:T(8,128)S(1)}, f32[64,64,8]{1,2,0:T(8,128)S(1)}, f32[64,64,8]{1,2,0:T(8,128)S(1)}, f32[64,64,8]{1,2,0:T(8,128)S...) while((s32[]{:T(128)}, f32[64,64,8]{1,2,0:T(8,128)S(1)}, ...), condition=%wide.region_35.36_spmd.clone.clone.clone.clone, body=%wide.region_18.35_spmd.clone.clone.clone.clone.clone.sunk | while | flops 6441923 | bytes 9549688 | solution.py:40
  136.2 1.2 fusion.913
  149.9 1.2 fusion.913
  163.5 1.2 fusion.913
  177.2 1.2 fusion.913
  180.5 1.7 collective-permute-start.1
  183.5 11.3 %collective-permute-done.1 = f32[2,64,64,8]{2,1,3,0:T(8,128)S(1)} collective-permute-done((f32[2,64,64,8]{2,1,3,0:T(8,128)S(1)}, f32[2,64,64,8]{2,1,3,0:T(8,128)S(1)}, u32[]{:S(2)}, u32[]{:S(2)}) %collective-permute-start.1) | collective-permute-done | bytes 262176 | tf_op jit(solution)/shard_map/ppermute | solution.py:13
  197.5 54.6 %while.187 = (s32[]{:T(128)}, f32[64,64,8]{1,2,0:T(8,128)S(1)}, f32[64,64,8]{1,2,0:T(8,128)S(1)}, f32[64,64,8]{1,2,0:T(8,128)S(1)}, f32[64,64,8]{1,2,0:T(8,128)S...) while((s32[]{:T(128)}, f32[64,64,8]{1,2,0:T(8,128)S(1)}, ...), condition=%wide.region_53.54_spmd.clone.clone.clone.clone, body=%wide.region_36.53_spmd.clone.clone.clone.clone.clone.sunk | while | flops 6441923 | bytes 9549688 | solution.py:40
  208.7 1.2 fusion.947
  222.3 1.2 fusion.947
  236.0 1.2 fusion.947
  249.6 1.2 fusion.947
  253.0 3.3 collective-permute-start.2
  257.5 10.4 %collective-permute-done.2 = f32[2,64,64,8]{2,1,3,0:T(8,128)S(1)} collective-permute-done((f32[2,64,64,8]{2,1,3,0:T(8,128)S(1)}, f32[2,64,64,8]{2,1,3,0:T(8,128)S(1)}, u32[]{:S(2)}, u32[]{:S(2)}) %collective-permute-start.2) | collective-permute-done | bytes 262176 | tf_op jit(solution)/shard_map/ppermute | solution.py:13
  270.6 54.6 %while.188 = (s32[]{:T(128)}, f32[64,64,8]{1,2,0:T(8,128)S(1)}, f32[64,64,8]{1,2,0:T(8,128)S(1)}, f32[64,64,8]{1,2,0:T(8,128)S(1)}, f32[64,64,8]{1,2,0:T(8,128)S...) while((s32[]{:T(128)}, f32[64,64,8]{1,2,0:T(8,128)S(1)}, ...), condition=%wide.region_71.72_spmd.clone.clone.clone.clone, body=%wide.region_54.71_spmd.clone.clone.clone.clone.clone.sunk | while | flops 6441923 | bytes 9549688 | solution.py:40
  281.9 1.2 fusion.981
  295.5 1.2 fusion.981
  309.2 1.2 fusion.981
  326.1 2.4 collective-permute-start.3
  329.7 9.2 %collective-permute-done.3 = f32[2,64,64,8]{2,1,3,0:T(8,128)S(1)} collective-permute-done((f32[2,64,64,8]{2,1,3,0:T(8,128)S(1)}, f32[2,64,64,8]{2,1,3,0:T(8,128)S(1)}, u32[]{:S(2)}, u32[]{:S(2)}) %collective-permute-start.3) | collective-permute-done | bytes 262176 | tf_op jit(solution)/shard_map/ppermute | solution.py:13
  341.7 54.6 %while.189 = (s32[]{:T(128)}, f32[64,64,8]{1,2,0:T(8,128)S(1)}, f32[64,64,8]{1,2,0:T(8,128)S(1)}, f32[64,64,8]{1,2,0:T(8,128)S(1)}, f32[64,64,8]{1,2,0:T(8,128)S...) while((s32[]{:T(128)}, f32[64,64,8]{1,2,0:T(8,128)S(1)}, ...), condition=%wide.region_89.90_spmd.clone.clone.clone.clone, body=%wide.region_72.89_spmd.clone.clone.clone.clone.clone.sunk | while | flops 6441923 | bytes 9549688 | solution.py:40
  352.9 1.2 fusion.1015
  366.6 1.2 fusion.1015
  380.2 1.2 fusion.1015
  393.9 1.2 fusion.1015
  397.2 4.0 collective-permute-start.4
  402.4 8.3 %collective-permute-done.4 = f32[2,64,64,8]{2,1,3,0:T(8,128)S(1)} collective-permute-done((f32[2,64,64,8]{2,1,3,0:T(8,128)S(1)}, f32[2,64,64,8]{2,1,3,0:T(8,128)S(1)}, u32[]{:S(2)}, u32[]{:S(2)}) %collective-permute-start.4) | collective-permute-done | bytes 262176 | tf_op jit(solution)/shard_map/ppermute | solution.py:13
  413.5 54.6 %while.190 = (s32[]{:T(128)}, f32[64,64,8]{1,2,0:T(8,128)S(1)}, f32[64,64,8]{1,2,0:T(8,128)S(1)}, f32[64,64,8]{1,2,0:T(8,128)S(1)}, f32[64,64,8]{1,2,0:T(8,128)S...) while((s32[]{:T(128)}, f32[64,64,8]{1,2,0:T(8,128)S(1)}, ...), condition=%wide.region_107.108_spmd.clone.clone.clone.clone, body=%wide.region_90.107_spmd.clone.clone.clone.clone.clone.sunk | while | flops 6441923 | bytes 9549688 | solution.py:40
  424.7 1.2 fusion.1049
  468.2 2.0 copy.683
  470.2 1.9 copy.684
  472.1 57.3 %while.191 = (s32[]{:T(128)}, f32[64,64,8]{1,2,0:T(8,128)S(1)}, f32[64,64,8]{1,2,0:T(8,128)S(1)}, f32[64,64,8]{2,1,0:T(8,128)}, f32[64,64,8]{2,1,0:T(8,128)}, /*...) while((s32[]{:T(128)}, f32[64,64,8]{1,2,0:T(8,128)S(1)}, ...), condition=%wide.region_157.158_spmd.clone.clone.clone.clone, body=%wide.region_108.157_spmd.clone.clone.clone.clone.clone.sunk | while | flops 13274067 | bytes 6447504 | solution.py:72
  529.7 1.6 fusion.531
  531.4 1.6 fusion.529
  533.0 1.6 fusion.490
  534.6 1.6 fusion.491
  537.3 1.7 pad_maximum_fusion
  (3908 shorter events, 402.7 us)
Async XLA Ops:
  3.2 19.6 %all-to-all-start = ((bf16[2,2,4,64,4,128]{5,4,3,1,0,2:T(4,128)(2,1)}), bf16[2,2,4,64,4,128]{5,4,3,1,0,2:T(4,128)(2,1)S(1)}, u32[]{:S(2)}, u32[]{:S(2)}) async-start(bf16[2,2,4,64,4,128]{5,4,3,1,0,2:T(4,128)(2,1)} %copy.594), calls=%async_computation | async-start | bytes 2097152 | tf_op jit(solution)/shard_map/all_to_all | solution.py:118
  25.9 0.8 copy-start.17
  27.4 1.0 copy-start.18
  27.4 1.7 copy-start.19
  28.5 10.6 %copy-start.4 = (f32[8,32768]{1,0:T(8,128)}, f32[8,32768]{1,0:T(8,128)S(1)}, u32[]{:S(2)}) copy-start(f32[8,32768]{1,0:T(8,128)S(1)} %convolution_add_fusion) | copy-start | bytes 3145732
  29.2 10.0 %copy-start.2 = (f32[8,32768]{1,0:T(8,128)}, f32[8,32768]{1,0:T(8,128)S(1)}, u32[]{:S(2)}) copy-start(f32[8,32768]{1,0:T(8,128)S(1)} %convolution_subtract_fusion) | copy-start | bytes 3145732
  56.5 2.7 copy-start.9
  57.0 3.4 copy-start.12
  60.4 1.2 copy-start.10
  61.7 0.7 copy-start.13
  74.4 2.7 copy-start.9
  74.9 3.4 copy-start.12
  78.3 1.2 copy-start.10
  79.6 0.7 copy-start.13
  92.3 2.7 copy-start.9
  92.8 3.4 copy-start.12
  96.2 1.2 copy-start.10
  97.4 0.7 copy-start.13
  110.2 2.7 copy-start.9
  110.6 3.4 copy-start.12
  114.1 1.2 copy-start.10
  115.3 0.7 copy-start.13
  116.0 3.4 copy-start.11
  116.0 4.4 copy-start.14
  119.9 2.4 collective-permute-start
  122.9 2.1 copy-start.8
  180.5 14.2 %collective-permute-start.1 = (f32[2,64,64,8]{2,1,3,0:T(8,128)S(1)}, f32[2,64,64,8]{2,1,3,0:T(8,128)S(1)}, u32[]{:S(2)}, u32[]{:S(2)}) collective-permute-start(f32[2,64,64,8]{2,1,3,0:T(8,128)S(1)} %pad_maximum_fusion.2), channel_id=1, source_target_pairs={{0,2},{1,3},{2,0},{3,1},{4,6},{5,7},{6,4},{7,5},{8,10},{9,11},{10,... | collective-permute-start | bytes 786440 | tf_op jit(solution)/shard_map/ppermute | solution.py:13
  195.3 2.1 copy-start.7
  253.0 14.9 %collective-permute-start.2 = (f32[2,64,64,8]{2,1,3,0:T(8,128)S(1)}, f32[2,64,64,8]{2,1,3,0:T(8,128)S(1)}, u32[]{:S(2)}, u32[]{:S(2)}) collective-permute-start(f32[2,64,64,8]{2,1,3,0:T(8,128)S(1)} %pad_maximum_fusion.3), channel_id=1, source_target_pairs={{0,4},{1,5},{2,6},{3,7},{4,0},{5,1},{6,2},{7,3},{8,12},{9,13},{10,... | collective-permute-start | bytes 786440 | tf_op jit(solution)/shard_map/ppermute | solution.py:13
  268.5 2.1 copy-start.6
  326.1 12.9 %collective-permute-start.3 = (f32[2,64,64,8]{2,1,3,0:T(8,128)S(1)}, f32[2,64,64,8]{2,1,3,0:T(8,128)S(1)}, u32[]{:S(2)}, u32[]{:S(2)}) collective-permute-start(f32[2,64,64,8]{2,1,3,0:T(8,128)S(1)} %pad_maximum_fusion.4), channel_id=1, source_target_pairs={{0,8},{1,9},{2,10},{3,11},{4,12},{5,13},{6,14},{7,15},{8,0},{9,1},... | collective-permute-start | bytes 786440 | tf_op jit(solution)/shard_map/ppermute | solution.py:13
  397.2 13.5 %collective-permute-start.4 = (f32[2,64,64,8]{2,1,3,0:T(8,128)S(1)}, f32[2,64,64,8]{2,1,3,0:T(8,128)S(1)}, u32[]{:S(2)}, u32[]{:S(2)}) collective-permute-start(f32[2,64,64,8]{2,1,3,0:T(8,128)S(1)} %pad_maximum_fusion.5), channel_id=1, source_target_pairs={{0,16},{1,17},{2,18},{3,19},{4,20},{5,21},{6,22},{7,23},{8,24},{9,... | collective-permute-start | bytes 786440 | tf_op jit(solution)/shard_map/ppermute | solution.py:13
  411.3 2.1 copy-start.15
  411.3 2.1 copy-start.16
  468.1 4.0 copy-start
  468.2 4.0 copy-start.1
  472.1 57.6 %copy-start.3 = (f32[8,32768]{1,0:T(8,128)S(1)}, f32[8,32768]{1,0:T(8,128)}, u32[]{:S(2)}) copy-start(f32[8,32768]{1,0:T(8,128)} %copy-done.2) | copy-start | bytes 3145732
  529.7 3.2 copy-start.5
where the time goes:
time: 550 us; the launch traced here: 539 us
  other arithmetic  314 us (57%)
  local copies, waits for them, and re-layouts  96.5 us (18%)
  waiting for transfers between devices  54.9 us (10%)
  matrix products  41.4 us (8%)
  starting transfers between devices  16.4 us (3%)
  loops' own time  13.9 us (3%)
    sub x384, other arithmetic, cholesky_advance(): work_imag - (row_real[:, None] * row_imag[None] - row_imag[:, None] * row...  88.1 us
    reduce_sum x384, other arithmetic, cholesky_advance(): pivot = jnp.sqrt(jnp.sum(jnp.where(on_diag, row_real, 0.0), axis=0))  49.2 us
    ppermute x5, waiting for transfers between devices, partner_2(): lax.ppermute(value, axis, [(i, i ^ 1 << distance) for i in range(lax.axis...  39.9 us
    div x384, local copies, waits for them, and re-layouts, cholesky_advance(): row_real = jnp.where((counter >= column)[:, None], row_real, 0.0) / pivot  33.8 us
    div x384, local copies, waits for them, and re-layouts, cholesky_advance(): row_imag = jnp.where((counter > column)[:, None], row_imag, 0.0) / pivot  32.1 us
    div x384, other arithmetic, cholesky_advance(): row_real = jnp.where((counter >= column)[:, None], row_real, 0.0) / pivot  31.4 us
    mul x384, other arithmetic, cholesky_advance(): row_real[:, None] * row_real[None] + row_imag[:, None] * row_imag[None]  30 us
    add x24, other arithmetic, cholesky_advance(): upper_imag = upper_imag + jnp.where(on_row, row_imag[None], 0.0)  28.9 us
  transfers between devices with their start and end apart: 6, of which 6 were waited for; matrix products, arithmetic and copies ran while one was open for 1% of the time, Pallas kernels for 0%

commit v1 on v0

v1 whole, which is shorter than its diff:
```python
import math

import jax
import jax.numpy as jnp
import numpy as np
from jax import lax
from jax.experimental import pallas as pl
from jax.experimental.pallas import tpu as pltpu
from jax.sharding import PartitionSpec as P

SUBS = 8
WIDTH = 64
FIELDS = 4
LANES = 128
ROWS = WIDTH * FIELDS
F32 = jnp.float32
BF16 = jnp.bfloat16


def twiddle_table():
    table = np.zeros((4, 16), np.float32)
    for t in range(4):
        for d in range(4):
            angle = -2.0 * math.pi * (((t - d) % 4) * t) / 16.0
            table[t, 2 * d] = math.cos(angle)
            table[t, 2 * d + 1] = math.sin(angle)
        for q in range(4):
            angle = -2.0 * math.pi * (t / 32.0 + q / 8.0)
            table[t, 8 + 2 * q] = math.cos(angle)
            table[t, 9 + 2 * q] = math.sin(angle)
    return table


def phase_table():
    table = np.zeros((4, 16), np.float32)
    for t in range(4):
        for q in range(8):
            re, im = [(1, 0), (0, -1), (-1, 0), (0, 1)][(t * q) % 4]
            table[t, 2 * q] = re
            table[t, 2 * q + 1] = im
    return table


def split(value):
    high = value.astype(BF16)
    return high, (value - high.astype(F32)).astype(BF16)


def lane_iota(shape):
    return lax.broadcasted_iota(jnp.int32, shape, len(shape) - 1)


def gram_kernel(own, near1, near2, near3, weight16, twiddle, sh_ref, sl_ref, gram_ref, work):
    t = lax.axis_index("tm")
    root = jnp.sqrt(weight16[...])
    sources = (own, near1, near2, near3)
    tw = [(root * twiddle[t, 2 * d], root * twiddle[t, 2 * d + 1]) for d in range(4)]
    tq = [(twiddle[t, 8 + 2 * q], twiddle[t, 9 + 2 * q]) for q in range(4)]

    def transform(step, _):
        row = pl.multiple_of(step * 16, 16)
        rows = pl.ds(row, 16)
        radix = []
        for s in range(2):
            y = []
            for d in range(4):
                re = sources[d][0, s, rows, :].astype(F32)
                im = sources[d][1, s, rows, :].astype(F32)
                y.append((re * tw[d][0] - im * tw[d][1], re * tw[d][1] + im * tw[d][0]))
            a = (y[0][0] + y[2][0], y[0][1] + y[2][1])
            b = (y[0][0] - y[2][0], y[0][1] - y[2][1])
            c = (y[1][0] + y[3][0], y[1][1] + y[3][1])
            e = (y[1][0] - y[3][0], y[1][1] - y[3][1])
            radix.append(
                [
                    (a[0] + c[0], a[1] + c[1]),
                    (b[0] - e[1], b[1] + e[0]),
                    (a[0] - c[0], a[1] - c[1]),
                    (b[0] + e[1], b[1] - e[0]),
                ]
            )
        for q in range(4):
            x0 = radix[0][q]
            x1 = radix[1][q]
            v = (x1[0] * tq[q][0] - x1[1] * tq[q][1], x1[0] * tq[q][1] + x1[1] * tq[q][0])
            work[q, 0, rows, :] = x0[0] + v[0]
            work[q, 1, rows, :] = x0[1] + v[1]
            work[q + 4, 0, rows, :] = x0[0] - v[0]
            work[q + 4, 1, rows, :] = x0[1] - v[1]
        return 0

    lax.fori_loop(0, ROWS // 16, transform, 0)

    lane = lane_iota((WIDTH, LANES))
    line = lax.broadcasted_iota(jnp.int32, (WIDTH, LANES), 0)
    left = lane < WIDTH
    keep = (lane % WIDTH) >= line

    def one_gram(q):
        for part in range(2):
            for f in range(FIELDS):
                value = work[q, part, pl.ds(f, WIDTH, stride=FIELDS), :]
                high, low = split(value)
                sh_ref[q, part * WIDTH : (part + 1) * WIDTH, f * LANES : (f + 1) * LANES] = high
                sl_ref[q, part * WIDTH : (part + 1) * WIDTH, f * LANES : (f + 1) * LANES] = low
        high = sh_ref[q]
        both = jnp.concatenate([high, sl_ref[q]], axis=0)
        prod = lax.dot_general(both, high, (((1,), (1,)), ((), ())), preferred_element_type=F32)
        cross = prod[LANES:]
        full = prod[:LANES] + (cross + cross.T)
        low = pltpu.roll(full[WIDTH:], WIDTH, 1)
        return full[:WIDTH] + jnp.where(left, low, -low)

    def pair(index, _):
        first = one_gram(2 * index)
        second = one_gram(2 * index + 1)
        first_r = pltpu.roll(first, WIDTH, 1)
        second_r = pltpu.roll(second, WIDTH, 1)
        gram_ref[pl.ds(pl.multiple_of(index * WIDTH, WIDTH), WIDTH), :] = jnp.where(
            left, jnp.where(keep, first, first_r), jnp.where(keep, second_r, second)
        )
        return 0

    lax.fori_loop(0, SUBS // 2, pair, 0)


def lane_at(value, lane):
    return jnp.broadcast_to(value[:, lane : lane + 1], value.shape)


def factor_kernel(gram, sh_ref, sl_ref, weight, phase, modes_ref, upper_ref, work, spread):
    t = lax.axis_index("tm")
    wide = (WIDTH, LANES)
    lane = lane_iota(wide)
    column = lane % WIDTH
    line = lax.broadcasted_iota(jnp.int32, wide, 0)
    left = lane < WIDTH
    for pair in range(SUBS // 2):
        packed = gram[pair * WIDTH : (pair + 1) * WIDTH, :]
        turned = jnp.concatenate([packed, packed], axis=0).T
        work[pl.ds(2 * pair * WIDTH, WIDTH), :] = jnp.where(left, packed, -turned[:WIDTH])
        rolled = pltpu.roll(packed, WIDTH, 1)
        work[pl.ds((2 * pair + 1) * WIDTH, WIDTH), :] = jnp.where(left, rolled, -turned[WIDTH:])
    rows = [work[pl.ds(i, SUBS, stride=WIDTH), :] for i in range(WIDTH)]

    small = (SUBS, LANES)
    lane8 = lane_iota(small)
    sign = jnp.where(lane8 < WIDTH, 1.0, -1.0).astype(F32)
    zero = jnp.zeros(small, F32)

    def turn(value):
        return pltpu.roll(value, WIDTH, 1) * sign

    for k in range(WIDTH // 2):
        c0 = 2 * k
        c1 = c0 + 1
        a, b = rows[c0], rows[c1]
        at0 = (lane8 == c0) | (lane8 == WIDTH + c0)
        at1 = (lane8 == c1) | (lane8 == WIDTH + c1)
        p1 = lane_at(a, c0)
        ar = lane_at(a, c1)
        ai = lane_at(a, WIDTH + c1)
        p2 = lane_at(b, c1)
        one0 = jnp.where(lane8 == c0, 1.0, 0.0).astype(F32)
        one1 = jnp.where(lane8 == c1, 1.0, 0.0).astype(F32)
        ae = jnp.where(at0, one0, a)
        ae_t = turn(ae)
        b0 = jnp.where(at0, 0.0, b)
        b0_t = turn(b0)
        i1 = 1.0 / p1
        mr = ar * i1
        mi = ai * i1
        d = p2 - (ar * mr + ai * mi)
        i2 = 1.0 / d
        bn = b0 - mr * ae - mi * ae_t
        bn_t = b0_t - mr * ae_t + mi * ae
        be = jnp.where(at1, one1, bn)
        one1_t = jnp.where(lane8 == WIDTH + c1, -1.0, 0.0).astype(F32)
        be_t = jnp.where(at1, one1_t, bn_t)
        y1 = jnp.where(at1, 0.0, ae) * i1
        y1_t = jnp.where(at1, 0.0, ae_t) * i1
        y2 = be * i2
        y2_t = be_t * i2
        clear = at0 | at1
        for i in range(c0 + 2, WIDTH):
            rows[i] = (
                jnp.where(clear, 0.0, rows[i])
                - (lane_at(a, i) * y1 + lane_at(a, WIDTH + i) * y1_t)
                - (lane_at(bn, i) * y2 + lane_at(bn, WIDTH + i) * y2_t)
            )
        spread[c0 * SUBS : (c0 + 1) * SUBS, :] = ae * lax.rsqrt(p1)
        spread[c1 * SUBS : (c1 + 1) * SUBS, :] = be * lax.rsqrt(d)

    root = lax.rsqrt(weight[...])

    def emit(q, _):
        both = spread[pl.ds(q, WIDTH, stride=SUBS), :]
        inverse = jnp.where(column <= line, both, 0.0)
        diag = jnp.where(left, 1.0 / both, 0.0)
        upper = jnp.where(column > line, both, jnp.where(column == line, diag, 0.0))
        upper_ref[0, q] = upper[:, :WIDTH]
        upper_ref[1, q] = upper[:, WIDTH:]
        swapped = pltpu.roll(inverse, WIDTH, 1)
        swapped = jnp.where(left, -swapped, swapped)
        pr = phase[t, 2 * q]
        pi = phase[t, 2 * q + 1]
        lhs = jnp.concatenate([pr * inverse - pi * swapped, pr * swapped + pi * inverse], axis=0)
        lh, ll = split(lhs)
        sh = sh_ref[q]
        out = jnp.dot(lh, sh, preferred_element_type=F32)
        out = out + jnp.dot(ll, sh, preferred_element_type=F32)
        out = out + jnp.dot(lh, sl_ref[q], preferred_element_type=F32)
        for part in range(2):
            for f in range(FIELDS):
                block = out[part * WIDTH : (part + 1) * WIDTH, f * LANES : (f + 1) * LANES]
                work[pl.ds(part * ROWS + f, WIDTH, stride=FIELDS), :] = block * root[f : f + 1, :]
            modes_ref[part, q] = work[part * ROWS : (part + 1) * ROWS, :].astype(BF16)
        return 0

    lax.fori_loop(0, SUBS, emit, 0)


def vmem():
    return pl.BlockSpec(memory_space=pltpu.VMEM)


def smem():
    return pl.BlockSpec(memory_space=pltpu.SMEM)


def run_gram(own, near, weight16, table):
    return pl.pallas_call(
        gram_kernel,
        name="gram",
        out_shape=(
            jax.ShapeDtypeStruct((SUBS, LANES, FIELDS * LANES), BF16),
            jax.ShapeDtypeStruct((SUBS, LANES, FIELDS * LANES), BF16),
            jax.ShapeDtypeStruct((SUBS // 2 * WIDTH, LANES), F32),
        ),
        in_specs=[vmem()] * 5 + [smem()],
        out_specs=(vmem(), vmem(), vmem()),
        scratch_shapes=[pltpu.VMEM((SUBS, 2, ROWS, LANES), F32)],
        compiler_params=pltpu.CompilerParams(vmem_limit_bytes=32 * 1024 * 1024),
    )(own, *near, weight16, table)


def run_factor(gram, sh, sl, weights, table):
    return pl.pallas_call(
        factor_kernel,
        name="factor",
        out_shape=(
            jax.ShapeDtypeStruct((2, SUBS, ROWS, LANES), BF16),
            jax.ShapeDtypeStruct((2, SUBS, WIDTH, WIDTH), F32),
        ),
        in_specs=[vmem()] * 4 + [smem()],
        out_specs=(vmem(), vmem()),
        scratch_shapes=[
            pltpu.VMEM((SUBS * WIDTH, LANES), F32),
            pltpu.VMEM((SUBS * WIDTH, LANES), F32),
        ],
        compiler_params=pltpu.CompilerParams(vmem_limit_bytes=32 * 1024 * 1024),
    )(gram, sh, sl, weights, table)


def space_perm(along, shift):
    pairs = []
    for i in range(32):
        z, x, core = i // 8, i // 2 % 4, i % 2
        if along == "x":
            x = (x + shift) % 4
        elif along == "z":
            z = (z + shift) % 4
        else:
            core = 1 - core
        pairs.append((i, (z * 4 + x) * 2 + core))
    return pairs


def sum_over_space(value):
    value = value + lax.ppermute(value, "space", space_perm("core", 1))
    for along in ("x", "z"):
        far = [lax.ppermute(value, "space", space_perm(along, d)) for d in (1, 3, 2)]
        value = (value + far[2]) + (far[0] + far[1])
    return value


def on_device(spectra, weights):
    t = lax.axis_index("tm")
    flat = spectra.reshape(2, 2, 4, ROWS, LANES)
    own = lax.dynamic_index_in_dim(flat, t, 2, keepdims=False)
    near = []
    for d in range(1, 4):
        piece = lax.dynamic_index_in_dim(flat, (t + d) % 4, 2, keepdims=False)
        near.append(lax.ppermute(piece, "tm", [(i, (i + d) % 4) for i in range(4)]))
    weight16 = jnp.tile(weights, (4, 1))
    sh, sl, gram = run_gram(own, near, weight16, jnp.asarray(twiddle_table()))
    gram = sum_over_space(gram)
    modes, upper = run_factor(gram, sh, sl, weights, jnp.asarray(phase_table()))
    return (
        modes.reshape(2, SUBS, 1, WIDTH, FIELDS, LANES),
        upper.reshape(2, SUBS, 1, WIDTH, WIDTH),
    )


def solution(mesh):
    placed = (P(None, "tm", None, None, None, "space"), P(None, "space"))
    return jax.shard_map(
        on_device,
        mesh=mesh,
        in_specs=placed,
        out_specs=(P(None, None, "tm", None, None, "space"), P(None, None, "tm", None, None)),
        check_vma=False,
    )
```

time: 550 us -> 64.9 us (0.12); the launches traced: 539 us -> 64.7 us
  other arithmetic: 314 us -> 0.07 us
  local copies, waits for them, and re-layouts: 96.5 us -> 2.66 us
  matrix products: 41.4 us -> 0 us
  waiting for transfers between devices: 54.9 us -> 27.3 us
  Pallas kernels: 0 us -> 17.9 us
  loops' own time: 13.9 us -> 0 us
    reduce_sum x464 -> x0, other arithmetic: 92.3 us -> none  [the longest x384 49.2 us: cholesky_advance(): pivot = jnp.sqrt(jnp.sum(jnp.where(on_diag, row_real, 0.0), axis=0))]
    sub x384 -> x0, other arithmetic: 88.1 us -> none  [cholesky_advance(): work_imag - (row_real[:, None] * row_imag[None] - row_imag[:, None] * row...]
    div x768 -> x0, local copies, waits for them, and re-layouts: 66 us -> none  [the longest x384 33.8 us: cholesky_advance(): row_real = jnp.where((counter >= column)[:, None], row_real, 0.0) / pivot]
    add x53 -> x3, other arithmetic: 59.9 us -> 0.07 us  [the longest x2 0.06 us: sum_over_space(): value = value + far[2] + (far[0] + far[1])]
    dot_general x52 -> x0, matrix products: 41.4 us -> none  [the longest x10 5.01 us: gram_of_upper(): jnp.einsum('jab,jcb->acb', upper_real, upper_imag, precision=HIGHEST)]
    div x448 -> x0, other arithmetic: 36.1 us -> none  [the longest x384 31.4 us: cholesky_advance(): row_real = jnp.where((counter >= column)[:, None], row_real, 0.0) / pivot]
    mul x384 -> x0, other arithmetic: 30 us -> none  [cholesky_advance(): row_real[:, None] * row_real[None] + row_imag[:, None] * row_imag[None]]
    pallas_call x0 -> x2, Pallas kernels: none -> 17.9 us  [the longest x1 14.4 us: run_factor(): pl.pallas_call(factor_kernel, name='factor', out_shape=(jax.ShapeDtypeStr...]
  transfers between devices with their start and end apart: 6 -> 10, of which waited for: 6 -> 7; matrix products, arithmetic and copies ran while one was open for 1% -> 0% of each run, Pallas kernels for 0% -> 0%
where the time goes in v1:
time: 64.9 us; the launch traced here: 64.7 us
  waiting for transfers between devices  27.3 us (42%)
  Pallas kernels  17.9 us (28%)
  starting transfers between devices  15.9 us (24%)
  local copies, waits for them, and re-layouts  2.66 us (4%)
  between operations  0.73 us (1%)
    pallas_call x1, Pallas kernels, run_factor(): pl.pallas_call(factor_kernel, name='factor', out_shape=(jax.ShapeDtypeStr...  14.4 us
    ppermute x3, waiting for transfers between devices, on_device(): near.append(lax.ppermute(piece, 'tm', [(i, (i + d) % 4) for i in range(4)]))  13.3 us
    ppermute x6, waiting for transfers between devices, sum_over_space(): lax.ppermute(value, 'space', space_perm(along, d))  12.7 us
    ppermute x6, starting transfers between devices, sum_over_space(): lax.ppermute(value, 'space', space_perm(along, d))  11.1 us
    ppermute x3, starting transfers between devices, on_device(): near.append(lax.ppermute(piece, 'tm', [(i, (i + d) % 4) for i in range(4)]))  4.77 us
    pallas_call x1, Pallas kernels, run_gram(): pl.pallas_call(gram_kernel, name='gram', out_shape=(jax.ShapeDtypeStruct(...  3.55 us
    unnamed x6, local copies, waits for them, and re-layouts  1.37 us
    ppermute x1, waiting for transfers between devices, sum_over_space(): value = value + lax.ppermute(value, 'space', space_perm('core', 1))  1.33 us
  transfers between devices with their start and end apart: 10, of which 7 were waited for; matrix products, arithmetic and copies ran while one was open for 0% of the time, Pallas kernels for 0%

profile of v1, /device:TPU:0, one launch (start us, length us, event | category | flops | bytes accessed | tf_op | source)
XLA Modules:
  0.0 64.7 jit_solution(3331863844190974803)
XLA Ops:
  0.7 1.3 %dynamic-slice_bitcast_fusion = (bf16[2,2,256,128]{3,2,1,0:T(8,128)(2,1)S(1)}, bf16[2,2,256,128]{3,2,1,0:T(8,128)(2,1)S(1)}, bf16[2,2,256,128]{3,2,1,0:T(8,128)(2,1)S(1)}, bf16[2,2,256,128]{3,2,1,0:T(8,128)(2,1)S(1)}) fusion(bf16[2,2,4,256,128]{4,3,2,1,0:T(8,128)(2,1)} %bitcast.25, s32[]{:T(128)S(6)} %select_n.34, s32[]{:T(128)S(6)} %select_n.32, ...), kind=kLoop, calls=%fused_computation | loop fusion | bytes 2097168 | tf_op jit(solution)/shard_map/jit(dynamic_index_in_dim)/squeeze | solution.py:293
  2.0 0.0 copy-start
  2.0 3.2 %collective-permute-start.2 = (bf16[2,2,256,128]{3,2,1,0:T(8,128)(2,1)S(1)}, bf16[2,2,256,128]{3,2,1,0:T(8,128)(2,1)S(1)}, u32[]{:S(2)}, u32[]{:S(2)}) collective-permute-start(bf16[2,2,256,128]{3,2,1,0:T(8,128)(2,1)S(1)} %get-tuple-element.14), channel_id=1, source_target_pairs={{0,96},{32,0},{64,32},{96,64},{1,97},{33,1},{65,33},{97,65},{2,98}... | collective-permute-start | bytes 786440 | tf_op jit(solution)/shard_map/ppermute | solution.py:294
  5.2 0.6 collective-permute-start.1
  5.8 1.0 %collective-permute-start = (bf16[2,2,256,128]{3,2,1,0:T(8,128)(2,1)S(1)}, bf16[2,2,256,128]{3,2,1,0:T(8,128)(2,1)S(1)}, u32[]{:S(2)}, u32[]{:S(2)}) collective-permute-start(bf16[2,2,256,128]{3,2,1,0:T(8,128)(2,1)S(1)} %get-tuple-element.16), channel_id=1, source_target_pairs={{0,32},{32,64},{64,96},{96,0},{1,33},{33,65},{65,97},{97,1},{2,34}... | collective-permute-start | bytes 786440 | tf_op jit(solution)/shard_map/ppermute | solution.py:294
  6.8 9.6 %collective-permute-done.2.near3 = bf16[2,2,256,128]{3,2,1,0:T(8,128)(2,1)S(1)} collective-permute-done((bf16[2,2,256,128]{3,2,1,0:T(8,128)(2,1)S(1)}, bf16[2,2,256,128]{3,2,1,0:T(8,128)(2,1)S(1)}, u32[]{:S(2)}, u32[]{:S(2)}) %collective-permute-start.2) | collective-permute-done | bytes 262176 | tf_op jit(solution)/shard_map/ppermute | solution.py:294
  16.3 0.0 collective-permute-done.1.near2
  16.3 3.7 %collective-permute-done.near1 = bf16[2,2,256,128]{3,2,1,0:T(8,128)(2,1)S(1)} collective-permute-done((bf16[2,2,256,128]{3,2,1,0:T(8,128)(2,1)S(1)}, bf16[2,2,256,128]{3,2,1,0:T(8,128)(2,1)S(1)}, u32[]{:S(2)}, u32[]{:S(2)}) %collective-permute-start) | collective-permute-done | bytes 262176 | tf_op jit(solution)/shard_map/ppermute | solution.py:294
  20.0 0.0 copy-done
  20.1 0.0 copy-start.1
  20.1 0.7 %copy-done.1 = f32[4,16]{1,0:T(4,128)S(1)} copy-done((f32[4,16]{1,0:T(4,128)S(1)}, f32[4,16]{1,0:T(4,128)}, u32[]{:S(2)}) %copy-start.1) | copy-done | bytes 280
  20.7 3.6 %gram.1 = (bf16[8,128,512]{2,1,0:T(8,128)(2,1)S(1)}, bf16[8,128,512]{2,1,0:T(8,128)(2,1)S(1)}, f32[256,128]{1,0:T(8,128)S(1)}) custom-call(bf16[2,2,256,128]{3,2,1,0:T(8,128)(2,1)S(1)} %get-tuple-element.17.own, bf16[2,2,256,128]{3,2,1,0:T(8,128)(2,1)S(1)} %collective-permute-done.near1, bf16[2,2,256,128]{3,2,1,0:T(8,128)(2,1)S(1)} %collective-permute-done.1.near2, ...), custom_call_target="tpu_custom_call" | custom-call | tf_op jit(solution)/shard_map/gram/pallas_call | solution.py:232
  24.3 0.1 collective-permute-start.3
  24.4 1.3 %collective-permute-done.3 = f32[256,128]{1,0:T(8,128)S(1)} collective-permute-done((f32[256,128]{1,0:T(8,128)S(1)}, f32[256,128]{1,0:T(8,128)S(1)}, u32[]{:S(2)}, u32[]{:S(2)}) %collective-permute-start.3) | collective-permute-done | bytes 131104 | tf_op jit(solution)/shard_map/ppermute | solution.py:280
  25.7 2.8 %collective-permute-start.6 = (f32[256,128]{1,0:T(8,128)S(1)}, f32[256,128]{1,0:T(8,128)S(1)}, u32[]{:S(2)}, u32[]{:S(2)}) collective-permute-start(f32[256,128]{1,0:T(8,128)S(1)} %add.63), channel_id=1, source_target_pairs={{0,6},{1,7},{2,0},{3,1},{4,2},{5,3},{6,4},{7,5},{8,14},{9,15},{10,... | collective-permute-start | bytes 393224 | tf_op jit(solution)/shard_map/ppermute | solution.py:282
  28.6 0.0 collective-permute-start.5
  28.6 2.3 %collective-permute-start.4 = (f32[256,128]{1,0:T(8,128)S(1)}, f32[256,128]{1,0:T(8,128)S(1)}, u32[]{:S(2)}, u32[]{:S(2)}) collective-permute-start(f32[256,128]{1,0:T(8,128)S(1)} %add.63), channel_id=1, source_target_pairs={{0,4},{1,5},{2,6},{3,7},{4,0},{5,1},{6,2},{7,3},{8,12},{9,13},{10,... | collective-permute-start | bytes 393224 | tf_op jit(solution)/shard_map/ppermute | solution.py:282
  30.9 0.8 %collective-permute-done.6 = f32[256,128]{1,0:T(8,128)S(1)} collective-permute-done((f32[256,128]{1,0:T(8,128)S(1)}, f32[256,128]{1,0:T(8,128)S(1)}, u32[]{:S(2)}, u32[]{:S(2)}) %collective-permute-start.6) | collective-permute-done | bytes 131104 | tf_op jit(solution)/shard_map/ppermute | solution.py:282
  31.6 6.2 %collective-permute-done.5 = f32[256,128]{1,0:T(8,128)S(1)} collective-permute-done((f32[256,128]{1,0:T(8,128)S(1)}, f32[256,128]{1,0:T(8,128)S(1)}, u32[]{:S(2)}, u32[]{:S(2)}) %collective-permute-start.5) | collective-permute-done | bytes 131104 | tf_op jit(solution)/shard_map/ppermute | solution.py:282
  37.9 0.0 collective-permute-done.4
  37.9 4.1 %collective-permute-start.9 = (f32[256,128]{1,0:T(8,128)S(1)}, f32[256,128]{1,0:T(8,128)S(1)}, u32[]{:S(2)}, u32[]{:S(2)}) collective-permute-start(f32[256,128]{1,0:T(8,128)S(1)} %add_add_fusion.1), channel_id=1, source_target_pairs={{0,24},{1,25},{2,26},{3,27},{4,28},{5,29},{6,30},{7,31},{8,0},{9,1... | collective-permute-start | bytes 393224 | tf_op jit(solution)/shard_map/ppermute | solution.py:282
  42.0 0.0 collective-permute-start.8
  42.0 1.9 %collective-permute-start.7 = (f32[256,128]{1,0:T(8,128)S(1)}, f32[256,128]{1,0:T(8,128)S(1)}, u32[]{:S(2)}, u32[]{:S(2)}) collective-permute-start(f32[256,128]{1,0:T(8,128)S(1)} %add_add_fusion.1), channel_id=1, source_target_pairs={{0,16},{1,17},{2,18},{3,19},{4,20},{5,21},{6,22},{7,23},{8,24},{9,... | collective-permute-start | bytes 393224 | tf_op jit(solution)/shard_map/ppermute | solution.py:282
  43.9 2.0 %collective-permute-done.9 = f32[256,128]{1,0:T(8,128)S(1)} collective-permute-done((f32[256,128]{1,0:T(8,128)S(1)}, f32[256,128]{1,0:T(8,128)S(1)}, u32[]{:S(2)}, u32[]{:S(2)}) %collective-permute-start.9) | collective-permute-done | bytes 131104 | tf_op jit(solution)/shard_map/ppermute | solution.py:282
  45.9 3.7 %collective-permute-done.8 = f32[256,128]{1,0:T(8,128)S(1)} collective-permute-done((f32[256,128]{1,0:T(8,128)S(1)}, f32[256,128]{1,0:T(8,128)S(1)}, u32[]{:S(2)}, u32[]{:S(2)}) %collective-permute-start.8) | collective-permute-done | bytes 131104 | tf_op jit(solution)/shard_map/ppermute | solution.py:282
  49.6 0.0 collective-permute-done.7
  49.6 0.0 copy-start.2
  49.6 0.7 %copy-done.2 = f32[4,16]{1,0:T(4,128)S(1)} copy-done((f32[4,16]{1,0:T(4,128)S(1)}, f32[4,16]{1,0:T(4,128)}, u32[]{:S(2)}) %copy-start.2) | copy-done | bytes 280
  50.3 14.4 %factor.1 = (bf16[2,8,256,128]{3,2,1,0:T(8,128)(2,1)}, f32[2,8,64,64]{3,2,1,0:T(8,128)}) custom-call(f32[256,128]{1,0:T(8,128)S(1)} %add_add_fusion.gram, bf16[8,128,512]{2,1,0:T(8,128)(2,1)S(1)} %get-tuple-element.8.sh_ref, bf16[8,128,512]{2,1,0:T(8,128)(2,1)S(1)} %get-tuple-element.9.sl_ref, f32[4,128]{1,0:T(4,128)S(1)} %copy-done, f32[4,16]{1,0:T(4,128)S(1)} %copy-done.2), custom_call_target="tpu_custom_call" | custom-call | tf_op jit(solution)/shard_map/factor/pallas_call | solution.py:248
  (4 shorter events, 0.1 us)
Async XLA Ops:
  2.0 18.1 %copy-start = (f32[4,128]{1,0:T(4,128)S(1)}, f32[4,128]{1,0:T(4,128)}, u32[]{:S(2)}) copy-start(f32[4,128]{1,0:T(4,128)} %weight.1) | copy-start | bytes 6148
  2.0 14.3 %collective-permute-start.2 = (bf16[2,2,256,128]{3,2,1,0:T(8,128)(2,1)S(1)}, bf16[2,2,256,128]{3,2,1,0:T(8,128)(2,1)S(1)}, u32[]{:S(2)}, u32[]{:S(2)}) collective-permute-start(bf16[2,2,256,128]{3,2,1,0:T(8,128)(2,1)S(1)} %get-tuple-element.14), channel_id=1, source_target_pairs={{0,96},{32,0},{64,32},{96,64},{1,97},{33,1},{65,33},{97,65},{2,98}... | collective-permute-start | bytes 786440 | tf_op jit(solution)/shard_map/ppermute | solution.py:294
  5.2 11.2 %collective-permute-start.1 = (bf16[2,2,256,128]{3,2,1,0:T(8,128)(2,1)S(1)}, bf16[2,2,256,128]{3,2,1,0:T(8,128)(2,1)S(1)}, u32[]{:S(2)}, u32[]{:S(2)}) collective-permute-start(bf16[2,2,256,128]{3,2,1,0:T(8,128)(2,1)S(1)} %get-tuple-element.15), channel_id=1, source_target_pairs={{0,64},{32,96},{64,0},{96,32},{1,65},{33,97},{65,1},{97,33},{2,66}... | collective-permute-start | bytes 786440 | tf_op jit(solution)/shard_map/ppermute | solution.py:294
  5.8 14.3 %collective-permute-start = (bf16[2,2,256,128]{3,2,1,0:T(8,128)(2,1)S(1)}, bf16[2,2,256,128]{3,2,1,0:T(8,128)(2,1)S(1)}, u32[]{:S(2)}, u32[]{:S(2)}) collective-permute-start(bf16[2,2,256,128]{3,2,1,0:T(8,128)(2,1)S(1)} %get-tuple-element.16), channel_id=1, source_target_pairs={{0,32},{32,64},{64,96},{96,0},{1,33},{33,65},{65,97},{97,1},{2,34}... | collective-permute-start | bytes 786440 | tf_op jit(solution)/shard_map/ppermute | solution.py:294
  20.1 0.7 %copy-start.1 = (f32[4,16]{1,0:T(4,128)S(1)}, f32[4,16]{1,0:T(4,128)}, u32[]{:S(2)}) copy-start(f32[4,16]{1,0:T(4,128)} %constant.46.clone.twiddle) | copy-start | bytes 772
  24.3 1.4 %collective-permute-start.3 = (f32[256,128]{1,0:T(8,128)S(1)}, f32[256,128]{1,0:T(8,128)S(1)}, u32[]{:S(2)}, u32[]{:S(2)}) collective-permute-start(f32[256,128]{1,0:T(8,128)S(1)} %get-tuple-element.7), channel_id=1, source_target_pairs={{0,1},{1,0},{2,3},{3,2},{4,5},{5,4},{6,7},{7,6},{8,9},{9,8},{10,11... | collective-permute-start | bytes 393224 | tf_op jit(solution)/shard_map/ppermute | solution.py:280
  25.7 5.9 %collective-permute-start.6 = (f32[256,128]{1,0:T(8,128)S(1)}, f32[256,128]{1,0:T(8,128)S(1)}, u32[]{:S(2)}, u32[]{:S(2)}) collective-permute-start(f32[256,128]{1,0:T(8,128)S(1)} %add.63), channel_id=1, source_target_pairs={{0,6},{1,7},{2,0},{3,1},{4,2},{5,3},{6,4},{7,5},{8,14},{9,15},{10,... | collective-permute-start | bytes 393224 | tf_op jit(solution)/shard_map/ppermute | solution.py:282
  28.6 9.3 %collective-permute-start.5 = (f32[256,128]{1,0:T(8,128)S(1)}, f32[256,128]{1,0:T(8,128)S(1)}, u32[]{:S(2)}, u32[]{:S(2)}) collective-permute-start(f32[256,128]{1,0:T(8,128)S(1)} %add.63), channel_id=1, source_target_pairs={{0,2},{1,3},{2,4},{3,5},{4,6},{5,7},{6,0},{7,1},{8,10},{9,11},{10,... | collective-permute-start | bytes 393224 | tf_op jit(solution)/shard_map/ppermute | solution.py:282
  28.6 9.3 %collective-permute-start.4 = (f32[256,128]{1,0:T(8,128)S(1)}, f32[256,128]{1,0:T(8,128)S(1)}, u32[]{:S(2)}, u32[]{:S(2)}) collective-permute-start(f32[256,128]{1,0:T(8,128)S(1)} %add.63), channel_id=1, source_target_pairs={{0,4},{1,5},{2,6},{3,7},{4,0},{5,1},{6,2},{7,3},{8,12},{9,13},{10,... | collective-permute-start | bytes 393224 | tf_op jit(solution)/shard_map/ppermute | solution.py:282
  37.9 8.0 %collective-permute-start.9 = (f32[256,128]{1,0:T(8,128)S(1)}, f32[256,128]{1,0:T(8,128)S(1)}, u32[]{:S(2)}, u32[]{:S(2)}) collective-permute-start(f32[256,128]{1,0:T(8,128)S(1)} %add_add_fusion.1), channel_id=1, source_target_pairs={{0,24},{1,25},{2,26},{3,27},{4,28},{5,29},{6,30},{7,31},{8,0},{9,1... | collective-permute-start | bytes 393224 | tf_op jit(solution)/shard_map/ppermute | solution.py:282
  42.0 7.6 %collective-permute-start.8 = (f32[256,128]{1,0:T(8,128)S(1)}, f32[256,128]{1,0:T(8,128)S(1)}, u32[]{:S(2)}, u32[]{:S(2)}) collective-permute-start(f32[256,128]{1,0:T(8,128)S(1)} %add_add_fusion.1), channel_id=1, source_target_pairs={{0,8},{1,9},{2,10},{3,11},{4,12},{5,13},{6,14},{7,15},{8,16},{9,17... | collective-permute-start | bytes 393224 | tf_op jit(solution)/shard_map/ppermute | solution.py:282
  42.0 7.6 %collective-permute-start.7 = (f32[256,128]{1,0:T(8,128)S(1)}, f32[256,128]{1,0:T(8,128)S(1)}, u32[]{:S(2)}, u32[]{:S(2)}) collective-permute-start(f32[256,128]{1,0:T(8,128)S(1)} %add_add_fusion.1), channel_id=1, source_target_pairs={{0,16},{1,17},{2,18},{3,19},{4,20},{5,21},{6,22},{7,23},{8,24},{9,... | collective-permute-start | bytes 393224 | tf_op jit(solution)/shard_map/ppermute | solution.py:282
  49.6 0.7 %copy-start.2 = (f32[4,16]{1,0:T(4,128)S(1)}, f32[4,16]{1,0:T(4,128)}, u32[]{:S(2)}) copy-start(f32[4,16]{1,0:T(4,128)} %constant.47.clone.phase) | copy-start | bytes 772

commit v2 on v1

v2 whole, which is shorter than its diff:
```python
import math

import jax
import jax.numpy as jnp
import numpy as np
from jax import lax
from jax.experimental import pallas as pl
from jax.experimental.pallas import tpu as pltpu
from jax.sharding import PartitionSpec as P

SUBS = 8
WIDTH = 64
FIELDS = 4
LANES = 128
ROWS = WIDTH * FIELDS
F32 = jnp.float32
BF16 = jnp.bfloat16


def twiddle_table():
    table = np.zeros((4, 16), np.float32)
    for t in range(4):
        for d in range(4):
            angle = -2.0 * math.pi * (((t - d) % 4) * t) / 16.0
            table[t, 2 * d] = math.cos(angle)
            table[t, 2 * d + 1] = math.sin(angle)
        for q in range(4):
            angle = -2.0 * math.pi * (t / 32.0 + q / 8.0)
            table[t, 8 + 2 * q] = math.cos(angle)
            table[t, 9 + 2 * q] = math.sin(angle)
    return table


def phase_table():
    table = np.zeros((4, 16), np.float32)
    for t in range(4):
        for q in range(8):
            re, im = [(1, 0), (0, -1), (-1, 0), (0, 1)][(t * q) % 4]
            table[t, 2 * q] = re
            table[t, 2 * q + 1] = im
    return table


def split(value):
    high = value.astype(BF16)
    return high, (value - high.astype(F32)).astype(BF16)


def lane_iota(shape):
    return lax.broadcasted_iota(jnp.int32, shape, len(shape) - 1)


SMALL = (8, LANES)


def places():
    lane = lane_iota(SMALL)
    sub = lax.broadcasted_iota(jnp.int32, SMALL, 0)
    parity = lane // WIDTH
    group = lane % 16
    return lane, sub, parity, group, group * 4 + sub % 4


def block_transpose(tiles):
    block = lane_iota(tiles[0].shape) // 16
    for bit in range(3):
        step = 1 << bit
        low = (block & step) == 0
        out = list(tiles)
        for x in range(8):
            if x & step == 0:
                y = x | step
                out[x] = jnp.where(low, tiles[x], pltpu.roll(tiles[y], 16 * step, 1))
                out[y] = jnp.where(low, pltpu.roll(tiles[x], LANES - 16 * step, 1), tiles[y])
        tiles = out
    return tiles


def gather_lanes(value, index):
    return jnp.take_along_axis(value, index, axis=1)


def reverse_rows(value, lane, sub):
    index = (1 - lane // WIDTH) * WIDTH + (lane % WIDTH) // 16 * 16 + 15 - lane % 16
    value = gather_lanes(value, index)
    value = jnp.where(sub % 2 == 0, pltpu.roll(value, 7, 0), pltpu.roll(value, 1, 0))
    return jnp.where(sub % 4 < 2, pltpu.roll(value, 6, 0), pltpu.roll(value, 2, 0))


def gram_kernel(own, near1, near2, near3, weight16, twiddle, sh_ref, sl_ref, keep_ref, send_ref, work, mixed):
    t = lax.axis_index("tm")
    root = jnp.sqrt(weight16[...])
    sources = (own, near1, near2, near3)
    tw = [(root * twiddle[t, 2 * d], root * twiddle[t, 2 * d + 1]) for d in range(4)]
    tq = [(twiddle[t, 8 + 2 * q], twiddle[t, 9 + 2 * q]) for q in range(4)]

    def transform(step, _):
        row = pl.multiple_of(step * 16, 16)
        rows = pl.ds(row, 16)
        radix = []
        for s in range(2):
            y = []
            for d in range(4):
                re = sources[d][0, s, rows, :].astype(F32)
                im = sources[d][1, s, rows, :].astype(F32)
                y.append((re * tw[d][0] - im * tw[d][1], re * tw[d][1] + im * tw[d][0]))
            a = (y[0][0] + y[2][0], y[0][1] + y[2][1])
            b = (y[0][0] - y[2][0], y[0][1] - y[2][1])
            c = (y[1][0] + y[3][0], y[1][1] + y[3][1])
            e = (y[1][0] - y[3][0], y[1][1] - y[3][1])
            radix.append(
                [
                    (a[0] + c[0], a[1] + c[1]),
                    (b[0] - e[1], b[1] + e[0]),
                    (a[0] - c[0], a[1] - c[1]),
                    (b[0] + e[1], b[1] - e[0]),
                ]
            )
        for q in range(4):
            x0 = radix[0][q]
            x1 = radix[1][q]
            v = (x1[0] * tq[q][0] - x1[1] * tq[q][1], x1[0] * tq[q][1] + x1[1] * tq[q][0])
            work[q, 0, rows, :] = x0[0] + v[0]
            work[q, 1, rows, :] = x0[1] + v[1]
            work[q + 4, 0, rows, :] = x0[0] - v[0]
            work[q + 4, 1, rows, :] = x0[1] - v[1]
        return 0

    lax.fori_loop(0, ROWS // 16, transform, 0)

    left = lane_iota((WIDTH, LANES)) < WIDTH

    def one_gram(q):
        for part in range(2):
            for f in range(FIELDS):
                for s in range(4):
                    value = work[q, part, pl.ds(s * 4 + f, 16, stride=16), :]
                    high, low = split(value)
                    place = slice(part * WIDTH + s * 16, part * WIDTH + s * 16 + 16)
                    sh_ref[q, place, f * LANES : (f + 1) * LANES] = high
                    sl_ref[q, place, f * LANES : (f + 1) * LANES] = low
        high = sh_ref[q]
        both = jnp.concatenate([high, sl_ref[q]], axis=0)
        prod = lax.dot_general(both, high, (((1,), (1,)), ((), ())), preferred_element_type=F32)
        cross = prod[LANES:]
        full = prod[:LANES] + (cross + cross.T)
        low = pltpu.roll(full[WIDTH:], WIDTH, 1)
        return full[:WIDTH] + jnp.where(left, low, -low)

    lane, sub, parity, _, column = places()

    def half(base):
        tiles = [None] * 8
        for qq in range(4):
            tile = one_gram(base + qq)
            for p in range(2):
                tiles[p * 4 + qq] = jnp.concatenate(
                    [tile[p * 16 : p * 16 + 16], tile[32 + p * 16 : 48 + p * 16]], axis=0
                )
        for a, tile in enumerate(block_transpose(tiles)):
            mixed[a * 32 : (a + 1) * 32, :] = tile
        out = []
        for m in range(16):
            near = mixed[pl.ds(m % 2 * 16 + m // 2, 8, stride=32), :]
            far_m = 31 - m
            far = mixed[pl.ds(far_m % 2 * 16 + far_m // 2, 8, stride=32), :]
            far = reverse_rows(far, lane, sub)
            line = 2 * m + parity
            far = jnp.where(column == line, pltpu.roll(far, 4, 0), far)
            upper = (column > line) | ((column == line) & (sub < 4))
            out.append(jnp.where(upper, near, far))
        return out

    mine = lax.axis_index("space") % 2
    first = half(0)
    second = half(4)
    for m in range(16):
        keep_ref[m * 8 : (m + 1) * 8, :] = jnp.where(mine == 0, first[m], second[m])
        send_ref[m * 8 : (m + 1) * 8, :] = jnp.where(mine == 0, second[m], first[m])


def at_sub(value, index):
    return jnp.broadcast_to(value[index : index + 1, :], value.shape)


def factor_kernel(gram, out_ref):
    lane, sub, parity, group, column = places()
    first = parity == 0
    sign = jnp.where(sub < 4, 1.0, -1.0).astype(F32)
    real = sub < 4
    lane_base = lane // 16 * 16

    def turn(value):
        return pltpu.roll(value, 4, 0) * sign

    def lifted(value):
        return jnp.where(first, value, pltpu.roll(value, 7, 0))

    rows = [None] * 32
    for m in range(16):
        packed = gram[m * 8 : (m + 1) * 8, :]
        rows[m] = packed
        far = reverse_rows(packed, lane, sub)
        line = 2 * (31 - m) + parity
        rows[31 - m] = jnp.where(column == line, pltpu.roll(far, 4, 0), far)

    for g in range(16):
        pair = (rows[2 * g], rows[2 * g + 1])
        full, block, ahead = [], [], []
        for v in pair:
            turned = pltpu.roll(v, WIDTH, 1)
            one = jnp.where(first, v, turned)
            two = jnp.where(first, turned, v)
            full += [one, two]
            for p in range(2):
                block.append(gather_lanes(v, lane % WIDTH // 16 * 16 + p * WIDTH + g))
        if g < 15:
            for r in range(4):
                ahead.append(gather_lanes(lifted(full[r]), lane_base + g + 1))
        in_group = group == g
        inverse, root, scaled = [], [], []
        for s in range(4):
            here = in_group & (sub % 4 == s)
            pivot = at_sub(block[s], s)
            ip = 1.0 / pivot
            inverse.append(ip)
            root.append(lax.rsqrt(pivot))
            full[s] = jnp.where(here, jnp.where(real, 1.0, 0.0), full[s])
            y = full[s] * ip
            y_t = turn(y)
            b = block[s] * ip
            b_t = turn(b)
            if g < 15:
                n = ahead[s] * ip
                n_t = turn(n)
            for r in range(s + 1, 4):
                mr = at_sub(block[s], r)
                mi = at_sub(block[s], 4 + r)
                full[r] = jnp.where(here, 0.0, full[r]) - mr * y - mi * y_t
                block[r] = block[r] - mr * b - mi * b_t
                if g < 15:
                    ahead[r] = ahead[r] - mr * n - mi * n_t
            later = in_group & (sub % 4 > s)
            y = jnp.where(later, 0.0, y)
            scaled.append((y, jnp.where(later, 0.0, y_t)))
        raised = [lifted(full[r]) for r in range(4)]
        for h in range(g + 1, 16):
            if h == g + 1:
                multi = ahead
            else:
                multi = [gather_lanes(raised[r], lane_base + h) for r in range(4)]
            for odd in range(2):
                m = 2 * h + odd
                value = jnp.where(in_group, 0.0, rows[m])
                terms = []
                for r in range(4):
                    y, y_t = scaled[r]
                    terms.append(at_sub(multi[r], 2 * odd) * y + at_sub(multi[r], 4 + 2 * odd) * y_t)
                rows[m] = value - ((terms[0] + terms[1]) + (terms[2] + terms[3]))
        for odd in range(2):
            m = 2 * g + odd
            out_ref[m * 8 : (m + 1) * 8, :] = jnp.where(
                first, full[2 * odd] * root[2 * odd], full[2 * odd + 1] * root[2 * odd + 1]
            )


def modes_kernel(own, far, sh_ref, sl_ref, weight, phase, modes_ref, upper_ref, turned, work, natural):
    t = lax.axis_index("tm")
    mine = lax.axis_index("space") % 2
    wide = (WIDTH, LANES)
    lane = lane_iota(wide)
    order = lax.broadcasted_iota(jnp.int32, wide, 0)
    line = order % 16 * 4 + order // 16 % 2 * 2 + order // 32
    column = lane % 16 * 4 + lane // 16 % 4
    left = lane < WIDTH
    lane8 = lane_iota(SMALL)
    natural_index = lane8 // WIDTH * WIDTH + lane8 % 4 * 16 + lane8 % WIDTH // 4
    root = lax.rsqrt(weight[...])

    for slot, source in enumerate((own, far)):
        tiles = []
        for a in range(8):
            tiles.append(
                jnp.concatenate(
                    [source[pl.ds(a + 8 * odd, 16, stride=16), :] for odd in range(2)], axis=0
                )
            )
        for b, tile in enumerate(block_transpose(tiles)):
            turned[slot, b % 4, b // 4 * 32 : b // 4 * 32 + 32, :] = tile

    def emit(index, _):
        slot = index // 4
        q = ((mine + slot) % 2) * 4 + index % 4
        both = turned[slot, index % 4]
        inverse = jnp.where(column <= line, both, 0.0)
        diag = jnp.where(left, 1.0 / both, 0.0)
        upper = jnp.where(column > line, both, jnp.where(column == line, diag, 0.0))
        for j in range(4):
            s = 2 * (j % 2) + j // 2
            for k in range(2):
                piece = gather_lanes(upper[j * 16 + k * 8 : j * 16 + k * 8 + 8], natural_index)
                natural[pl.ds(s + 32 * k, 8, stride=4), :] = piece
        upper_ref[0, q] = natural[:, :WIDTH]
        upper_ref[1, q] = natural[:, WIDTH:]
        swapped = pltpu.roll(inverse, WIDTH, 1)
        swapped = jnp.where(left, -swapped, swapped)
        pr = phase[t, 2 * q]
        pi = phase[t, 2 * q + 1]
        lhs = jnp.concatenate([pr * inverse - pi * swapped, pr * swapped + pi * inverse], axis=0)
        lh, ll = split(lhs)
        sh = sh_ref[q]
        out = jnp.dot(lh, sh, preferred_element_type=F32)
        out = out + jnp.dot(ll, sh, preferred_element_type=F32)
        out = out + jnp.dot(lh, sl_ref[q], preferred_element_type=F32)
        for part in range(2):
            for f in range(FIELDS):
                block = out[part * WIDTH : (part + 1) * WIDTH, f * LANES : (f + 1) * LANES] * root[f : f + 1, :]
                for j in range(4):
                    s = 2 * (j % 2) + j // 2
                    work[pl.ds(part * ROWS + s * 4 + f, 16, stride=16), :] = block[j * 16 : j * 16 + 16]
            modes_ref[part, q] = work[part * ROWS : (part + 1) * ROWS, :].astype(BF16)
        return 0

    lax.fori_loop(0, SUBS, emit, 0)


def vmem():
    return pl.BlockSpec(memory_space=pltpu.VMEM)


def smem():
    return pl.BlockSpec(memory_space=pltpu.SMEM)


HALF = (LANES, LANES)
PARAMS = pltpu.CompilerParams(vmem_limit_bytes=32 * 1024 * 1024)


def run_gram(own, near, weight16, table):
    return pl.pallas_call(
        gram_kernel,
        name="gram",
        out_shape=(
            jax.ShapeDtypeStruct((SUBS, LANES, FIELDS * LANES), BF16),
            jax.ShapeDtypeStruct((SUBS, LANES, FIELDS * LANES), BF16),
            jax.ShapeDtypeStruct(HALF, F32),
            jax.ShapeDtypeStruct(HALF, F32),
        ),
        in_specs=[vmem()] * 5 + [smem()],
        out_specs=(vmem(),) * 4,
        scratch_shapes=[pltpu.VMEM((SUBS, 2, ROWS, LANES), F32), pltpu.VMEM((ROWS, LANES), F32)],
        compiler_params=PARAMS,
    )(own, *near, weight16, table)


def run_factor(gram):
    return pl.pallas_call(
        factor_kernel,
        name="factor",
        out_shape=jax.ShapeDtypeStruct((2 * LANES, LANES), F32),
        in_specs=[vmem()],
        out_specs=vmem(),
        compiler_params=PARAMS,
    )(gram)


def run_modes(own, far, sh, sl, weights, table):
    return pl.pallas_call(
        modes_kernel,
        name="modes",
        out_shape=(
            jax.ShapeDtypeStruct((2, SUBS, ROWS, LANES), BF16),
            jax.ShapeDtypeStruct((2, SUBS, WIDTH, WIDTH), F32),
        ),
        in_specs=[vmem()] * 5 + [smem()],
        out_specs=(vmem(), vmem()),
        scratch_shapes=[
            pltpu.VMEM((2, 4, WIDTH, LANES), F32),
            pltpu.VMEM((2 * ROWS, LANES), F32),
            pltpu.VMEM((WIDTH, LANES), F32),
        ],
        compiler_params=PARAMS,
    )(own, far, sh, sl, weights, table)


def space_perm(along, shift):
    pairs = []
    for i in range(32):
        z, x, core = i // 8, i // 2 % 4, i % 2
        if along == "x":
            x = (x + shift) % 4
        elif along == "z":
            z = (z + shift) % 4
        else:
            core = 1 - core
        pairs.append((i, (z * 4 + x) * 2 + core))
    return pairs


def sum_over_chips(value):
    for along in ("x", "z"):
        far = [lax.ppermute(value, "space", space_perm(along, d)) for d in (1, 3, 2)]
        value = (value + far[2]) + (far[0] + far[1])
    return value


def on_device(spectra, weights):
    t = lax.axis_index("tm")
    flat = spectra.reshape(2, 2, 4, ROWS, LANES)
    own = lax.dynamic_index_in_dim(flat, t, 2, keepdims=False)
    near = []
    for d in range(1, 4):
        piece = lax.dynamic_index_in_dim(flat, (t + d) % 4, 2, keepdims=False)
        near.append(lax.ppermute(piece, "tm", [(i, (i + d) % 4) for i in range(4)]))
    weight16 = jnp.tile(weights, (4, 1))
    sh, sl, keep, send = run_gram(own, near, weight16, jnp.asarray(twiddle_table()))
    across = space_perm("core", 1)
    gram = sum_over_chips(keep + lax.ppermute(send, "space", across))
    factor = run_factor(gram)
    far = lax.ppermute(factor, "space", across)
    modes, upper = run_modes(factor, far, sh, sl, weights, jnp.asarray(phase_table()))
    return (
        modes.reshape(2, SUBS, 1, WIDTH, FIELDS, LANES),
        upper.reshape(2, SUBS, 1, WIDTH, WIDTH),
    )


def solution(mesh):
    placed = (P(None, "tm", None, None, None, "space"), P(None, "space"))
    return jax.shard_map(
        on_device,
        mesh=mesh,
        in_specs=placed,
        out_specs=(P(None, None, "tm", None, None, "space"), P(None, None, "tm", None, None)),
        check_vma=False,
    )
```

time: 64.9 us -> 55.3 us (0.85)
  the two profiles are of different devices: /device:TPU:0 before, /device:TPU:1 now
where the time goes in v2:
time: 55.3 us; the launch traced here: 55.2 us
  waiting for transfers between devices  23.8 us (43%)
  starting transfers between devices  17.7 us (32%)
  Pallas kernels  10.9 us (20%)
  local copies, waits for them, and re-layouts  1.99 us (4%)
  between operations  0.73 us (1%)
    ppermute x3, waiting for transfers between devices, on_device(): near.append(lax.ppermute(piece, 'tm', [(i, (i + d) % 4) for i in range(4)]))  14.3 us
    ppermute x6, starting transfers between devices, sum_over_chips(): lax.ppermute(value, 'space', space_perm(along, d))  9.41 us
    ppermute x6, waiting for transfers between devices, sum_over_chips(): lax.ppermute(value, 'space', space_perm(along, d))  7.61 us
    pallas_call x1, Pallas kernels, run_modes(): pl.pallas_call(modes_kernel, name='modes', out_shape=(jax.ShapeDtypeStruc...  4.94 us
    ppermute x3, starting transfers between devices, on_device(): near.append(lax.ppermute(piece, 'tm', [(i, (i + d) % 4) for i in range(4)]))  4.67 us
    pallas_call x1, Pallas kernels, run_gram(): pl.pallas_call(gram_kernel, name='gram', out_shape=(jax.ShapeDtypeStruct(...  3.33 us
    ppermute x1, starting transfers between devices, on_device(): far = lax.ppermute(factor, 'space', across)  3.02 us
    pallas_call x1, Pallas kernels, run_factor(): pl.pallas_call(factor_kernel, name='factor', out_shape=jax.ShapeDtypeStru...  2.65 us
  transfers between devices with their start and end apart: 11, of which 7 were waited for; matrix products, arithmetic and copies ran while one was open for 0% of the time, Pallas kernels for 0%

profile of v2, /device:TPU:1, one launch (start us, length us, event | category | flops | bytes accessed | tf_op | source)
XLA Modules:
  0.0 55.2 jit_solution(6782129767785144157)
XLA Ops:
  0.7 1.3 %dynamic-slice_bitcast_fusion = (bf16[2,2,256,128]{3,2,1,0:T(8,128)(2,1)S(1)}, bf16[2,2,256,128]{3,2,1,0:T(8,128)(2,1)S(1)}, bf16[2,2,256,128]{3,2,1,0:T(8,128)(2,1)S(1)}, bf16[2,2,256,128]{3,2,1,0:T(8,128)(2,1)S(1)}) fusion(bf16[2,2,4,256,128]{4,3,2,1,0:T(8,128)(2,1)} %bitcast.25, s32[]{:T(128)S(6)} %select_n.34, s32[]{:T(128)S(6)} %select_n.32, ...), kind=kLoop, calls=%fused_computation | loop fusion | bytes 2097168 | tf_op jit(solution)/shard_map/jit(dynamic_index_in_dim)/squeeze | solution.py:413
  2.0 0.0 copy-start
  2.0 3.6 %collective-permute-start.2 = (bf16[2,2,256,128]{3,2,1,0:T(8,128)(2,1)S(1)}, bf16[2,2,256,128]{3,2,1,0:T(8,128)(2,1)S(1)}, u32[]{:S(2)}, u32[]{:S(2)}) collective-permute-start(bf16[2,2,256,128]{3,2,1,0:T(8,128)(2,1)S(1)} %get-tuple-element.16), channel_id=1, source_target_pairs={{0,96},{32,0},{64,32},{96,64},{1,97},{33,1},{65,33},{97,65},{2,98}... | collective-permute-start | bytes 786440 | tf_op jit(solution)/shard_map/ppermute | solution.py:414
  5.6 0.3 collective-permute-start.1
  6.0 0.7 %collective-permute-start = (bf16[2,2,256,128]{3,2,1,0:T(8,128)(2,1)S(1)}, bf16[2,2,256,128]{3,2,1,0:T(8,128)(2,1)S(1)}, u32[]{:S(2)}, u32[]{:S(2)}) collective-permute-start(bf16[2,2,256,128]{3,2,1,0:T(8,128)(2,1)S(1)} %get-tuple-element.18), channel_id=1, source_target_pairs={{0,32},{32,64},{64,96},{96,0},{1,33},{33,65},{65,97},{97,1},{2,34}... | collective-permute-start | bytes 786440 | tf_op jit(solution)/shard_map/ppermute | solution.py:414
  6.7 9.4 %collective-permute-done.2.near3 = bf16[2,2,256,128]{3,2,1,0:T(8,128)(2,1)S(1)} collective-permute-done((bf16[2,2,256,128]{3,2,1,0:T(8,128)(2,1)S(1)}, bf16[2,2,256,128]{3,2,1,0:T(8,128)(2,1)S(1)}, u32[]{:S(2)}, u32[]{:S(2)}) %collective-permute-start.2) | collective-permute-done | bytes 262176 | tf_op jit(solution)/shard_map/ppermute | solution.py:414
  16.1 0.0 collective-permute-done.1.near2
  16.1 4.9 %collective-permute-done.near1 = bf16[2,2,256,128]{3,2,1,0:T(8,128)(2,1)S(1)} collective-permute-done((bf16[2,2,256,128]{3,2,1,0:T(8,128)(2,1)S(1)}, bf16[2,2,256,128]{3,2,1,0:T(8,128)(2,1)S(1)}, u32[]{:S(2)}, u32[]{:S(2)}) %collective-permute-start) | collective-permute-done | bytes 262176 | tf_op jit(solution)/shard_map/ppermute | solution.py:414
  21.0 0.0 copy-done
  21.0 0.0 copy-start.2
  21.0 0.7 %copy-done.2 = f32[4,16]{1,0:T(4,128)S(1)} copy-done((f32[4,16]{1,0:T(4,128)S(1)}, f32[4,16]{1,0:T(4,128)}, u32[]{:S(2)}) %copy-start.2) | copy-done | bytes 280
  21.7 3.3 %gram.1 = (bf16[8,128,512]{2,1,0:T(8,128)(2,1)S(1)}, bf16[8,128,512]{2,1,0:T(8,128)(2,1)S(1)}, f32[128,128]{1,0:T(8,128)S(1)}, f32[128,128]{1,0:T(8,128)S(1)}) custom-call(bf16[2,2,256,128]{3,2,1,0:T(8,128)(2,1)S(1)} %get-tuple-element.19.own, bf16[2,2,256,128]{3,2,1,0:T(8,128)(2,1)S(1)} %collective-permute-done.near1, ...), custom_call_target="tpu_custom_call" | custom-call | tf_op jit(solution)/shard_map/gram/pallas_call | solution.py:340
  25.0 0.6 %collective-permute-start.3 = (f32[128,128]{1,0:T(8,128)S(1)}, f32[128,128]{1,0:T(8,128)S(1)}, u32[]{:S(2)}, u32[]{:S(2)}) collective-permute-start(f32[128,128]{1,0:T(8,128)S(1)} %get-tuple-element.9), channel_id=1, source_target_pairs={{0,1},{1,0},{2,3},{3,2},{4,5},{5,4},{6,7},{7,6},{8,9},{9,8},{10,11... | collective-permute-start | bytes 196616 | tf_op jit(solution)/shard_map/ppermute | solution.py:418
  25.6 0.9 %collective-permute-done.3 = f32[128,128]{1,0:T(8,128)S(1)} collective-permute-done((f32[128,128]{1,0:T(8,128)S(1)}, f32[128,128]{1,0:T(8,128)S(1)}, u32[]{:S(2)}, u32[]{:S(2)}) %collective-permute-start.3) | collective-permute-done | bytes 65568 | tf_op jit(solution)/shard_map/ppermute | solution.py:418
  26.5 2.5 %collective-permute-start.6 = (f32[128,128]{1,0:T(8,128)S(1)}, f32[128,128]{1,0:T(8,128)S(1)}, u32[]{:S(2)}, u32[]{:S(2)}) collective-permute-start(f32[128,128]{1,0:T(8,128)S(1)} %add.63), channel_id=1, source_target_pairs={{0,6},{1,7},{2,0},{3,1},{4,2},{5,3},{6,4},{7,5},{8,14},{9,15},{10,... | collective-permute-start | bytes 196616 | tf_op jit(solution)/shard_map/ppermute | solution.py:402
  29.0 0.0 collective-permute-start.5
  29.0 1.7 %collective-permute-start.4 = (f32[128,128]{1,0:T(8,128)S(1)}, f32[128,128]{1,0:T(8,128)S(1)}, u32[]{:S(2)}, u32[]{:S(2)}) collective-permute-start(f32[128,128]{1,0:T(8,128)S(1)} %add.63), channel_id=1, source_target_pairs={{0,4},{1,5},{2,6},{3,7},{4,0},{5,1},{6,2},{7,3},{8,12},{9,13},{10,... | collective-permute-start | bytes 196616 | tf_op jit(solution)/shard_map/ppermute | solution.py:402
  30.8 0.0 collective-permute-done.6
  30.8 3.0 %collective-permute-done.5 = f32[128,128]{1,0:T(8,128)S(1)} collective-permute-done((f32[128,128]{1,0:T(8,128)S(1)}, f32[128,128]{1,0:T(8,128)S(1)}, u32[]{:S(2)}, u32[]{:S(2)}) %collective-permute-start.5) | collective-permute-done | bytes 65568 | tf_op jit(solution)/shard_map/ppermute | solution.py:402
  33.8 0.9 %collective-permute-done.4 = f32[128,128]{1,0:T(8,128)S(1)} collective-permute-done((f32[128,128]{1,0:T(8,128)S(1)}, f32[128,128]{1,0:T(8,128)S(1)}, u32[]{:S(2)}, u32[]{:S(2)}) %collective-permute-start.4) | collective-permute-done | bytes 65568 | tf_op jit(solution)/shard_map/ppermute | solution.py:402
  34.7 3.8 %collective-permute-start.9 = (f32[128,128]{1,0:T(8,128)S(1)}, f32[128,128]{1,0:T(8,128)S(1)}, u32[]{:S(2)}, u32[]{:S(2)}) collective-permute-start(f32[128,128]{1,0:T(8,128)S(1)} %add_add_fusion.1), channel_id=1, source_target_pairs={{0,24},{1,25},{2,26},{3,27},{4,28},{5,29},{6,30},{7,31},{8,0},{9,1... | collective-permute-start | bytes 196616 | tf_op jit(solution)/shard_map/ppermute | solution.py:402
  38.5 0.0 collective-permute-start.8
  38.5 1.3 %collective-permute-start.7 = (f32[128,128]{1,0:T(8,128)S(1)}, f32[128,128]{1,0:T(8,128)S(1)}, u32[]{:S(2)}, u32[]{:S(2)}) collective-permute-start(f32[128,128]{1,0:T(8,128)S(1)} %add_add_fusion.1), channel_id=1, source_target_pairs={{0,16},{1,17},{2,18},{3,19},{4,20},{5,21},{6,22},{7,23},{8,24},{9,... | collective-permute-start | bytes 196616 | tf_op jit(solution)/shard_map/ppermute | solution.py:402
  39.8 0.0 collective-permute-done.9
  39.8 3.7 %collective-permute-done.8 = f32[128,128]{1,0:T(8,128)S(1)} collective-permute-done((f32[128,128]{1,0:T(8,128)S(1)}, f32[128,128]{1,0:T(8,128)S(1)}, u32[]{:S(2)}, u32[]{:S(2)}) %collective-permute-start.8) | collective-permute-done | bytes 65568 | tf_op jit(solution)/shard_map/ppermute | solution.py:402
  43.5 0.0 collective-permute-done.7
  43.6 2.6 %factor.1.own = f32[256,128]{1,0:T(8,128)S(1)} custom-call(f32[128,128]{1,0:T(8,128)S(1)} %add_add_fusion.gram), custom_call_target="tpu_custom_call" | custom-call | tf_op jit(solution)/shard_map/factor/pallas_call | solution.py:357
  46.2 0.0 copy-start.1
  46.2 3.0 %collective-permute-start.10 = (f32[256,128]{1,0:T(8,128)S(1)}, f32[256,128]{1,0:T(8,128)S(1)}, u32[]{:S(2)}, u32[]{:S(2)}) collective-permute-start(f32[256,128]{1,0:T(8,128)S(1)} %factor.1.own), channel_id=1, source_target_pairs={{0,1},{1,0},{2,3},{3,2},{4,5},{5,4},{6,7},{7,6},{8,9},{9,8},{10,11... | collective-permute-start | bytes 393224 | tf_op jit(solution)/shard_map/ppermute | solution.py:420
  49.2 1.0 %collective-permute-done.10.far = f32[256,128]{1,0:T(8,128)S(1)} collective-permute-done((f32[256,128]{1,0:T(8,128)S(1)}, f32[256,128]{1,0:T(8,128)S(1)}, u32[]{:S(2)}, u32[]{:S(2)}) %collective-permute-start.10) | collective-permute-done | bytes 131104 | tf_op jit(solution)/shard_map/ppermute | solution.py:420
  50.2 0.0 copy-done.1
  50.2 4.9 %modes.1 = (bf16[2,8,256,128]{3,2,1,0:T(8,128)(2,1)}, f32[2,8,64,64]{3,2,1,0:T(8,128)}) custom-call(f32[256,128]{1,0:T(8,128)S(1)} %factor.1.own, f32[256,128]{1,0:T(8,128)S(1)} %collective-permute-done.10.far, bf16[8,128,512]{2,1,0:T(8,128)(2,1)S(1)} %get-tuple-element.10.sh_ref, bf16[8,128,512]{2,1,0:T(8,128)(2,1)S(1)} %get-tuple-element.11.sl_ref, ...), custom_call_target="tpu_custom_call" | custom-call | tf_op jit(solution)/shard_map/modes/pallas_call | solution.py:368
  (4 shorter events, 0.0 us)
Async XLA Ops:
  2.0 19.0 %copy-start = (f32[4,128]{1,0:T(4,128)S(1)}, f32[4,128]{1,0:T(4,128)}, u32[]{:S(2)}) copy-start(f32[4,128]{1,0:T(4,128)} %weight.1) | copy-start | bytes 6148
  2.0 14.1 %collective-permute-start.2 = (bf16[2,2,256,128]{3,2,1,0:T(8,128)(2,1)S(1)}, bf16[2,2,256,128]{3,2,1,0:T(8,128)(2,1)S(1)}, u32[]{:S(2)}, u32[]{:S(2)}) collective-permute-start(bf16[2,2,256,128]{3,2,1,0:T(8,128)(2,1)S(1)} %get-tuple-element.16), channel_id=1, source_target_pairs={{0,96},{32,0},{64,32},{96,64},{1,97},{33,1},{65,33},{97,65},{2,98}... | collective-permute-start | bytes 786440 | tf_op jit(solution)/shard_map/ppermute | solution.py:414
  5.6 10.5 %collective-permute-start.1 = (bf16[2,2,256,128]{3,2,1,0:T(8,128)(2,1)S(1)}, bf16[2,2,256,128]{3,2,1,0:T(8,128)(2,1)S(1)}, u32[]{:S(2)}, u32[]{:S(2)}) collective-permute-start(bf16[2,2,256,128]{3,2,1,0:T(8,128)(2,1)S(1)} %get-tuple-element.17), channel_id=1, source_target_pairs={{0,64},{32,96},{64,0},{96,32},{1,65},{33,97},{65,1},{97,33},{2,66}... | collective-permute-start | bytes 786440 | tf_op jit(solution)/shard_map/ppermute | solution.py:414
  6.0 15.0 %collective-permute-start = (bf16[2,2,256,128]{3,2,1,0:T(8,128)(2,1)S(1)}, bf16[2,2,256,128]{3,2,1,0:T(8,128)(2,1)S(1)}, u32[]{:S(2)}, u32[]{:S(2)}) collective-permute-start(bf16[2,2,256,128]{3,2,1,0:T(8,128)(2,1)S(1)} %get-tuple-element.18), channel_id=1, source_target_pairs={{0,32},{32,64},{64,96},{96,0},{1,33},{33,65},{65,97},{97,1},{2,34}... | collective-permute-start | bytes 786440 | tf_op jit(solution)/shard_map/ppermute | solution.py:414
  21.0 0.7 %copy-start.2 = (f32[4,16]{1,0:T(4,128)S(1)}, f32[4,16]{1,0:T(4,128)}, u32[]{:S(2)}) copy-start(f32[4,16]{1,0:T(4,128)} %constant.46.clone.twiddle) | copy-start | bytes 772
  25.0 1.5 %collective-permute-start.3 = (f32[128,128]{1,0:T(8,128)S(1)}, f32[128,128]{1,0:T(8,128)S(1)}, u32[]{:S(2)}, u32[]{:S(2)}) collective-permute-start(f32[128,128]{1,0:T(8,128)S(1)} %get-tuple-element.9), channel_id=1, source_target_pairs={{0,1},{1,0},{2,3},{3,2},{4,5},{5,4},{6,7},{7,6},{8,9},{9,8},{10,11... | collective-permute-start | bytes 196616 | tf_op jit(solution)/shard_map/ppermute | solution.py:418
  26.5 4.3 %collective-permute-start.6 = (f32[128,128]{1,0:T(8,128)S(1)}, f32[128,128]{1,0:T(8,128)S(1)}, u32[]{:S(2)}, u32[]{:S(2)}) collective-permute-start(f32[128,128]{1,0:T(8,128)S(1)} %add.63), channel_id=1, source_target_pairs={{0,6},{1,7},{2,0},{3,1},{4,2},{5,3},{6,4},{7,5},{8,14},{9,15},{10,... | collective-permute-start | bytes 196616 | tf_op jit(solution)/shard_map/ppermute | solution.py:402
  29.0 4.7 %collective-permute-start.5 = (f32[128,128]{1,0:T(8,128)S(1)}, f32[128,128]{1,0:T(8,128)S(1)}, u32[]{:S(2)}, u32[]{:S(2)}) collective-permute-start(f32[128,128]{1,0:T(8,128)S(1)} %add.63), channel_id=1, source_target_pairs={{0,2},{1,3},{2,4},{3,5},{4,6},{5,7},{6,0},{7,1},{8,10},{9,11},{10,... | collective-permute-start | bytes 196616 | tf_op jit(solution)/shard_map/ppermute | solution.py:402
  29.0 5.6 %collective-permute-start.4 = (f32[128,128]{1,0:T(8,128)S(1)}, f32[128,128]{1,0:T(8,128)S(1)}, u32[]{:S(2)}, u32[]{:S(2)}) collective-permute-start(f32[128,128]{1,0:T(8,128)S(1)} %add.63), channel_id=1, source_target_pairs={{0,4},{1,5},{2,6},{3,7},{4,0},{5,1},{6,2},{7,3},{8,12},{9,13},{10,... | collective-permute-start | bytes 196616 | tf_op jit(solution)/shard_map/ppermute | solution.py:402
  34.7 5.2 %collective-permute-start.9 = (f32[128,128]{1,0:T(8,128)S(1)}, f32[128,128]{1,0:T(8,128)S(1)}, u32[]{:S(2)}, u32[]{:S(2)}) collective-permute-start(f32[128,128]{1,0:T(8,128)S(1)} %add_add_fusion.1), channel_id=1, source_target_pairs={{0,24},{1,25},{2,26},{3,27},{4,28},{5,29},{6,30},{7,31},{8,0},{9,1... | collective-permute-start | bytes 196616 | tf_op jit(solution)/shard_map/ppermute | solution.py:402
  38.5 5.0 %collective-permute-start.8 = (f32[128,128]{1,0:T(8,128)S(1)}, f32[128,128]{1,0:T(8,128)S(1)}, u32[]{:S(2)}, u32[]{:S(2)}) collective-permute-start(f32[128,128]{1,0:T(8,128)S(1)} %add_add_fusion.1), channel_id=1, source_target_pairs={{0,8},{1,9},{2,10},{3,11},{4,12},{5,13},{6,14},{7,15},{8,16},{9,17... | collective-permute-start | bytes 196616 | tf_op jit(solution)/shard_map/ppermute | solution.py:402
  38.5 5.0 %collective-permute-start.7 = (f32[128,128]{1,0:T(8,128)S(1)}, f32[128,128]{1,0:T(8,128)S(1)}, u32[]{:S(2)}, u32[]{:S(2)}) collective-permute-start(f32[128,128]{1,0:T(8,128)S(1)} %add_add_fusion.1), channel_id=1, source_target_pairs={{0,16},{1,17},{2,18},{3,19},{4,20},{5,21},{6,22},{7,23},{8,24},{9,... | collective-permute-start | bytes 196616 | tf_op jit(solution)/shard_map/ppermute | solution.py:402
  46.2 4.0 %copy-start.1 = (f32[4,16]{1,0:T(4,128)S(1)}, f32[4,16]{1,0:T(4,128)}, u32[]{:S(2)}) copy-start(f32[4,16]{1,0:T(4,128)} %constant.47.clone.phase) | copy-start | bytes 772
  46.2 4.0 %collective-permute-start.10 = (f32[256,128]{1,0:T(8,128)S(1)}, f32[256,128]{1,0:T(8,128)S(1)}, u32[]{:S(2)}, u32[]{:S(2)}) collective-permute-start(f32[256,128]{1,0:T(8,128)S(1)} %factor.1.own), channel_id=1, source_target_pairs={{0,1},{1,0},{2,3},{3,2},{4,5},{5,4},{6,7},{7,6},{8,9},{9,8},{10,11... | collective-permute-start | bytes 393224 | tf_op jit(solution)/shard_map/ppermute | solution.py:420

commit v3 on v2

--- a/solution.py
+++ b/solution.py
@@ -1,3 +1,4 @@
+import functools
 import math
 
 import jax
@@ -17,28 +18,25 @@
 BF16 = jnp.bfloat16
 
 
-def twiddle_table():
-    table = np.zeros((4, 16), np.float32)
-    for t in range(4):
-        for d in range(4):
-            angle = -2.0 * math.pi * (((t - d) % 4) * t) / 16.0
-            table[t, 2 * d] = math.cos(angle)
-            table[t, 2 * d + 1] = math.sin(angle)
-        for q in range(4):
-            angle = -2.0 * math.pi * (t / 32.0 + q / 8.0)
-            table[t, 8 + 2 * q] = math.cos(angle)
-            table[t, 9 + 2 * q] = math.sin(angle)
-    return table
-
-
-def phase_table():
-    table = np.zeros((4, 16), np.float32)
-    for t in range(4):
-        for q in range(8):
-            re, im = [(1, 0), (0, -1), (-1, 0), (0, 1)][(t * q) % 4]
-            table[t, 2 * q] = re
-            table[t, 2 * q + 1] = im
-    return table
+def by_bin(t, values):
+    values = [float(v) for v in values]
+    if len(set(values)) == 1:
+        return F32(values[0])
+    return jnp.where(
+        t < 2, jnp.where(t == 0, values[0], values[1]), jnp.where(t == 2, values[2], values[3])
+    ).astype(F32)
+
+
+def unit(t, angles):
+    return by_bin(t, np.cos(angles)), by_bin(t, np.sin(angles))
+
+
+def source_twiddle(t, d):
+    return unit(t, [-2.0 * math.pi * (((b - d) % 4) * b) / 16.0 for b in range(4)])
+
+
+def second_twiddle(t, q):
+    return unit(t, [-2.0 * math.pi * (b / 32.0 + q / 8.0) for b in range(4)])
 
 
 def split(value):
@@ -87,12 +85,15 @@
     return jnp.where(sub % 4 < 2, pltpu.roll(value, 6, 0), pltpu.roll(value, 2, 0))
 
 
-def gram_kernel(own, near1, near2, near3, weight16, twiddle, sh_ref, sl_ref, keep_ref, send_ref, work, mixed):
+def gram_kernel(own, near3, near1, near2, weight, sh_ref, sl_ref, keep_ref, send_ref, work, mixed):
     t = lax.axis_index("tm")
-    root = jnp.sqrt(weight16[...])
+    root = jnp.sqrt(jnp.concatenate([weight[...]] * 4, axis=0))
     sources = (own, near1, near2, near3)
-    tw = [(root * twiddle[t, 2 * d], root * twiddle[t, 2 * d + 1]) for d in range(4)]
-    tq = [(twiddle[t, 8 + 2 * q], twiddle[t, 9 + 2 * q]) for q in range(4)]
+    tw = []
+    for d in range(4):
+        re, im = source_twiddle(t, d)
+        tw.append((root * re, root * im))
+    tq = [second_twiddle(t, q) for q in range(4)]
 
     def transform(step, _):
         row = pl.multiple_of(step * 16, 16)
@@ -264,9 +265,14 @@
             )
 
 
-def modes_kernel(own, far, sh_ref, sl_ref, weight, phase, modes_ref, upper_ref, turned, work, natural):
+def modes_kernel(slot, *refs):
+    if slot == 0:
+        source, sh_ref, sl_ref, weight = refs[:4]
+    else:
+        source, sh_ref, sl_ref, weight, _, _ = refs[:6]
+    modes_ref, upper_ref, turned, work, natural, modes_own, upper_own, modes_sem, upper_sem = refs[-9:]
     t = lax.axis_index("tm")
-    mine = lax.axis_index("space") % 2
+    mine = (lax.axis_index("space") + slot) % 2
     wide = (WIDTH, LANES)
     lane = lane_iota(wide)
     order = lax.broadcasted_iota(jnp.int32, wide, 0)
@@ -277,35 +283,38 @@
     natural_index = lane8 // WIDTH * WIDTH + lane8 % 4 * 16 + lane8 % WIDTH // 4
     root = lax.rsqrt(weight[...])
 
-    for slot, source in enumerate((own, far)):
-        tiles = []
-        for a in range(8):
-            tiles.append(
-                jnp.concatenate(
-                    [source[pl.ds(a + 8 * odd, 16, stride=16), :] for odd in range(2)], axis=0
-                )
+    tiles = []
+    for a in range(8):
+        tiles.append(
+            jnp.concatenate(
+                [source[pl.ds(a + 8 * odd, 16, stride=16), :] for odd in range(2)], axis=0
             )
-        for b, tile in enumerate(block_transpose(tiles)):
-            turned[slot, b % 4, b // 4 * 32 : b // 4 * 32 + 32, :] = tile
-
-    def emit(index, _):
-        slot = index // 4
-        q = ((mine + slot) % 2) * 4 + index % 4
-        both = turned[slot, index % 4]
+        )
+    for b, tile in enumerate(block_transpose(tiles)):
+        turned[b % 4, b // 4 * 32 : b // 4 * 32 + 32, :] = tile
+
+    copies = []
+    for k in range(4):
+        q = mine * 4 + k
+        both = turned[k]
         inverse = jnp.where(column <= line, both, 0.0)
         diag = jnp.where(left, 1.0 / both, 0.0)
         upper = jnp.where(column > line, both, jnp.where(column == line, diag, 0.0))
         for j in range(4):
             s = 2 * (j % 2) + j // 2
-            for k in range(2):
-                piece = gather_lanes(upper[j * 16 + k * 8 : j * 16 + k * 8 + 8], natural_index)
-                natural[pl.ds(s + 32 * k, 8, stride=4), :] = piece
-        upper_ref[0, q] = natural[:, :WIDTH]
-        upper_ref[1, q] = natural[:, WIDTH:]
+            for h in range(2):
+                piece = gather_lanes(upper[j * 16 + h * 8 : j * 16 + h * 8 + 8], natural_index)
+                natural[k, pl.ds(s + 32 * h, 8, stride=4), :] = piece
+        upper_own[0, k] = natural[k, :, :WIDTH]
+        upper_own[1, k] = natural[k, :, WIDTH:]
+        copies.append(
+            pltpu.make_async_copy(upper_own.at[:, k], upper_ref.at[:, q], upper_sem.at[k])
+        )
+        copies[-1].start()
         swapped = pltpu.roll(inverse, WIDTH, 1)
         swapped = jnp.where(left, -swapped, swapped)
-        pr = phase[t, 2 * q]
-        pi = phase[t, 2 * q + 1]
+        pr = by_bin(t, [(1, 0, -1, 0)[b * k % 4] for b in range(4)])
+        pi = by_bin(t, [(0, -1, 0, 1)[b * k % 4] for b in range(4)])
         lhs = jnp.concatenate([pr * inverse - pi * swapped, pr * swapped + pi * inverse], axis=0)
         lh, ll = split(lhs)
         sh = sh_ref[q]
@@ -317,26 +326,26 @@
                 block = out[part * WIDTH : (part + 1) * WIDTH, f * LANES : (f + 1) * LANES] * root[f : f + 1, :]
                 for j in range(4):
                     s = 2 * (j % 2) + j // 2
-                    work[pl.ds(part * ROWS + s * 4 + f, 16, stride=16), :] = block[j * 16 : j * 16 + 16]
-            modes_ref[part, q] = work[part * ROWS : (part + 1) * ROWS, :].astype(BF16)
-        return 0
-
-    lax.fori_loop(0, SUBS, emit, 0)
+                    work[k % 2, pl.ds(part * ROWS + s * 4 + f, 16, stride=16), :] = block[j * 16 : j * 16 + 16]
+            modes_own[part, k] = work[k % 2, part * ROWS : (part + 1) * ROWS, :].astype(BF16)
+        copies.append(
+            pltpu.make_async_copy(modes_own.at[:, k], modes_ref.at[:, q], modes_sem.at[k])
+        )
+        copies[-1].start()
+    for copy in copies:
+        copy.wait()
 
 
 def vmem():
     return pl.BlockSpec(memory_space=pltpu.VMEM)
 
 
-def smem():
-    return pl.BlockSpec(memory_space=pltpu.SMEM)
-
-
 HALF = (LANES, LANES)
+ORDER = (3, 1, 2)
 PARAMS = pltpu.CompilerParams(vmem_limit_bytes=32 * 1024 * 1024)
 
 
-def run_gram(own, near, weight16, table):
+def run_gram(own, near, weights):
     return pl.pallas_call(
         gram_kernel,
         name="gram",
@@ -346,11 +355,11 @@
             jax.ShapeDtypeStruct(HALF, F32),
             jax.ShapeDtypeStruct(HALF, F32),
         ),
-        in_specs=[vmem()] * 5 + [smem()],
+        in_specs=[vmem()] * 5,
         out_specs=(vmem(),) * 4,
         scratch_shapes=[pltpu.VMEM((SUBS, 2, ROWS, LANES), F32), pltpu.VMEM((ROWS, LANES), F32)],
         compiler_params=PARAMS,
-    )(own, *near, weight16, table)
+    )(own, *near, weights)
 
 
 def run_factor(gram):
@@ -364,23 +373,30 @@
     )(gram)
 
 
-def run_modes(own, far, sh, sl, weights, table):
+def run_modes(slot, factor, sh, sl, weights, outputs=()):
+    anywhere = pl.BlockSpec(memory_space=pl.ANY)
     return pl.pallas_call(
-        modes_kernel,
-        name="modes",
+        functools.partial(modes_kernel, slot),
+        name="modes_far" if slot else "modes_own",
         out_shape=(
             jax.ShapeDtypeStruct((2, SUBS, ROWS, LANES), BF16),
             jax.ShapeDtypeStruct((2, SUBS, WIDTH, WIDTH), F32),
         ),
-        in_specs=[vmem()] * 5 + [smem()],
-        out_specs=(vmem(), vmem()),
+        in_specs=[vmem()] * 4 + [anywhere] * len(outputs),
+        out_specs=(anywhere, anywhere),
         scratch_shapes=[
-            pltpu.VMEM((2, 4, WIDTH, LANES), F32),
-            pltpu.VMEM((2 * ROWS, LANES), F32),
-            pltpu.VMEM((WIDTH, LANES), F32),
+            pltpu.VMEM((4, WIDTH, LANES), F32),
+            pltpu.VMEM((2, 2 * ROWS, LANES), F32),
+            pltpu.VMEM((4, WIDTH, LANES), F32),
+            pltpu.VMEM((2, 4, ROWS, LANES), BF16),
+            pltpu.VMEM((2, 4, WIDTH, WIDTH), F32),
+            pltpu.SemaphoreType.DMA((4,)),
+            pltpu.SemaphoreType.DMA((4,)),
         ],
+        input_output_aliases={4: 0, 5: 1} if outputs else {},
         compiler_params=PARAMS,
-    )(own, far, sh, sl, weights, table)
+        cost_estimate=pl.CostEstimate(flops=3 * 10**8, bytes_accessed=2**22, transcendentals=0),
+    )(factor, sh, sl, weights, *outputs)
 
 
 def space_perm(along, shift):
@@ -399,26 +415,30 @@
 
 def sum_over_chips(value):
     for along in ("x", "z"):
-        far = [lax.ppermute(value, "space", space_perm(along, d)) for d in (1, 3, 2)]
-        value = (value + far[2]) + (far[0] + far[1])
+        far = [lax.ppermute(value, "space", space_perm(along, d)) for d in (3, 1, 2)]
+        value = ((value + far[0]) + far[1]) + far[2]
     return value
 
 
 def on_device(spectra, weights):
     t = lax.axis_index("tm")
     flat = spectra.reshape(2, 2, 4, ROWS, LANES)
-    own = lax.dynamic_index_in_dim(flat, t, 2, keepdims=False)
-    near = []
-    for d in range(1, 4):
-        piece = lax.dynamic_index_in_dim(flat, (t + d) % 4, 2, keepdims=False)
-        near.append(lax.ppermute(piece, "tm", [(i, (i + d) % 4) for i in range(4)]))
-    weight16 = jnp.tile(weights, (4, 1))
-    sh, sl, keep, send = run_gram(own, near, weight16, jnp.asarray(twiddle_table()))
+
+    def piece(d):
+        source = lax.optimization_barrier(flat)
+        return lax.dynamic_index_in_dim(source, (t + d) % 4, 2, keepdims=False)
+
+    near = {}
+    for d in ORDER:
+        near[d] = lax.ppermute(piece(d), "tm", [(i, (i + d) % 4) for i in range(4)])
+    own = piece(0)
+    sh, sl, keep, send = run_gram(own, [near[d] for d in ORDER], weights)
     across = space_perm("core", 1)
     gram = sum_over_chips(keep + lax.ppermute(send, "space", across))
     factor = run_factor(gram)
     far = lax.ppermute(factor, "space", across)
-    modes, upper = run_modes(factor, far, sh, sl, weights, jnp.asarray(phase_table()))
+    outputs = run_modes(0, factor, sh, sl, weights)
+    modes, upper = run_modes(1, far, sh, sl, weights, outputs)
     return (
         modes.reshape(2, SUBS, 1, WIDTH, FIELDS, LANES),
         upper.reshape(2, SUBS, 1, WIDTH, WIDTH),

time: 55.3 us -> 48.2 us (0.87)
  waiting for transfers between devices: 23.8 us -> 14.2 us
  starting transfers between devices: 17.7 us -> 22.3 us
  Pallas kernels: 10.9 us -> 9.38 us
  local copies, waits for them, and re-layouts: 1.99 us -> 1.3 us
    ppermute x3, waiting for transfers between devices: 14.3 us -> 9.71 us  [on_device(): near[d] = lax.ppermute(piece(d), 'tm', [(i, (i + d) % 4) for i in range(4)])]
    ppermute x6, waiting for transfers between devices: 7.61 us -> 3.6 us  [sum_over_chips(): lax.ppermute(value, 'space', space_perm(along, d))]
    ppermute x6, starting transfers between devices: 9.41 us -> 11.9 us  [sum_over_chips(): lax.ppermute(value, 'space', space_perm(along, d))]
    ppermute x3, starting transfers between devices: 4.67 us -> 6.5 us  [on_device(): near[d] = lax.ppermute(piece(d), 'tm', [(i, (i + d) % 4) for i in range(4)])]
    ppermute x1, waiting for transfers between devices: 0.99 us -> 0.01 us  [on_device(): far = lax.ppermute(factor, 'space', across)]
    pallas_call x1 -> x2, Pallas kernels: 4.94 us -> 3.98 us  [run_modes(): pl.pallas_call(functools.partial(modes_kernel, slot), name='modes_far' if...]
    unnamed x6 -> x2, local copies, waits for them, and re-layouts: 0.7 us -> 0.01 us
    pallas_call x1, Pallas kernels: 3.33 us -> 2.76 us  [run_gram(): pl.pallas_call(gram_kernel, name='gram', out_shape=(jax.ShapeDtypeStruct(...]
  transfers between devices with their start and end apart: 11 -> 11, of which waited for: 7 -> 5; matrix products, arithmetic and copies ran while one was open for 0% -> 0% of each run, Pallas kernels for 0% -> 4%
where the time goes in v3:
time: 48.2 us; the launch traced here: 48 us
  starting transfers between devices  22.3 us (46%)
  waiting for transfers between devices  14.2 us (29%)
  Pallas kernels  9.38 us (19%)
  local copies, waits for them, and re-layouts  1.3 us (3%)
  between operations  0.75 us (2%)
    ppermute x6, starting transfers between devices, sum_over_chips(): lax.ppermute(value, 'space', space_perm(along, d))  11.9 us
    ppermute x3, waiting for transfers between devices, on_device(): near[d] = lax.ppermute(piece(d), 'tm', [(i, (i + d) % 4) for i in range(4)])  9.71 us
    ppermute x3, starting transfers between devices, on_device(): near[d] = lax.ppermute(piece(d), 'tm', [(i, (i + d) % 4) for i in range(4)])  6.5 us
    pallas_call x2, Pallas kernels, run_modes(): pl.pallas_call(functools.partial(modes_kernel, slot), name='modes_far' if...  3.98 us
    ppermute x6, waiting for transfers between devices, sum_over_chips(): lax.ppermute(value, 'space', space_perm(along, d))  3.6 us
    ppermute x1, starting transfers between devices, on_device(): far = lax.ppermute(factor, 'space', across)  2.99 us
    pallas_call x1, Pallas kernels, run_gram(): pl.pallas_call(gram_kernel, name='gram', out_shape=(jax.ShapeDtypeStruct(...  2.76 us
    pallas_call x1, Pallas kernels, run_factor(): pl.pallas_call(factor_kernel, name='factor', out_shape=jax.ShapeDtypeStru...  2.65 us
  transfers between devices with their start and end apart: 11, of which 5 were waited for; matrix products, arithmetic and copies ran while one was open for 0% of the time, Pallas kernels for 4%

profile of v3, /device:TPU:1, one launch (start us, length us, event | category | flops | bytes accessed | tf_op | source)
XLA Modules:
  0.0 48.0 jit_solution(3207930338621165615)
XLA Ops:
  0.7 1.3 %dynamic-slice_bitcast_fusion = (bf16[2,2,256,128]{3,2,1,0:T(8,128)(2,1)S(1)}, bf16[2,2,256,128]{3,2,1,0:T(8,128)(2,1)S(1)}, bf16[2,2,256,128]{3,2,1,0:T(8,128)(2,1)S(1)}, bf16[2,2,256,128]{3,2,1,0:T(8,128)(2,1)S(1)}) fusion(bf16[2,2,4,256,128]{4,3,2,1,0:T(8,128)(2,1)} %bitcast.24, s32[]{:T(128)S(6)} %select_n.39, s32[]{:T(128)S(6)} %select_n.37, ...), kind=kLoop, calls=%fused_computation | loop fusion | bytes 2097168 | tf_op jit(solution)/shard_map/jit(dynamic_index_in_dim)/squeeze | solution.py:429
  2.0 3.8 %collective-permute-start.2 = (bf16[2,2,256,128]{3,2,1,0:T(8,128)(2,1)S(1)}, bf16[2,2,256,128]{3,2,1,0:T(8,128)(2,1)S(1)}, u32[]{:S(2)}, u32[]{:S(2)}) collective-permute-start(bf16[2,2,256,128]{3,2,1,0:T(8,128)(2,1)S(1)} %get-tuple-element.20), channel_id=1, source_target_pairs={{0,64},{32,96},{64,0},{96,32},{1,65},{33,97},{65,1},{97,33},{2,66}... | collective-permute-start | bytes 786440 | tf_op jit(solution)/shard_map/ppermute | solution.py:433
  5.8 0.0 copy-start
  5.8 0.4 collective-permute-start.1
  6.2 2.3 %collective-permute-start = (bf16[2,2,256,128]{3,2,1,0:T(8,128)(2,1)S(1)}, bf16[2,2,256,128]{3,2,1,0:T(8,128)(2,1)S(1)}, u32[]{:S(2)}, u32[]{:S(2)}) collective-permute-start(bf16[2,2,256,128]{3,2,1,0:T(8,128)(2,1)S(1)} %get-tuple-element.22), channel_id=1, source_target_pairs={{0,96},{32,0},{64,32},{96,64},{1,97},{33,1},{65,33},{97,65},{2,98}... | collective-permute-start | bytes 786440 | tf_op jit(solution)/shard_map/ppermute | solution.py:433
  8.5 3.1 %collective-permute-done.2.near2 = bf16[2,2,256,128]{3,2,1,0:T(8,128)(2,1)S(1)} collective-permute-done((bf16[2,2,256,128]{3,2,1,0:T(8,128)(2,1)S(1)}, bf16[2,2,256,128]{3,2,1,0:T(8,128)(2,1)S(1)}, u32[]{:S(2)}, u32[]{:S(2)}) %collective-permute-start.2) | collective-permute-done | bytes 262176 | tf_op jit(solution)/shard_map/ppermute | solution.py:433
  11.6 6.6 %collective-permute-done.1.near1 = bf16[2,2,256,128]{3,2,1,0:T(8,128)(2,1)S(1)} collective-permute-done((bf16[2,2,256,128]{3,2,1,0:T(8,128)(2,1)S(1)}, bf16[2,2,256,128]{3,2,1,0:T(8,128)(2,1)S(1)}, u32[]{:S(2)}, u32[]{:S(2)}) %collective-permute-start.1) | collective-permute-done | bytes 262176 | tf_op jit(solution)/shard_map/ppermute | solution.py:433
  18.2 0.0 collective-permute-done.near3
  18.2 0.0 copy-done
  18.2 2.8 %gram.1 = (bf16[8,128,512]{2,1,0:T(8,128)(2,1)S(1)}, bf16[8,128,512]{2,1,0:T(8,128)(2,1)S(1)}, f32[128,128]{1,0:T(8,128)S(1)}, f32[128,128]{1,0:T(8,128)S(1)}) custom-call(bf16[2,2,256,128]{3,2,1,0:T(8,128)(2,1)S(1)} %get-tuple-element.23.own, bf16[2,2,256,128]{3,2,1,0:T(8,128)(2,1)S(1)} %collective-permute-done.near3, ...), custom_call_target="tpu_custom_call" | custom-call | tf_op jit(solution)/shard_map/gram/pallas_call | solution.py:349
  21.0 1.0 %collective-permute-start.3 = (f32[128,128]{1,0:T(8,128)S(1)}, f32[128,128]{1,0:T(8,128)S(1)}, u32[]{:S(2)}, u32[]{:S(2)}) collective-permute-start(f32[128,128]{1,0:T(8,128)S(1)} %get-tuple-element.11), channel_id=1, source_target_pairs={{0,1},{1,0},{2,3},{3,2},{4,5},{5,4},{6,7},{7,6},{8,9},{9,8},{10,11... | collective-permute-start | bytes 196616 | tf_op jit(solution)/shard_map/ppermute | solution.py:437
  22.0 0.9 %collective-permute-done.3 = f32[128,128]{1,0:T(8,128)S(1)} collective-permute-done((f32[128,128]{1,0:T(8,128)S(1)}, f32[128,128]{1,0:T(8,128)S(1)}, u32[]{:S(2)}, u32[]{:S(2)}) %collective-permute-start.3) | collective-permute-done | bytes 65568 | tf_op jit(solution)/shard_map/ppermute | solution.py:437
  22.9 2.8 %collective-permute-start.6 = (f32[128,128]{1,0:T(8,128)S(1)}, f32[128,128]{1,0:T(8,128)S(1)}, u32[]{:S(2)}, u32[]{:S(2)}) collective-permute-start(f32[128,128]{1,0:T(8,128)S(1)} %add.67), channel_id=1, source_target_pairs={{0,4},{1,5},{2,6},{3,7},{4,0},{5,1},{6,2},{7,3},{8,12},{9,13},{10,... | collective-permute-start | bytes 196616 | tf_op jit(solution)/shard_map/ppermute | solution.py:418
  25.7 0.3 collective-permute-start.5
  26.0 2.4 %collective-permute-start.4 = (f32[128,128]{1,0:T(8,128)S(1)}, f32[128,128]{1,0:T(8,128)S(1)}, u32[]{:S(2)}, u32[]{:S(2)}) collective-permute-start(f32[128,128]{1,0:T(8,128)S(1)} %add.67), channel_id=1, source_target_pairs={{0,6},{1,7},{2,0},{3,1},{4,2},{5,3},{6,4},{7,5},{8,14},{9,15},{10,... | collective-permute-start | bytes 196616 | tf_op jit(solution)/shard_map/ppermute | solution.py:418
  28.4 0.0 collective-permute-done.6
  28.4 1.6 %collective-permute-done.5 = f32[128,128]{1,0:T(8,128)S(1)} collective-permute-done((f32[128,128]{1,0:T(8,128)S(1)}, f32[128,128]{1,0:T(8,128)S(1)}, u32[]{:S(2)}, u32[]{:S(2)}) %collective-permute-start.5) | collective-permute-done | bytes 65568 | tf_op jit(solution)/shard_map/ppermute | solution.py:418
  30.0 0.0 collective-permute-done.4
  30.1 3.7 %collective-permute-start.9 = (f32[128,128]{1,0:T(8,128)S(1)}, f32[128,128]{1,0:T(8,128)S(1)}, u32[]{:S(2)}, u32[]{:S(2)}) collective-permute-start(f32[128,128]{1,0:T(8,128)S(1)} %add_add_fusion.1), channel_id=1, source_target_pairs={{0,16},{1,17},{2,18},{3,19},{4,20},{5,21},{6,22},{7,23},{8,24},{9,... | collective-permute-start | bytes 196616 | tf_op jit(solution)/shard_map/ppermute | solution.py:418
  33.7 0.7 %collective-permute-start.8 = (f32[128,128]{1,0:T(8,128)S(1)}, f32[128,128]{1,0:T(8,128)S(1)}, u32[]{:S(2)}, u32[]{:S(2)}) collective-permute-start(f32[128,128]{1,0:T(8,128)S(1)} %add_add_fusion.1), channel_id=1, source_target_pairs={{0,8},{1,9},{2,10},{3,11},{4,12},{5,13},{6,14},{7,15},{8,16},{9,17... | collective-permute-start | bytes 196616 | tf_op jit(solution)/shard_map/ppermute | solution.py:418
  34.5 1.9 %collective-permute-start.7 = (f32[128,128]{1,0:T(8,128)S(1)}, f32[128,128]{1,0:T(8,128)S(1)}, u32[]{:S(2)}, u32[]{:S(2)}) collective-permute-start(f32[128,128]{1,0:T(8,128)S(1)} %add_add_fusion.1), channel_id=1, source_target_pairs={{0,24},{1,25},{2,26},{3,27},{4,28},{5,29},{6,30},{7,31},{8,0},{9,1... | collective-permute-start | bytes 196616 | tf_op jit(solution)/shard_map/ppermute | solution.py:418
  36.4 0.0 collective-permute-done.9
  36.4 1.9 %collective-permute-done.8 = f32[128,128]{1,0:T(8,128)S(1)} collective-permute-done((f32[128,128]{1,0:T(8,128)S(1)}, f32[128,128]{1,0:T(8,128)S(1)}, u32[]{:S(2)}, u32[]{:S(2)}) %collective-permute-start.8) | collective-permute-done | bytes 65568 | tf_op jit(solution)/shard_map/ppermute | solution.py:418
  38.4 0.0 collective-permute-done.7
  38.4 2.6 %factor.1.refs_0_ = f32[256,128]{1,0:T(8,128)S(1)} custom-call(f32[128,128]{1,0:T(8,128)S(1)} %add_add_fusion.gram), custom_call_target="tpu_custom_call" | custom-call | tf_op jit(solution)/shard_map/factor/pallas_call | solution.py:366
  41.0 3.0 %collective-permute-start.10 = (f32[256,128]{1,0:T(8,128)S(1)}, f32[256,128]{1,0:T(8,128)S(1)}, u32[]{:S(2)}, u32[]{:S(2)}) collective-permute-start(f32[256,128]{1,0:T(8,128)S(1)} %factor.1.refs_0_), channel_id=1, source_target_pairs={{0,1},{1,0},{2,3},{3,2},{4,5},{5,4},{6,7},{7,6},{8,9},{9,8},{10,11... | collective-permute-start | bytes 393224 | tf_op jit(solution)/shard_map/ppermute | solution.py:439
  44.0 2.0 %modes_own.1 = (bf16[2,8,256,128]{3,2,1,0:T(8,128)(2,1)}, f32[2,8,64,64]{3,2,1,0:T(8,128)}) custom-call(f32[256,128]{1,0:T(8,128)S(1)} %factor.1.refs_0_, bf16[8,128,512]{2,1,0:T(8,128)(2,1)S(1)} %get-tuple-element.12.refs_1_, bf16[8,128,512]{2,1,0:T(8,128)(2,1)S(1)} %get-tuple-element.13.refs_2_, f32[4,128]{1,0:T(4,128)S(1)} %copy-done), custom_call_target="tpu_custom_call" | custom-call | flops 300000000 | bytes 4194304 | tf_op jit(solution)/shard_map/modes_own/pallas_call | solution.py:378
  46.0 0.0 collective-permute-done.10.refs_0_
  46.0 2.0 %modes_far.1 = (bf16[2,8,256,128]{3,2,1,0:T(8,128)(2,1)}, f32[2,8,64,64]{3,2,1,0:T(8,128)}) custom-call(f32[256,128]{1,0:T(8,128)S(1)} %collective-permute-done.10.refs_0_, bf16[8,128,512]{2,1,0:T(8,128)(2,1)S(1)} %get-tuple-element.12.refs_1_, bf16[8,128,512]{2,1,0:T(8,128)(2,1)S(1)} %get-tuple-element.13.refs_2_, ...), custom_call_target="tpu_custom_call", output_to_operand_aliasing={{0}: (4, {}), {1}: (5, {})} | custom-call | flops 300000000 | bytes 4194304 | tf_op jit(solution)/shard_map/modes_far/pallas_call | solution.py:378
  (3 shorter events, 0.0 us)
Async XLA Ops:
  2.0 9.6 %collective-permute-start.2 = (bf16[2,2,256,128]{3,2,1,0:T(8,128)(2,1)S(1)}, bf16[2,2,256,128]{3,2,1,0:T(8,128)(2,1)S(1)}, u32[]{:S(2)}, u32[]{:S(2)}) collective-permute-start(bf16[2,2,256,128]{3,2,1,0:T(8,128)(2,1)S(1)} %get-tuple-element.20), channel_id=1, source_target_pairs={{0,64},{32,96},{64,0},{96,32},{1,65},{33,97},{65,1},{97,33},{2,66}... | collective-permute-start | bytes 786440 | tf_op jit(solution)/shard_map/ppermute | solution.py:433
  5.8 12.4 %copy-start = (f32[4,128]{1,0:T(4,128)S(1)}, f32[4,128]{1,0:T(4,128)}, u32[]{:S(2)}) copy-start(f32[4,128]{1,0:T(4,128)} %refs_3_.3) | copy-start | bytes 6148
  5.8 12.4 %collective-permute-start.1 = (bf16[2,2,256,128]{3,2,1,0:T(8,128)(2,1)S(1)}, bf16[2,2,256,128]{3,2,1,0:T(8,128)(2,1)S(1)}, u32[]{:S(2)}, u32[]{:S(2)}) collective-permute-start(bf16[2,2,256,128]{3,2,1,0:T(8,128)(2,1)S(1)} %get-tuple-element.21), channel_id=1, source_target_pairs={{0,32},{32,64},{64,96},{96,0},{1,33},{33,65},{65,97},{97,1},{2,34}... | collective-permute-start | bytes 786440 | tf_op jit(solution)/shard_map/ppermute | solution.py:433
  6.2 12.0 %collective-permute-start = (bf16[2,2,256,128]{3,2,1,0:T(8,128)(2,1)S(1)}, bf16[2,2,256,128]{3,2,1,0:T(8,128)(2,1)S(1)}, u32[]{:S(2)}, u32[]{:S(2)}) collective-permute-start(bf16[2,2,256,128]{3,2,1,0:T(8,128)(2,1)S(1)} %get-tuple-element.22), channel_id=1, source_target_pairs={{0,96},{32,0},{64,32},{96,64},{1,97},{33,1},{65,33},{97,65},{2,98}... | collective-permute-start | bytes 786440 | tf_op jit(solution)/shard_map/ppermute | solution.py:433
  21.0 1.9 %collective-permute-start.3 = (f32[128,128]{1,0:T(8,128)S(1)}, f32[128,128]{1,0:T(8,128)S(1)}, u32[]{:S(2)}, u32[]{:S(2)}) collective-permute-start(f32[128,128]{1,0:T(8,128)S(1)} %get-tuple-element.11), channel_id=1, source_target_pairs={{0,1},{1,0},{2,3},{3,2},{4,5},{5,4},{6,7},{7,6},{8,9},{9,8},{10,11... | collective-permute-start | bytes 196616 | tf_op jit(solution)/shard_map/ppermute | solution.py:437
  22.9 5.5 %collective-permute-start.6 = (f32[128,128]{1,0:T(8,128)S(1)}, f32[128,128]{1,0:T(8,128)S(1)}, u32[]{:S(2)}, u32[]{:S(2)}) collective-permute-start(f32[128,128]{1,0:T(8,128)S(1)} %add.67), channel_id=1, source_target_pairs={{0,4},{1,5},{2,6},{3,7},{4,0},{5,1},{6,2},{7,3},{8,12},{9,13},{10,... | collective-permute-start | bytes 196616 | tf_op jit(solution)/shard_map/ppermute | solution.py:418
  25.7 4.3 %collective-permute-start.5 = (f32[128,128]{1,0:T(8,128)S(1)}, f32[128,128]{1,0:T(8,128)S(1)}, u32[]{:S(2)}, u32[]{:S(2)}) collective-permute-start(f32[128,128]{1,0:T(8,128)S(1)} %add.67), channel_id=1, source_target_pairs={{0,2},{1,3},{2,4},{3,5},{4,6},{5,7},{6,0},{7,1},{8,10},{9,11},{10,... | collective-permute-start | bytes 196616 | tf_op jit(solution)/shard_map/ppermute | solution.py:418
  26.0 4.0 %collective-permute-start.4 = (f32[128,128]{1,0:T(8,128)S(1)}, f32[128,128]{1,0:T(8,128)S(1)}, u32[]{:S(2)}, u32[]{:S(2)}) collective-permute-start(f32[128,128]{1,0:T(8,128)S(1)} %add.67), channel_id=1, source_target_pairs={{0,6},{1,7},{2,0},{3,1},{4,2},{5,3},{6,4},{7,5},{8,14},{9,15},{10,... | collective-permute-start | bytes 196616 | tf_op jit(solution)/shard_map/ppermute | solution.py:418
  30.1 6.4 %collective-permute-start.9 = (f32[128,128]{1,0:T(8,128)S(1)}, f32[128,128]{1,0:T(8,128)S(1)}, u32[]{:S(2)}, u32[]{:S(2)}) collective-permute-start(f32[128,128]{1,0:T(8,128)S(1)} %add_add_fusion.1), channel_id=1, source_target_pairs={{0,16},{1,17},{2,18},{3,19},{4,20},{5,21},{6,22},{7,23},{8,24},{9,... | collective-permute-start | bytes 196616 | tf_op jit(solution)/shard_map/ppermute | solution.py:418
  33.7 4.6 %collective-permute-start.8 = (f32[128,128]{1,0:T(8,128)S(1)}, f32[128,128]{1,0:T(8,128)S(1)}, u32[]{:S(2)}, u32[]{:S(2)}) collective-permute-start(f32[128,128]{1,0:T(8,128)S(1)} %add_add_fusion.1), channel_id=1, source_target_pairs={{0,8},{1,9},{2,10},{3,11},{4,12},{5,13},{6,14},{7,15},{8,16},{9,17... | collective-permute-start | bytes 196616 | tf_op jit(solution)/shard_map/ppermute | solution.py:418
  34.5 3.9 %collective-permute-start.7 = (f32[128,128]{1,0:T(8,128)S(1)}, f32[128,128]{1,0:T(8,128)S(1)}, u32[]{:S(2)}, u32[]{:S(2)}) collective-permute-start(f32[128,128]{1,0:T(8,128)S(1)} %add_add_fusion.1), channel_id=1, source_target_pairs={{0,24},{1,25},{2,26},{3,27},{4,28},{5,29},{6,30},{7,31},{8,0},{9,1... | collective-permute-start | bytes 196616 | tf_op jit(solution)/shard_map/ppermute | solution.py:418
  41.0 5.0 %collective-permute-start.10 = (f32[256,128]{1,0:T(8,128)S(1)}, f32[256,128]{1,0:T(8,128)S(1)}, u32[]{:S(2)}, u32[]{:S(2)}) collective-permute-start(f32[256,128]{1,0:T(8,128)S(1)} %factor.1.refs_0_), channel_id=1, source_target_pairs={{0,1},{1,0},{2,3},{3,2},{4,5},{5,4},{6,7},{7,6},{8,9},{9,8},{10,11... | collective-permute-start | bytes 393224 | tf_op jit(solution)/shard_map/ppermute | solution.py:439

commit v4 on v3

v4 whole, which is shorter than its diff:
```python
import functools
import math

import jax
import jax.numpy as jnp
import numpy as np
from jax import lax
from jax.experimental import pallas as pl
from jax.experimental.pallas import tpu as pltpu
from jax.sharding import PartitionSpec as P

SUBS = 8
WIDTH = 64
FIELDS = 4
LANES = 128
ROWS = WIDTH * FIELDS
F32 = jnp.float32
BF16 = jnp.bfloat16


def by_bin(t, values):
    values = [float(v) for v in values]
    if len(set(values)) == 1:
        return F32(values[0])
    return jnp.where(
        t < 2, jnp.where(t == 0, values[0], values[1]), jnp.where(t == 2, values[2], values[3])
    ).astype(F32)


def unit(t, angles):
    return by_bin(t, np.cos(angles)), by_bin(t, np.sin(angles))


def source_twiddle(t, d):
    return unit(t, [-2.0 * math.pi * (((b - d) % 4) * b) / 16.0 for b in range(4)])


def second_twiddle(t, q):
    return unit(t, [-2.0 * math.pi * (b / 32.0 + q / 8.0) for b in range(4)])


def split(value):
    high = value.astype(BF16)
    return high, (value - high.astype(F32)).astype(BF16)


def lane_iota(shape):
    return lax.broadcasted_iota(jnp.int32, shape, len(shape) - 1)


SMALL = (8, LANES)


def places():
    lane = lane_iota(SMALL)
    sub = lax.broadcasted_iota(jnp.int32, SMALL, 0)
    parity = lane // WIDTH
    group = lane % 16
    return lane, sub, parity, group, group * 4 + sub % 4


def block_transpose(tiles):
    block = lane_iota(tiles[0].shape) // 16
    for bit in range(3):
        step = 1 << bit
        low = (block & step) == 0
        out = list(tiles)
        for x in range(8):
            if x & step == 0:
                y = x | step
                out[x] = jnp.where(low, tiles[x], pltpu.roll(tiles[y], 16 * step, 1))
                out[y] = jnp.where(low, pltpu.roll(tiles[x], LANES - 16 * step, 1), tiles[y])
        tiles = out
    return tiles


def gather_lanes(value, index):
    return jnp.take_along_axis(value, index, axis=1)


def reverse_rows(value, lane, sub):
    index = (1 - lane // WIDTH) * WIDTH + (lane % WIDTH) // 16 * 16 + 15 - lane % 16
    value = gather_lanes(value, index)
    value = jnp.where(sub % 2 == 0, pltpu.roll(value, 7, 0), pltpu.roll(value, 1, 0))
    return jnp.where(sub % 4 < 2, pltpu.roll(value, 6, 0), pltpu.roll(value, 2, 0))


def pack_gram(work, s_ref, out_ref, mixed, products):
    left = lane_iota((WIDTH, LANES)) < WIDTH
    for q in range(4):
        for part in range(2):
            for f in range(FIELDS):
                for j in range(4):
                    value = work[q, part, pl.ds(j * 4 + f, 16, stride=16), :]
                    high, low = split(value)
                    row = part * WIDTH + j * 16
                    s_ref[q, row : row + 16, f * LANES : (f + 1) * LANES] = high
                    s_ref[q, LANES + row : LANES + row + 16, f * LANES : (f + 1) * LANES] = low

    for q in range(4):
        products[q] = lax.dot_general(
            s_ref[q], s_ref[q, :LANES], (((1,), (1,)), ((), ())), preferred_element_type=F32
        )

    tiles = [None] * 8
    for q in range(4):
        cross = products[q, LANES:]
        full = products[q, :LANES] + (cross + cross.T)
        low = pltpu.roll(full[WIDTH:], WIDTH, 1)
        tile = full[:WIDTH] + jnp.where(left, low, -low)
        for p in range(2):
            tiles[p * 4 + q] = jnp.concatenate(
                [tile[p * 16 : p * 16 + 16], tile[32 + p * 16 : 48 + p * 16]], axis=0
            )
    for a, tile in enumerate(block_transpose(tiles)):
        mixed[a * 32 : (a + 1) * 32, :] = tile
    lane, sub, parity, _, column = places()
    for m in range(16):
        near = mixed[pl.ds(m % 2 * 16 + m // 2, 8, stride=32), :]
        far_m = 31 - m
        far = mixed[pl.ds(far_m % 2 * 16 + far_m // 2, 8, stride=32), :]
        far = reverse_rows(far, lane, sub)
        line = 2 * m + parity
        far = jnp.where(column == line, pltpu.roll(far, 4, 0), far)
        upper = (column > line) | ((column == line) & (sub < 4))
        out_ref[m * 8 : (m + 1) * 8, :] = jnp.where(upper, near, far)


def send_kernel(own, near3, near1, near2, weight, other_ref, s_ref, send_ref, work, mixed, products):
    t = lax.axis_index("tm")
    side = jnp.where(lax.axis_index("space") % 2 == 0, -1.0, 1.0).astype(F32)
    root = jnp.sqrt(jnp.concatenate([weight[...]] * 4, axis=0))
    sources = (own, near1, near2, near3)
    tw = []
    for d in range(4):
        re, im = source_twiddle(t, d)
        tw.append((root * re, root * im))
    tq = []
    for q in range(4):
        re, im = second_twiddle(t, q)
        tq.append((re * side, im * side))

    def transform(step, _):
        row = pl.multiple_of(step * 16, 16)
        rows = pl.ds(row, 16)
        radix = []
        for s in range(2):
            y = []
            for d in range(4):
                re = sources[d][0, s, rows, :].astype(F32)
                im = sources[d][1, s, rows, :].astype(F32)
                y.append((re * tw[d][0] - im * tw[d][1], re * tw[d][1] + im * tw[d][0]))
            a = (y[0][0] + y[2][0], y[0][1] + y[2][1])
            b = (y[0][0] - y[2][0], y[0][1] - y[2][1])
            c = (y[1][0] + y[3][0], y[1][1] + y[3][1])
            e = (y[1][0] - y[3][0], y[1][1] - y[3][1])
            radix.append(
                [
                    (a[0] + c[0], a[1] + c[1]),
                    (b[0] - e[1], b[1] + e[0]),
                    (a[0] - c[0], a[1] - c[1]),
                    (b[0] + e[1], b[1] - e[0]),
                ]
            )
        for q in range(4):
            x0 = radix[0][q]
            x1 = radix[1][q]
            v = (x1[0] * tq[q][0] - x1[1] * tq[q][1], x1[0] * tq[q][1] + x1[1] * tq[q][0])
            work[q, 0, rows, :] = x0[0] + v[0]
            work[q, 1, rows, :] = x0[1] + v[1]
            other_ref[q, 0, rows, :] = x0[0] - v[0]
            other_ref[q, 1, rows, :] = x0[1] - v[1]
        return 0

    lax.fori_loop(0, ROWS // 16, transform, 0)
    pack_gram(work, s_ref, send_ref, mixed, products)


def at_sub(value, index):
    return jnp.broadcast_to(value[index : index + 1, :], value.shape)


def factor_kernel(gram, out_ref, spread):
    lane, sub, parity, group, column = places()
    first = parity == 0
    sign = jnp.where(sub < 4, 1.0, -1.0).astype(F32)
    real = sub < 4
    lane_base = lane // 16 * 16

    def turn(value):
        return pltpu.roll(value, 4, 0) * sign

    def lifted(value):
        return jnp.where(first, value, pltpu.roll(value, 7, 0))

    rows = [None] * 32
    for m in range(16):
        packed = gram[m * 8 : (m + 1) * 8, :]
        rows[m] = packed
        far = reverse_rows(packed, lane, sub)
        line = 2 * (31 - m) + parity
        rows[31 - m] = jnp.where(column == line, pltpu.roll(far, 4, 0), far)

    def block_of(v, p, g):
        return gather_lanes(v, lane % WIDTH // 16 * 16 + p * WIDTH + g)

    block = [block_of(rows[r // 2], r % 2, 0) for r in range(4)]
    for g in range(16):
        last = g == 15
        full, ahead, following = [], [], []
        for v in (rows[2 * g], rows[2 * g + 1]):
            turned = pltpu.roll(v, WIDTH, 1)
            full += [jnp.where(first, v, turned), jnp.where(first, turned, v)]
        if not last:
            ahead = [block_of(rows[2 * g + r // 2], r % 2, g + 1) for r in range(4)]
            following = [block_of(rows[2 * g + 2 + r // 2], r % 2, g + 1) for r in range(4)]
        in_group = group == g
        root, scaled = [], []
        for s in range(4):
            here = in_group & (sub % 4 == s)
            pivot = at_sub(block[s], s)
            ip = 1.0 / pivot
            root.append(lax.rsqrt(pivot))
            full[s] = jnp.where(here, jnp.where(real, 1.0, 0.0), full[s])
            y = full[s] * ip
            y_t = turn(y)
            b = block[s] * ip
            b_t = turn(b)
            if not last:
                n = ahead[s] * ip
                n_t = turn(n)
                for r in range(4):
                    mr = at_sub(ahead[s], r)
                    mi = at_sub(ahead[s], 4 + r)
                    following[r] = following[r] - (mr * n + mi * n_t)
            for r in range(s + 1, 4):
                mr = at_sub(block[s], r)
                mi = at_sub(block[s], 4 + r)
                full[r] = jnp.where(here, 0.0, full[r]) - (mr * y + mi * y_t)
                block[r] = block[r] - (mr * b + mi * b_t)
                if not last:
                    ahead[r] = ahead[r] - (mr * n + mi * n_t)
            later = in_group & (sub % 4 > s)
            scaled.append((jnp.where(later, 0.0, y), jnp.where(later, 0.0, y_t)))
        raised = [lifted(full[r]) for r in range(4)]
        for h in range(g + 1, 16):
            if h == g + 1:
                multi = [lifted(ahead[r]) for r in range(4)]
            else:
                multi = [gather_lanes(raised[r], lane_base + h) for r in range(4)]
            for odd in range(2):
                m = 2 * h + odd
                value = jnp.where(in_group, 0.0, rows[m])
                terms = []
                for r in range(4):
                    y, y_t = scaled[r]
                    terms.append(at_sub(multi[r], 2 * odd) * y + at_sub(multi[r], 4 + 2 * odd) * y_t)
                rows[m] = value - ((terms[0] + terms[1]) + (terms[2] + terms[3]))
        block = following
        for odd in range(2):
            m = 2 * g + odd
            spread[m * 8 : (m + 1) * 8, :] = jnp.where(
                first, full[2 * odd] * root[2 * odd], full[2 * odd + 1] * root[2 * odd + 1]
            )
        if g % 4 == 3:
            k = g // 4
            tiles = [spread[pl.ds(k * WIDTH + a, 8, stride=8), :] for a in range(8)]
            for b, tile in enumerate(block_transpose(tiles)):
                row = b // 4 * 32 + k * 8
                out_ref[b % 4, row : row + 8, :] = tile


def modes_kernel(slot, *refs):
    if slot == 0:
        source, s_ref, weight = refs[:3]
    else:
        source, s_ref, weight, _, _ = refs[:5]
    modes_ref, upper_ref, work, natural, modes_own, upper_own, modes_sem, upper_sem = refs[-8:]
    t = lax.axis_index("tm")
    mine = (lax.axis_index("space") + slot) % 2
    wide = (WIDTH, LANES)
    lane = lane_iota(wide)
    order = lax.broadcasted_iota(jnp.int32, wide, 0)
    line = order % 32 * 2 + order // 32
    column = lane % 16 * 4 + lane // 16 % 4
    left = lane < WIDTH
    lane8 = lane_iota(SMALL)
    natural_index = lane8 // WIDTH * WIDTH + lane8 % 4 * 16 + lane8 % WIDTH // 4
    root = lax.rsqrt(weight[...])

    copies = []
    for k in range(4):
        q = mine * 4 + k
        both = source[k]
        inverse = jnp.where(column <= line, both, 0.0)
        diag = jnp.where(left, 1.0 / both, 0.0)
        upper = jnp.where(column > line, both, jnp.where(column == line, diag, 0.0))
        for j in range(8):
            piece = gather_lanes(upper[j * 8 : j * 8 + 8], natural_index)
            natural[k, pl.ds(j // 4 + j % 4 * 16, 8, stride=2), :] = piece
        upper_own[0, k] = natural[k, :, :WIDTH]
        upper_own[1, k] = natural[k, :, WIDTH:]
        copies.append(
            pltpu.make_async_copy(upper_own.at[:, k], upper_ref.at[:, q], upper_sem.at[k])
        )
        copies[-1].start()
        swapped = pltpu.roll(inverse, WIDTH, 1)
        swapped = jnp.where(left, -swapped, swapped)
        pr = by_bin(t, [(1, 0, -1, 0)[b * k % 4] for b in range(4)])
        pi = by_bin(t, [(0, -1, 0, 1)[b * k % 4] for b in range(4)])
        lhs = jnp.concatenate([pr * inverse - pi * swapped, pr * swapped + pi * inverse], axis=0)
        lh, ll = split(lhs)
        out = jnp.dot(jnp.concatenate([lh, lh], axis=1), s_ref[k], preferred_element_type=F32)
        out = out + jnp.dot(ll, s_ref[k, :LANES], preferred_element_type=F32)
        for part in range(2):
            for f in range(FIELDS):
                for p in range(2):
                    row = part * WIDTH + p * 32
                    block = out[row : row + 32, f * LANES : (f + 1) * LANES] * root[f : f + 1, :]
                    work[k % 2, pl.ds(part * ROWS + p * 4 + f, 32, stride=8), :] = block
            modes_own[part, k] = work[k % 2, part * ROWS : (part + 1) * ROWS, :].astype(BF16)
        copies.append(
            pltpu.make_async_copy(modes_own.at[:, k], modes_ref.at[:, q], modes_sem.at[k])
        )
        copies[-1].start()
    for copy in copies:
        copy.wait()


def vmem():
    return pl.BlockSpec(memory_space=pltpu.VMEM)


HALF = (LANES, LANES)
ORDER = (3, 1, 2)
PARAMS = pltpu.CompilerParams(vmem_limit_bytes=32 * 1024 * 1024)


def run_send(own, near, weights):
    return pl.pallas_call(
        send_kernel,
        name="send_gram",
        out_shape=(
            jax.ShapeDtypeStruct((4, 2, ROWS, LANES), F32),
            jax.ShapeDtypeStruct((4, 2 * LANES, FIELDS * LANES), BF16),
            jax.ShapeDtypeStruct(HALF, F32),
        ),
        in_specs=[vmem()] * 5,
        out_specs=(vmem(),) * 3,
        scratch_shapes=[
            pltpu.VMEM((4, 2, ROWS, LANES), F32),
            pltpu.VMEM((ROWS, LANES), F32),
            pltpu.VMEM((4, 2 * LANES, LANES), F32),
        ],
        compiler_params=PARAMS,
    )(own, *near, weights)


def run_keep(work):
    return pl.pallas_call(
        pack_gram,
        name="keep_gram",
        out_shape=(
            jax.ShapeDtypeStruct((4, 2 * LANES, FIELDS * LANES), BF16),
            jax.ShapeDtypeStruct(HALF, F32),
        ),
        in_specs=[vmem()],
        out_specs=(vmem(),) * 2,
        scratch_shapes=[
            pltpu.VMEM((ROWS, LANES), F32),
            pltpu.VMEM((4, 2 * LANES, LANES), F32),
        ],
        compiler_params=PARAMS,
        cost_estimate=pl.CostEstimate(flops=3 * 10**8, bytes_accessed=2**21, transcendentals=0),
    )(work)


def run_factor(gram):
    return pl.pallas_call(
        factor_kernel,
        name="factor",
        out_shape=jax.ShapeDtypeStruct((4, WIDTH, LANES), F32),
        in_specs=[vmem()],
        out_specs=vmem(),
        scratch_shapes=[pltpu.VMEM((2 * LANES, LANES), F32)],
        compiler_params=PARAMS,
    )(gram)


def run_modes(slot, factor, s, weights, outputs=()):
    anywhere = pl.BlockSpec(memory_space=pl.ANY)
    return pl.pallas_call(
        functools.partial(modes_kernel, slot),
        name="modes_far" if slot else "modes_own",
        out_shape=(
            jax.ShapeDtypeStruct((2, SUBS, ROWS, LANES), BF16),
            jax.ShapeDtypeStruct((2, SUBS, WIDTH, WIDTH), F32),
        ),
        in_specs=[vmem()] * 3 + [anywhere] * len(outputs),
        out_specs=(anywhere, anywhere),
        scratch_shapes=[
            pltpu.VMEM((2, 2 * ROWS, LANES), F32),
            pltpu.VMEM((4, WIDTH, LANES), F32),
            pltpu.VMEM((2, 4, ROWS, LANES), BF16),
            pltpu.VMEM((2, 4, WIDTH, WIDTH), F32),
            pltpu.SemaphoreType.DMA((4,)),
            pltpu.SemaphoreType.DMA((4,)),
        ],
        input_output_aliases={3: 0, 4: 1} if outputs else {},
        compiler_params=PARAMS,
        cost_estimate=pl.CostEstimate(flops=3 * 10**8, bytes_accessed=2**22, transcendentals=0),
    )(factor, s, weights, *outputs)


def space_perm(along, shift):
    pairs = []
    for i in range(32):
        z, x, core = i // 8, i // 2 % 4, i % 2
        if along == "x":
            x = (x + shift) % 4
        elif along == "z":
            z = (z + shift) % 4
        else:
            core = 1 - core
        pairs.append((i, (z * 4 + x) * 2 + core))
    return pairs


def sum_over_chips(value):
    for along in ("x", "z"):
        far = [lax.ppermute(value, "space", space_perm(along, d)) for d in (3, 1, 2)]
        value = ((value + far[0]) + far[1]) + far[2]
    return value


def on_device(spectra, weights):
    t = lax.axis_index("tm")
    flat = spectra.reshape(2, 2, 4, ROWS, LANES)

    def piece(d):
        source = lax.optimization_barrier(flat)
        return lax.dynamic_index_in_dim(source, (t + d) % 4, 2, keepdims=False)

    near = {}
    for d in ORDER:
        near[d] = lax.ppermute(piece(d), "tm", [(i, (i + d) % 4) for i in range(4)])
    own = piece(0)
    other, s_far, send = run_send(own, [near[d] for d in ORDER], weights)
    across = space_perm("core", 1)
    arrived = lax.ppermute(send, "space", across)
    s_own, keep = run_keep(other)
    gram = sum_over_chips(keep + arrived)
    factor = run_factor(gram)
    far = lax.ppermute(factor, "space", across)
    outputs = run_modes(0, factor, s_own, weights)
    modes, upper = run_modes(1, far, s_far, weights, outputs)
    return (
        modes.reshape(2, SUBS, 1, WIDTH, FIELDS, LANES),
        upper.reshape(2, SUBS, 1, WIDTH, WIDTH),
    )


def solution(mesh):
    placed = (P(None, "tm", None, None, None, "space"), P(None, "space"))
    return jax.shard_map(
        on_device,
        mesh=mesh,
        in_specs=placed,
        out_specs=(P(None, None, "tm", None, None, "space"), P(None, None, "tm", None, None)),
        check_vma=False,
    )
```

time: 48.2 us -> 45.8 us (0.950)
  Pallas kernels: 9.38 us -> 8.27 us
  waiting for transfers between devices: 14.2 us -> 13.2 us
    pallas_call x2, Pallas kernels: 3.98 us -> 2.65 us  [run_modes(): pl.pallas_call(functools.partial(modes_kernel, slot), name='modes_far' if...]
    ppermute x1, waiting for transfers between devices: 0.9 us -> 0.01 us  [on_device(): arrived = lax.ppermute(send, 'space', across)]
    pallas_call x1 -> x2, Pallas kernels: 2.76 us -> 3.23 us  [the longest x1 2.01 us: run_send(): pl.pallas_call(send_kernel, name='send_gram', out_shape=(jax.ShapeDtypeSt...]
  transfers between devices with their start and end apart: 11 -> 11, of which waited for: 5 -> 4; matrix products, arithmetic and copies ran while one was open for 0% -> 0% of each run, Pallas kernels for 4% -> 6%
where the time goes in v4:
time: 45.8 us; the launch traced here: 45.7 us
  starting transfers between devices  22.1 us (48%)
  waiting for transfers between devices  13.2 us (29%)
  Pallas kernels  8.27 us (18%)
  local copies, waits for them, and re-layouts  1.3 us (3%)
  between operations  0.76 us (2%)
    ppermute x6, starting transfers between devices, sum_over_chips(): lax.ppermute(value, 'space', space_perm(along, d))  11.9 us
    ppermute x3, waiting for transfers between devices, on_device(): near[d] = lax.ppermute(piece(d), 'tm', [(i, (i + d) % 4) for i in range(4)])  9.71 us
    ppermute x3, starting transfers between devices, on_device(): near[d] = lax.ppermute(piece(d), 'tm', [(i, (i + d) % 4) for i in range(4)])  6.5 us
    ppermute x6, waiting for transfers between devices, sum_over_chips(): lax.ppermute(value, 'space', space_perm(along, d))  3.48 us
    ppermute x1, starting transfers between devices, on_device(): far = lax.ppermute(factor, 'space', across)  2.78 us
    pallas_call x2, Pallas kernels, run_modes(): pl.pallas_call(functools.partial(modes_kernel, slot), name='modes_far' if...  2.65 us
    pallas_call x1, Pallas kernels, run_factor(): pl.pallas_call(factor_kernel, name='factor', out_shape=jax.ShapeDtypeStru...  2.38 us
    pallas_call x1, Pallas kernels, run_send(): pl.pallas_call(send_kernel, name='send_gram', out_shape=(jax.ShapeDtypeSt...  2.01 us
  transfers between devices with their start and end apart: 11, of which 4 were waited for; matrix products, arithmetic and copies ran while one was open for 0% of the time, Pallas kernels for 6%

profile of v4, /device:TPU:1, one launch (start us, length us, event | category | flops | bytes accessed | tf_op | source)
XLA Modules:
  0.0 45.7 jit_solution(10918454455649191827)
XLA Ops:
  0.7 1.3 %dynamic-slice_bitcast_fusion = (bf16[2,2,256,128]{3,2,1,0:T(8,128)(2,1)S(1)}, bf16[2,2,256,128]{3,2,1,0:T(8,128)(2,1)S(1)}, bf16[2,2,256,128]{3,2,1,0:T(8,128)(2,1)S(1)}, bf16[2,2,256,128]{3,2,1,0:T(8,128)(2,1)S(1)}) fusion(bf16[2,2,4,256,128]{4,3,2,1,0:T(8,128)(2,1)} %bitcast.23, s32[]{:T(128)S(6)} %select_n.39, s32[]{:T(128)S(6)} %select_n.37, ...), kind=kLoop, calls=%fused_computation | loop fusion | bytes 2097168 | tf_op jit(solution)/shard_map/jit(dynamic_index_in_dim)/squeeze | solution.py:442
  2.0 3.8 %collective-permute-start.2 = (bf16[2,2,256,128]{3,2,1,0:T(8,128)(2,1)S(1)}, bf16[2,2,256,128]{3,2,1,0:T(8,128)(2,1)S(1)}, u32[]{:S(2)}, u32[]{:S(2)}) collective-permute-start(bf16[2,2,256,128]{3,2,1,0:T(8,128)(2,1)S(1)} %get-tuple-element.22), channel_id=1, source_target_pairs={{0,64},{32,96},{64,0},{96,32},{1,65},{33,97},{65,1},{97,33},{2,66}... | collective-permute-start | bytes 786440 | tf_op jit(solution)/shard_map/ppermute | solution.py:446
  5.8 0.0 copy-start
  5.8 0.4 collective-permute-start.1
  6.2 2.3 %collective-permute-start = (bf16[2,2,256,128]{3,2,1,0:T(8,128)(2,1)S(1)}, bf16[2,2,256,128]{3,2,1,0:T(8,128)(2,1)S(1)}, u32[]{:S(2)}, u32[]{:S(2)}) collective-permute-start(bf16[2,2,256,128]{3,2,1,0:T(8,128)(2,1)S(1)} %get-tuple-element.24), channel_id=1, source_target_pairs={{0,96},{32,0},{64,32},{96,64},{1,97},{33,1},{65,33},{97,65},{2,98}... | collective-permute-start | bytes 786440 | tf_op jit(solution)/shard_map/ppermute | solution.py:446
  8.5 3.1 %collective-permute-done.2.near2 = bf16[2,2,256,128]{3,2,1,0:T(8,128)(2,1)S(1)} collective-permute-done((bf16[2,2,256,128]{3,2,1,0:T(8,128)(2,1)S(1)}, bf16[2,2,256,128]{3,2,1,0:T(8,128)(2,1)S(1)}, u32[]{:S(2)}, u32[]{:S(2)}) %collective-permute-start.2) | collective-permute-done | bytes 262176 | tf_op jit(solution)/shard_map/ppermute | solution.py:446
  11.6 6.6 %collective-permute-done.1.near1 = bf16[2,2,256,128]{3,2,1,0:T(8,128)(2,1)S(1)} collective-permute-done((bf16[2,2,256,128]{3,2,1,0:T(8,128)(2,1)S(1)}, bf16[2,2,256,128]{3,2,1,0:T(8,128)(2,1)S(1)}, u32[]{:S(2)}, u32[]{:S(2)}) %collective-permute-start.1) | collective-permute-done | bytes 262176 | tf_op jit(solution)/shard_map/ppermute | solution.py:446
  18.2 0.0 collective-permute-done.near3
  18.2 0.0 copy-done
  18.2 2.0 %send_gram.1 = (f32[4,2,256,128]{3,2,1,0:T(8,128)S(1)}, bf16[4,256,512]{2,1,0:T(8,128)(2,1)S(1)}, f32[128,128]{1,0:T(8,128)S(1)}) custom-call(bf16[2,2,256,128]{3,2,1,0:T(8,128)(2,1)S(1)} %get-tuple-element.25.own, bf16[2,2,256,128]{3,2,1,0:T(8,128)(2,1)S(1)} %collective-permute-done.near3, bf16[2,2,256,128]{3,2,1,0:T(8,128)(2,1)S(1)} %collective-permute-done.1.near1, ...), custom_call_target="tpu_custom_call" | custom-call | tf_op jit(solution)/shard_map/send_gram/pallas_call | solution.py:340
  20.2 1.0 %collective-permute-start.3 = (f32[128,128]{1,0:T(8,128)S(1)}, f32[128,128]{1,0:T(8,128)S(1)}, u32[]{:S(2)}, u32[]{:S(2)}) collective-permute-start(f32[128,128]{1,0:T(8,128)S(1)} %get-tuple-element.13), channel_id=1, source_target_pairs={{0,1},{1,0},{2,3},{3,2},{4,5},{5,4},{6,7},{7,6},{8,9},{9,8},{10,11... | collective-permute-start | bytes 196616 | tf_op jit(solution)/shard_map/ppermute | solution.py:450
  21.2 1.2 %keep_gram.1 = (bf16[4,256,512]{2,1,0:T(8,128)(2,1)S(1)}, f32[128,128]{1,0:T(8,128)S(1)}) custom-call(f32[4,2,256,128]{3,2,1,0:T(8,128)S(1)} %get-tuple-element.11.work), custom_call_target="tpu_custom_call" | custom-call | flops 300000000 | bytes 2097152 | tf_op jit(solution)/shard_map/keep_gram/pallas_call | solution.py:360
  22.5 0.0 collective-permute-done.3
  22.5 2.8 %collective-permute-start.6 = (f32[128,128]{1,0:T(8,128)S(1)}, f32[128,128]{1,0:T(8,128)S(1)}, u32[]{:S(2)}, u32[]{:S(2)}) collective-permute-start(f32[128,128]{1,0:T(8,128)S(1)} %add.67), channel_id=1, source_target_pairs={{0,4},{1,5},{2,6},{3,7},{4,0},{5,1},{6,2},{7,3},{8,12},{9,13},{10,... | collective-permute-start | bytes 196616 | tf_op jit(solution)/shard_map/ppermute | solution.py:431
  25.3 0.3 collective-permute-start.5
  25.6 2.4 %collective-permute-start.4 = (f32[128,128]{1,0:T(8,128)S(1)}, f32[128,128]{1,0:T(8,128)S(1)}, u32[]{:S(2)}, u32[]{:S(2)}) collective-permute-start(f32[128,128]{1,0:T(8,128)S(1)} %add.67), channel_id=1, source_target_pairs={{0,6},{1,7},{2,0},{3,1},{4,2},{5,3},{6,4},{7,5},{8,14},{9,15},{10,... | collective-permute-start | bytes 196616 | tf_op jit(solution)/shard_map/ppermute | solution.py:431
  28.0 0.0 collective-permute-done.6
  28.0 1.6 %collective-permute-done.5 = f32[128,128]{1,0:T(8,128)S(1)} collective-permute-done((f32[128,128]{1,0:T(8,128)S(1)}, f32[128,128]{1,0:T(8,128)S(1)}, u32[]{:S(2)}, u32[]{:S(2)}) %collective-permute-start.5) | collective-permute-done | bytes 65568 | tf_op jit(solution)/shard_map/ppermute | solution.py:431
  29.6 0.0 collective-permute-done.4
  29.7 3.7 %collective-permute-start.9 = (f32[128,128]{1,0:T(8,128)S(1)}, f32[128,128]{1,0:T(8,128)S(1)}, u32[]{:S(2)}, u32[]{:S(2)}) collective-permute-start(f32[128,128]{1,0:T(8,128)S(1)} %add_add_fusion.1), channel_id=1, source_target_pairs={{0,16},{1,17},{2,18},{3,19},{4,20},{5,21},{6,22},{7,23},{8,24},{9,... | collective-permute-start | bytes 196616 | tf_op jit(solution)/shard_map/ppermute | solution.py:431
  33.3 0.7 %collective-permute-start.8 = (f32[128,128]{1,0:T(8,128)S(1)}, f32[128,128]{1,0:T(8,128)S(1)}, u32[]{:S(2)}, u32[]{:S(2)}) collective-permute-start(f32[128,128]{1,0:T(8,128)S(1)} %add_add_fusion.1), channel_id=1, source_target_pairs={{0,8},{1,9},{2,10},{3,11},{4,12},{5,13},{6,14},{7,15},{8,16},{9,17... | collective-permute-start | bytes 196616 | tf_op jit(solution)/shard_map/ppermute | solution.py:431
  34.1 1.9 %collective-permute-start.7 = (f32[128,128]{1,0:T(8,128)S(1)}, f32[128,128]{1,0:T(8,128)S(1)}, u32[]{:S(2)}, u32[]{:S(2)}) collective-permute-start(f32[128,128]{1,0:T(8,128)S(1)} %add_add_fusion.1), channel_id=1, source_target_pairs={{0,24},{1,25},{2,26},{3,27},{4,28},{5,29},{6,30},{7,31},{8,0},{9,1... | collective-permute-start | bytes 196616 | tf_op jit(solution)/shard_map/ppermute | solution.py:431
  36.0 0.0 collective-permute-done.9
  36.0 1.8 %collective-permute-done.8 = f32[128,128]{1,0:T(8,128)S(1)} collective-permute-done((f32[128,128]{1,0:T(8,128)S(1)}, f32[128,128]{1,0:T(8,128)S(1)}, u32[]{:S(2)}, u32[]{:S(2)}) %collective-permute-start.8) | collective-permute-done | bytes 65568 | tf_op jit(solution)/shard_map/ppermute | solution.py:431
  37.8 0.0 collective-permute-done.7
  37.9 2.4 %factor.1.refs_0_ = f32[4,64,128]{2,1,0:T(8,128)S(1)} custom-call(f32[128,128]{1,0:T(8,128)S(1)} %add_add_fusion.gram), custom_call_target="tpu_custom_call" | custom-call | tf_op jit(solution)/shard_map/factor/pallas_call | solution.py:379
  40.2 2.8 %collective-permute-start.10 = (f32[4,64,128]{2,1,0:T(8,128)S(1)}, f32[4,64,128]{2,1,0:T(8,128)S(1)}, u32[]{:S(2)}, u32[]{:S(2)}) collective-permute-start(f32[4,64,128]{2,1,0:T(8,128)S(1)} %factor.1.refs_0_), channel_id=1, source_target_pairs={{0,1},{1,0},{2,3},{3,2},{4,5},{5,4},{6,7},{7,6},{8,9},{9,8},{10,11... | collective-permute-start | bytes 393224 | tf_op jit(solution)/shard_map/ppermute | solution.py:454
  43.0 1.3 %modes_own.1 = (bf16[2,8,256,128]{3,2,1,0:T(8,128)(2,1)}, f32[2,8,64,64]{3,2,1,0:T(8,128)}) custom-call(f32[4,64,128]{2,1,0:T(8,128)S(1)} %factor.1.refs_0_, bf16[4,256,512]{2,1,0:T(8,128)(2,1)S(1)} %get-tuple-element.15.refs_1_, f32[4,128]{1,0:T(4,128)S(1)} %copy-done), custom_call_target="tpu_custom_call" | custom-call | flops 300000000 | bytes 4194304 | tf_op jit(solution)/shard_map/modes_own/pallas_call | solution.py:392
  44.3 0.0 collective-permute-done.10.refs_0_
  44.4 1.3 %modes_far.1 = (bf16[2,8,256,128]{3,2,1,0:T(8,128)(2,1)}, f32[2,8,64,64]{3,2,1,0:T(8,128)}) custom-call(f32[4,64,128]{2,1,0:T(8,128)S(1)} %collective-permute-done.10.refs_0_, bf16[4,256,512]{2,1,0:T(8,128)(2,1)S(1)} %get-tuple-element.14.refs_1_, f32[4,128]{1,0:T(4,128)S(1)} %copy-done, ...), custom_call_target="tpu_custom_call", output_to_operand_aliasing={{0}: (3, {}), {1}: (4, {})} | custom-call | flops 300000000 | bytes 4194304 | tf_op jit(solution)/shard_map/modes_far/pallas_call | solution.py:392
  (3 shorter events, 0.0 us)
Async XLA Ops:
  2.0 9.6 %collective-permute-start.2 = (bf16[2,2,256,128]{3,2,1,0:T(8,128)(2,1)S(1)}, bf16[2,2,256,128]{3,2,1,0:T(8,128)(2,1)S(1)}, u32[]{:S(2)}, u32[]{:S(2)}) collective-permute-start(bf16[2,2,256,128]{3,2,1,0:T(8,128)(2,1)S(1)} %get-tuple-element.22), channel_id=1, source_target_pairs={{0,64},{32,96},{64,0},{96,32},{1,65},{33,97},{65,1},{97,33},{2,66}... | collective-permute-start | bytes 786440 | tf_op jit(solution)/shard_map/ppermute | solution.py:446
  5.8 12.4 %copy-start = (f32[4,128]{1,0:T(4,128)S(1)}, f32[4,128]{1,0:T(4,128)}, u32[]{:S(2)}) copy-start(f32[4,128]{1,0:T(4,128)} %refs_2_.3) | copy-start | bytes 6148
  5.8 12.4 %collective-permute-start.1 = (bf16[2,2,256,128]{3,2,1,0:T(8,128)(2,1)S(1)}, bf16[2,2,256,128]{3,2,1,0:T(8,128)(2,1)S(1)}, u32[]{:S(2)}, u32[]{:S(2)}) collective-permute-start(bf16[2,2,256,128]{3,2,1,0:T(8,128)(2,1)S(1)} %get-tuple-element.23), channel_id=1, source_target_pairs={{0,32},{32,64},{64,96},{96,0},{1,33},{33,65},{65,97},{97,1},{2,34}... | collective-permute-start | bytes 786440 | tf_op jit(solution)/shard_map/ppermute | solution.py:446
  6.2 12.0 %collective-permute-start = (bf16[2,2,256,128]{3,2,1,0:T(8,128)(2,1)S(1)}, bf16[2,2,256,128]{3,2,1,0:T(8,128)(2,1)S(1)}, u32[]{:S(2)}, u32[]{:S(2)}) collective-permute-start(bf16[2,2,256,128]{3,2,1,0:T(8,128)(2,1)S(1)} %get-tuple-element.24), channel_id=1, source_target_pairs={{0,96},{32,0},{64,32},{96,64},{1,97},{33,1},{65,33},{97,65},{2,98}... | collective-permute-start | bytes 786440 | tf_op jit(solution)/shard_map/ppermute | solution.py:446
  20.2 2.2 %collective-permute-start.3 = (f32[128,128]{1,0:T(8,128)S(1)}, f32[128,128]{1,0:T(8,128)S(1)}, u32[]{:S(2)}, u32[]{:S(2)}) collective-permute-start(f32[128,128]{1,0:T(8,128)S(1)} %get-tuple-element.13), channel_id=1, source_target_pairs={{0,1},{1,0},{2,3},{3,2},{4,5},{5,4},{6,7},{7,6},{8,9},{9,8},{10,11... | collective-permute-start | bytes 196616 | tf_op jit(solution)/shard_map/ppermute | solution.py:450
  22.5 5.5 %collective-permute-start.6 = (f32[128,128]{1,0:T(8,128)S(1)}, f32[128,128]{1,0:T(8,128)S(1)}, u32[]{:S(2)}, u32[]{:S(2)}) collective-permute-start(f32[128,128]{1,0:T(8,128)S(1)} %add.67), channel_id=1, source_target_pairs={{0,4},{1,5},{2,6},{3,7},{4,0},{5,1},{6,2},{7,3},{8,12},{9,13},{10,... | collective-permute-start | bytes 196616 | tf_op jit(solution)/shard_map/ppermute | solution.py:431
  25.3 4.3 %collective-permute-start.5 = (f32[128,128]{1,0:T(8,128)S(1)}, f32[128,128]{1,0:T(8,128)S(1)}, u32[]{:S(2)}, u32[]{:S(2)}) collective-permute-start(f32[128,128]{1,0:T(8,128)S(1)} %add.67), channel_id=1, source_target_pairs={{0,2},{1,3},{2,4},{3,5},{4,6},{5,7},{6,0},{7,1},{8,10},{9,11},{10,... | collective-permute-start | bytes 196616 | tf_op jit(solution)/shard_map/ppermute | solution.py:431
  25.6 4.0 %collective-permute-start.4 = (f32[128,128]{1,0:T(8,128)S(1)}, f32[128,128]{1,0:T(8,128)S(1)}, u32[]{:S(2)}, u32[]{:S(2)}) collective-permute-start(f32[128,128]{1,0:T(8,128)S(1)} %add.67), channel_id=1, source_target_pairs={{0,6},{1,7},{2,0},{3,1},{4,2},{5,3},{6,4},{7,5},{8,14},{9,15},{10,... | collective-permute-start | bytes 196616 | tf_op jit(solution)/shard_map/ppermute | solution.py:431
  29.7 6.4 %collective-permute-start.9 = (f32[128,128]{1,0:T(8,128)S(1)}, f32[128,128]{1,0:T(8,128)S(1)}, u32[]{:S(2)}, u32[]{:S(2)}) collective-permute-start(f32[128,128]{1,0:T(8,128)S(1)} %add_add_fusion.1), channel_id=1, source_target_pairs={{0,16},{1,17},{2,18},{3,19},{4,20},{5,21},{6,22},{7,23},{8,24},{9,... | collective-permute-start | bytes 196616 | tf_op jit(solution)/shard_map/ppermute | solution.py:431
  33.3 4.5 %collective-permute-start.8 = (f32[128,128]{1,0:T(8,128)S(1)}, f32[128,128]{1,0:T(8,128)S(1)}, u32[]{:S(2)}, u32[]{:S(2)}) collective-permute-start(f32[128,128]{1,0:T(8,128)S(1)} %add_add_fusion.1), channel_id=1, source_target_pairs={{0,8},{1,9},{2,10},{3,11},{4,12},{5,13},{6,14},{7,15},{8,16},{9,17... | collective-permute-start | bytes 196616 | tf_op jit(solution)/shard_map/ppermute | solution.py:431
  34.1 3.8 %collective-permute-start.7 = (f32[128,128]{1,0:T(8,128)S(1)}, f32[128,128]{1,0:T(8,128)S(1)}, u32[]{:S(2)}, u32[]{:S(2)}) collective-permute-start(f32[128,128]{1,0:T(8,128)S(1)} %add_add_fusion.1), channel_id=1, source_target_pairs={{0,24},{1,25},{2,26},{3,27},{4,28},{5,29},{6,30},{7,31},{8,0},{9,1... | collective-permute-start | bytes 196616 | tf_op jit(solution)/shard_map/ppermute | solution.py:431
  40.2 4.1 %collective-permute-start.10 = (f32[4,64,128]{2,1,0:T(8,128)S(1)}, f32[4,64,128]{2,1,0:T(8,128)S(1)}, u32[]{:S(2)}, u32[]{:S(2)}) collective-permute-start(f32[4,64,128]{2,1,0:T(8,128)S(1)} %factor.1.refs_0_), channel_id=1, source_target_pairs={{0,1},{1,0},{2,3},{3,2},{4,5},{5,4},{6,7},{7,6},{8,9},{9,8},{10,11... | collective-permute-start | bytes 393224 | tf_op jit(solution)/shard_map/ppermute | solution.py:454

commit v5 on v4

--- a/solution.py
+++ b/solution.py
@@ -126,34 +126,58 @@
         out_ref[m * 8 : (m + 1) * 8, :] = jnp.where(upper, near, far)
 
 
-def send_kernel(own, near3, near1, near2, weight, other_ref, s_ref, send_ref, work, mixed, products):
+def twiddles(weight, shifts):
+    t = lax.axis_index("tm")
+    root = jnp.sqrt(jnp.concatenate([weight[...]] * 4, axis=0))
+    out = []
+    for d in shifts:
+        re, im = source_twiddle(t, d)
+        out.append((root * re, root * im))
+    return out
+
+
+def twisted(source, s, rows, tw):
+    re = source[0, s, rows, :].astype(F32)
+    im = source[1, s, rows, :].astype(F32)
+    return re * tw[0] - im * tw[1], re * tw[1] + im * tw[0]
+
+
+def even_kernel(own, near2, weight, even_ref):
+    tw = twiddles(weight, (0, 2))
+
+    def step(index, _):
+        rows = pl.ds(pl.multiple_of(index * 16, 16), 16)
+        for s in range(2):
+            y0 = twisted(own, s, rows, tw[0])
+            y2 = twisted(near2, s, rows, tw[1])
+            even_ref[s, 0, rows, :] = y0[0] + y2[0]
+            even_ref[s, 1, rows, :] = y0[1] + y2[1]
+            even_ref[s, 2, rows, :] = y0[0] - y2[0]
+            even_ref[s, 3, rows, :] = y0[1] - y2[1]
+        return 0
+
+    lax.fori_loop(0, ROWS // 16, step, 0)
+
+
+def send_kernel(near3, near1, weight, even, other_ref, s_ref, send_ref, work, mixed, products):
     t = lax.axis_index("tm")
     side = jnp.where(lax.axis_index("space") % 2 == 0, -1.0, 1.0).astype(F32)
-    root = jnp.sqrt(jnp.concatenate([weight[...]] * 4, axis=0))
-    sources = (own, near1, near2, near3)
-    tw = []
-    for d in range(4):
-        re, im = source_twiddle(t, d)
-        tw.append((root * re, root * im))
+    tw = twiddles(weight, (1, 3))
     tq = []
     for q in range(4):
         re, im = second_twiddle(t, q)
         tq.append((re * side, im * side))
 
-    def transform(step, _):
-        row = pl.multiple_of(step * 16, 16)
-        rows = pl.ds(row, 16)
+    def step(index, _):
+        rows = pl.ds(pl.multiple_of(index * 16, 16), 16)
         radix = []
         for s in range(2):
-            y = []
-            for d in range(4):
-                re = sources[d][0, s, rows, :].astype(F32)
-                im = sources[d][1, s, rows, :].astype(F32)
-                y.append((re * tw[d][0] - im * tw[d][1], re * tw[d][1] + im * tw[d][0]))
-            a = (y[0][0] + y[2][0], y[0][1] + y[2][1])
-            b = (y[0][0] - y[2][0], y[0][1] - y[2][1])
-            c = (y[1][0] + y[3][0], y[1][1] + y[3][1])
-            e = (y[1][0] - y[3][0], y[1][1] - y[3][1])
+            y1 = twisted(near1, s, rows, tw[0])
+            y3 = twisted(near3, s, rows, tw[1])
+            a = (even[s, 0, rows, :], even[s, 1, rows, :])
+            b = (even[s, 2, rows, :], even[s, 3, rows, :])
+            c = (y1[0] + y3[0], y1[1] + y3[1])
+            e = (y1[0] - y3[0], y1[1] - y3[1])
             radix.append(
                 [
                     (a[0] + c[0], a[1] + c[1]),
@@ -172,7 +196,7 @@
             other_ref[q, 1, rows, :] = x0[1] - v[1]
         return 0
 
-    lax.fori_loop(0, ROWS // 16, transform, 0)
+    lax.fori_loop(0, ROWS // 16, step, 0)
     pack_gram(work, s_ref, send_ref, mixed, products)
 
 
@@ -332,11 +356,22 @@
 
 
 HALF = (LANES, LANES)
-ORDER = (3, 1, 2)
 PARAMS = pltpu.CompilerParams(vmem_limit_bytes=32 * 1024 * 1024)
 
 
-def run_send(own, near, weights):
+def run_even(own, near2, weights):
+    return pl.pallas_call(
+        even_kernel,
+        name="even",
+        out_shape=jax.ShapeDtypeStruct((2, 4, ROWS, LANES), F32),
+        in_specs=[vmem()] * 3,
+        out_specs=vmem(),
+        compiler_params=PARAMS,
+        cost_estimate=pl.CostEstimate(flops=2**22, bytes_accessed=2**21, transcendentals=0),
+    )(own, near2, weights)
+
+
+def run_send(near3, near1, weights, even):
     return pl.pallas_call(
         send_kernel,
         name="send_gram",
@@ -345,7 +380,7 @@
             jax.ShapeDtypeStruct((4, 2 * LANES, FIELDS * LANES), BF16),
             jax.ShapeDtypeStruct(HALF, F32),
         ),
-        in_specs=[vmem()] * 5,
+        in_specs=[vmem()] * 4,
         out_specs=(vmem(),) * 3,
         scratch_shapes=[
             pltpu.VMEM((4, 2, ROWS, LANES), F32),
@@ -353,7 +388,7 @@
             pltpu.VMEM((4, 2 * LANES, LANES), F32),
         ],
         compiler_params=PARAMS,
-    )(own, *near, weights)
+    )(near3, near1, weights, even)
 
 
 def run_keep(work):
@@ -437,15 +472,22 @@
     t = lax.axis_index("tm")
     flat = spectra.reshape(2, 2, 4, ROWS, LANES)
 
-    def piece(d):
-        source = lax.optimization_barrier(flat)
+    def piece(d, source):
         return lax.dynamic_index_in_dim(source, (t + d) % 4, 2, keepdims=False)
 
+    def move(d, source):
+        return lax.ppermute(piece(d, source), "tm", [(i, (i + d) % 4) for i in range(4)])
+
     near = {}
-    for d in ORDER:
-        near[d] = lax.ppermute(piece(d), "tm", [(i, (i + d) % 4) for i in range(4)])
-    own = piece(0)
-    other, s_far, send = run_send(own, [near[d] for d in ORDER], weights)
+    first = piece(2, flat)
+    later, first = lax.optimization_barrier((flat, first))
+    near[2] = lax.ppermute(first, "tm", [(i, (i + 2) % 4) for i in range(4)])
+    for d in (3, 1):
+        near[d] = move(d, later)
+    last, near[2] = lax.optimization_barrier((flat, near[2]))
+    own = piece(0, last)
+    even = run_even(own, near[2], weights)
+    other, s_far, send = run_send(near[3], near[1], weights, even)
     across = space_perm("core", 1)
     arrived = lax.ppermute(send, "space", across)
     s_own, keep = run_keep(other)

time: 45.8 us -> 45.3 us (0.989)
  waiting for transfers between devices: 13.2 us -> 10.5 us
  local copies, waits for them, and re-layouts: 1.3 us -> 3.01 us
    ppermute x3, waiting for transfers between devices: 9.71 us -> 6.99 us  [the longest x2 5.05 us: move(): lax.ppermute(piece(d, source), 'tm', [(i, (i + d) % 4) for i in range(4)])]
    squeeze x1 -> x3, local copies, waits for them, and re-layouts: 1.3 us -> 3.01 us  [piece(): return lax.dynamic_index_in_dim(source, (t + d) % 4, 2, keepdims=False)]
  transfers between devices with their start and end apart: 11 -> 11, of which waited for: 4 -> 4; matrix products, arithmetic and copies ran while one was open for 0% -> 5% of each run, Pallas kernels for 6% -> 6%
where the time goes in v5:
time: 45.3 us; the launch traced here: 45.1 us
  starting transfers between devices  22.5 us (50%)
  waiting for transfers between devices  10.5 us (23%)
  Pallas kernels  8.31 us (18%)
  local copies, waits for them, and re-layouts  3.01 us (7%)
  between operations  0.74 us (2%)
    ppermute x6, starting transfers between devices, sum_over_chips(): lax.ppermute(value, 'space', space_perm(along, d))  11.9 us
    ppermute x2, waiting for transfers between devices, move(): lax.ppermute(piece(d, source), 'tm', [(i, (i + d) % 4) for i in range(4)])  5.05 us
    ppermute x1, starting transfers between devices, on_device(): near[2] = lax.ppermute(first, 'tm', [(i, (i + 2) % 4) for i in range(4)])  3.82 us
    ppermute x6, waiting for transfers between devices, sum_over_chips(): lax.ppermute(value, 'space', space_perm(along, d))  3.48 us
    squeeze x3, local copies, waits for them, and re-layouts, piece(): return lax.dynamic_index_in_dim(source, (t + d) % 4, 2, keepdims=False)  3.01 us
    ppermute x1, starting transfers between devices, on_device(): far = lax.ppermute(factor, 'space', across)  2.78 us
    ppermute x2, starting transfers between devices, move(): lax.ppermute(piece(d, source), 'tm', [(i, (i + d) % 4) for i in range(4)])  2.75 us
    pallas_call x2, Pallas kernels, run_modes(): pl.pallas_call(functools.partial(modes_kernel, slot), name='modes_far' if...  2.66 us
  transfers between devices with their start and end apart: 11, of which 4 were waited for; matrix products, arithmetic and copies ran while one was open for 5% of the time, Pallas kernels for 6%

profile of v5, /device:TPU:1, one launch (start us, length us, event | category | flops | bytes accessed | tf_op | source)
XLA Modules:
  0.0 45.1 jit_solution(9386054739145317435)
XLA Ops:
  0.6 1.0 %dynamic-slice_bitcast_fusion.3 = bf16[2,2,256,128]{3,2,1,0:T(8,128)(2,1)S(1)} fusion(bf16[2,2,4,256,128]{4,3,2,1,0:T(8,128)(2,1)} %bitcast.17, s32[]{:T(128)S(6)} %select_n.33), kind=kLoop, calls=%fused_computation.3 | loop fusion | bytes 524292 | tf_op jit(solution)/shard_map/jit(dynamic_index_in_dim)/squeeze | solution.py:476
  1.6 3.8 %collective-permute-start.2 = (bf16[2,2,256,128]{3,2,1,0:T(8,128)(2,1)S(1)}, bf16[2,2,256,128]{3,2,1,0:T(8,128)(2,1)S(1)}, u32[]{:S(2)}, u32[]{:S(2)}) collective-permute-start(bf16[2,2,256,128]{3,2,1,0:T(8,128)(2,1)S(1)} %dynamic-slice_bitcast_fusion.3), channel_id=1, source_target_pairs={{0,64},{32,96},{64,0},{96,32},{1,65},{33,97},{65,1},{97,33},{2,66}... | collective-permute-start | bytes 786440 | tf_op jit(solution)/shard_map/ppermute | solution.py:484
  5.5 1.1 %dynamic-slice_bitcast_fusion.1 = (bf16[2,2,256,128]{3,2,1,0:T(8,128)(2,1)S(1)}, bf16[2,2,256,128]{3,2,1,0:T(8,128)(2,1)S(1)}) fusion(s32[]{:T(128)S(6)} %select_n.37, s32[]{:T(128)S(6)} %select_n.35, bf16[2,2,4,256,128]{4,3,2,1,0:T(8,128)(2,1)} %bitcast.18), kind=kLoop, calls=%fused_computation.1 | loop fusion | bytes 1048584 | tf_op jit(solution)/shard_map/jit(dynamic_index_in_dim)/squeeze | solution.py:476
  6.5 0.5 %collective-permute-start.1 = (bf16[2,2,256,128]{3,2,1,0:T(8,128)(2,1)S(1)}, bf16[2,2,256,128]{3,2,1,0:T(8,128)(2,1)S(1)}, u32[]{:S(2)}, u32[]{:S(2)}) collective-permute-start(bf16[2,2,256,128]{3,2,1,0:T(8,128)(2,1)S(1)} %get-tuple-element.30), channel_id=1, source_target_pairs={{0,32},{32,64},{64,96},{96,0},{1,33},{33,65},{65,97},{97,1},{2,34}... | collective-permute-start | bytes 786440 | tf_op jit(solution)/shard_map/ppermute | solution.py:479
  7.0 2.3 %collective-permute-start = (bf16[2,2,256,128]{3,2,1,0:T(8,128)(2,1)S(1)}, bf16[2,2,256,128]{3,2,1,0:T(8,128)(2,1)S(1)}, u32[]{:S(2)}, u32[]{:S(2)}) collective-permute-start(bf16[2,2,256,128]{3,2,1,0:T(8,128)(2,1)S(1)} %get-tuple-element.31), channel_id=1, source_target_pairs={{0,96},{32,0},{64,32},{96,64},{1,97},{33,1},{65,33},{97,65},{2,98}... | collective-permute-start | bytes 786440 | tf_op jit(solution)/shard_map/ppermute | solution.py:479
  9.3 0.0 copy-start
  9.3 1.9 %collective-permute-done.2.near2 = bf16[2,2,256,128]{3,2,1,0:T(8,128)(2,1)S(1)} collective-permute-done((bf16[2,2,256,128]{3,2,1,0:T(8,128)(2,1)S(1)}, bf16[2,2,256,128]{3,2,1,0:T(8,128)(2,1)S(1)}, u32[]{:S(2)}, u32[]{:S(2)}) %collective-permute-start.2) | collective-permute-done | bytes 262176 | tf_op jit(solution)/shard_map/ppermute | solution.py:484
  11.2 1.0 %dynamic-slice_bitcast_fusion.own = bf16[2,2,256,128]{3,2,1,0:T(8,128)(2,1)S(1)} fusion(s32[]{:T(128)S(6)} %select_n.39, bf16[2,2,4,256,128]{4,3,2,1,0:T(8,128)(2,1)} %bitcast.19), kind=kLoop, calls=%fused_computation | loop fusion | bytes 524292 | tf_op jit(solution)/shard_map/jit(dynamic_index_in_dim)/squeeze | solution.py:476
  12.2 0.0 copy-done
  12.2 0.3 even.1
  12.5 5.1 %collective-permute-done.1.near1 = bf16[2,2,256,128]{3,2,1,0:T(8,128)(2,1)S(1)} collective-permute-done((bf16[2,2,256,128]{3,2,1,0:T(8,128)(2,1)S(1)}, bf16[2,2,256,128]{3,2,1,0:T(8,128)(2,1)S(1)}, u32[]{:S(2)}, u32[]{:S(2)}) %collective-permute-start.1) | collective-permute-done | bytes 262176 | tf_op jit(solution)/shard_map/ppermute | solution.py:479
  17.5 0.0 collective-permute-done.near3
  17.5 1.8 %send_gram.1 = (f32[4,2,256,128]{3,2,1,0:T(8,128)S(1)}, bf16[4,256,512]{2,1,0:T(8,128)(2,1)S(1)}, f32[128,128]{1,0:T(8,128)S(1)}) custom-call(bf16[2,2,256,128]{3,2,1,0:T(8,128)(2,1)S(1)} %collective-permute-done.near3, bf16[2,2,256,128]{3,2,1,0:T(8,128)(2,1)S(1)} %collective-permute-done.1.near1, f32[4,128]{1,0:T(4,128)S(1)} %copy-done, ...), custom_call_target="tpu_custom_call" | custom-call | tf_op jit(solution)/shard_map/send_gram/pallas_call | solution.py:375
  19.3 1.3 %collective-permute-start.3 = (f32[128,128]{1,0:T(8,128)S(1)}, f32[128,128]{1,0:T(8,128)S(1)}, u32[]{:S(2)}, u32[]{:S(2)}) collective-permute-start(f32[128,128]{1,0:T(8,128)S(1)} %get-tuple-element.21), channel_id=1, source_target_pairs={{0,1},{1,0},{2,3},{3,2},{4,5},{5,4},{6,7},{7,6},{8,9},{9,8},{10,11... | collective-permute-start | bytes 196616 | tf_op jit(solution)/shard_map/ppermute | solution.py:492
  20.6 1.2 %keep_gram.1 = (bf16[4,256,512]{2,1,0:T(8,128)(2,1)S(1)}, f32[128,128]{1,0:T(8,128)S(1)}) custom-call(f32[4,2,256,128]{3,2,1,0:T(8,128)S(1)} %get-tuple-element.19.work), custom_call_target="tpu_custom_call" | custom-call | flops 300000000 | bytes 2097152 | tf_op jit(solution)/shard_map/keep_gram/pallas_call | solution.py:395
  21.8 0.0 collective-permute-done.3
  21.8 2.8 %collective-permute-start.6 = (f32[128,128]{1,0:T(8,128)S(1)}, f32[128,128]{1,0:T(8,128)S(1)}, u32[]{:S(2)}, u32[]{:S(2)}) collective-permute-start(f32[128,128]{1,0:T(8,128)S(1)} %add.67), channel_id=1, source_target_pairs={{0,4},{1,5},{2,6},{3,7},{4,0},{5,1},{6,2},{7,3},{8,12},{9,13},{10,... | collective-permute-start | bytes 196616 | tf_op jit(solution)/shard_map/ppermute | solution.py:466
  24.7 0.3 collective-permute-start.5
  25.0 2.4 %collective-permute-start.4 = (f32[128,128]{1,0:T(8,128)S(1)}, f32[128,128]{1,0:T(8,128)S(1)}, u32[]{:S(2)}, u32[]{:S(2)}) collective-permute-start(f32[128,128]{1,0:T(8,128)S(1)} %add.67), channel_id=1, source_target_pairs={{0,6},{1,7},{2,0},{3,1},{4,2},{5,3},{6,4},{7,5},{8,14},{9,15},{10,... | collective-permute-start | bytes 196616 | tf_op jit(solution)/shard_map/ppermute | solution.py:466
  27.3 0.0 collective-permute-done.6
  27.3 1.6 %collective-permute-done.5 = f32[128,128]{1,0:T(8,128)S(1)} collective-permute-done((f32[128,128]{1,0:T(8,128)S(1)}, f32[128,128]{1,0:T(8,128)S(1)}, u32[]{:S(2)}, u32[]{:S(2)}) %collective-permute-start.5) | collective-permute-done | bytes 65568 | tf_op jit(solution)/shard_map/ppermute | solution.py:466
  29.0 0.0 collective-permute-done.4
  29.0 3.7 %collective-permute-start.9 = (f32[128,128]{1,0:T(8,128)S(1)}, f32[128,128]{1,0:T(8,128)S(1)}, u32[]{:S(2)}, u32[]{:S(2)}) collective-permute-start(f32[128,128]{1,0:T(8,128)S(1)} %add_add_fusion.1), channel_id=1, source_target_pairs={{0,16},{1,17},{2,18},{3,19},{4,20},{5,21},{6,22},{7,23},{8,24},{9,... | collective-permute-start | bytes 196616 | tf_op jit(solution)/shard_map/ppermute | solution.py:466
  32.7 0.7 %collective-permute-start.8 = (f32[128,128]{1,0:T(8,128)S(1)}, f32[128,128]{1,0:T(8,128)S(1)}, u32[]{:S(2)}, u32[]{:S(2)}) collective-permute-start(f32[128,128]{1,0:T(8,128)S(1)} %add_add_fusion.1), channel_id=1, source_target_pairs={{0,8},{1,9},{2,10},{3,11},{4,12},{5,13},{6,14},{7,15},{8,16},{9,17... | collective-permute-start | bytes 196616 | tf_op jit(solution)/shard_map/ppermute | solution.py:466
  33.4 1.9 %collective-permute-start.7 = (f32[128,128]{1,0:T(8,128)S(1)}, f32[128,128]{1,0:T(8,128)S(1)}, u32[]{:S(2)}, u32[]{:S(2)}) collective-permute-start(f32[128,128]{1,0:T(8,128)S(1)} %add_add_fusion.1), channel_id=1, source_target_pairs={{0,24},{1,25},{2,26},{3,27},{4,28},{5,29},{6,30},{7,31},{8,0},{9,1... | collective-permute-start | bytes 196616 | tf_op jit(solution)/shard_map/ppermute | solution.py:466
  35.4 0.0 collective-permute-done.9
  35.4 1.8 %collective-permute-done.8 = f32[128,128]{1,0:T(8,128)S(1)} collective-permute-done((f32[128,128]{1,0:T(8,128)S(1)}, f32[128,128]{1,0:T(8,128)S(1)}, u32[]{:S(2)}, u32[]{:S(2)}) %collective-permute-start.8) | collective-permute-done | bytes 65568 | tf_op jit(solution)/shard_map/ppermute | solution.py:466
  37.2 0.0 collective-permute-done.7
  37.2 2.4 %factor.1.refs_0_ = f32[4,64,128]{2,1,0:T(8,128)S(1)} custom-call(f32[128,128]{1,0:T(8,128)S(1)} %add_add_fusion.gram), custom_call_target="tpu_custom_call" | custom-call | tf_op jit(solution)/shard_map/factor/pallas_call | solution.py:414
  39.6 2.8 %collective-permute-start.10 = (f32[4,64,128]{2,1,0:T(8,128)S(1)}, f32[4,64,128]{2,1,0:T(8,128)S(1)}, u32[]{:S(2)}, u32[]{:S(2)}) collective-permute-start(f32[4,64,128]{2,1,0:T(8,128)S(1)} %factor.1.refs_0_), channel_id=1, source_target_pairs={{0,1},{1,0},{2,3},{3,2},{4,5},{5,4},{6,7},{7,6},{8,9},{9,8},{10,11... | collective-permute-start | bytes 393224 | tf_op jit(solution)/shard_map/ppermute | solution.py:496
  42.4 1.3 %modes_own.1 = (bf16[2,8,256,128]{3,2,1,0:T(8,128)(2,1)}, f32[2,8,64,64]{3,2,1,0:T(8,128)}) custom-call(f32[4,64,128]{2,1,0:T(8,128)S(1)} %factor.1.refs_0_, bf16[4,256,512]{2,1,0:T(8,128)(2,1)S(1)} %get-tuple-element.23.refs_1_, f32[4,128]{1,0:T(4,128)S(1)} %copy-done), custom_call_target="tpu_custom_call" | custom-call | flops 300000000 | bytes 4194304 | tf_op jit(solution)/shard_map/modes_own/pallas_call | solution.py:427
  43.7 0.0 collective-permute-done.10.refs_0_
  43.7 1.3 %modes_far.1 = (bf16[2,8,256,128]{3,2,1,0:T(8,128)(2,1)}, f32[2,8,64,64]{3,2,1,0:T(8,128)}) custom-call(f32[4,64,128]{2,1,0:T(8,128)S(1)} %collective-permute-done.10.refs_0_, bf16[4,256,512]{2,1,0:T(8,128)(2,1)S(1)} %get-tuple-element.22.refs_1_, f32[4,128]{1,0:T(4,128)S(1)} %copy-done, ...), custom_call_target="tpu_custom_call", output_to_operand_aliasing={{0}: (3, {}), {1}: (4, {})} | custom-call | flops 300000000 | bytes 4194304 | tf_op jit(solution)/shard_map/modes_far/pallas_call | solution.py:427
  (3 shorter events, 0.0 us)
Async XLA Ops:
  1.6 9.6 %collective-permute-start.2 = (bf16[2,2,256,128]{3,2,1,0:T(8,128)(2,1)S(1)}, bf16[2,2,256,128]{3,2,1,0:T(8,128)(2,1)S(1)}, u32[]{:S(2)}, u32[]{:S(2)}) collective-permute-start(bf16[2,2,256,128]{3,2,1,0:T(8,128)(2,1)S(1)} %dynamic-slice_bitcast_fusion.3), channel_id=1, source_target_pairs={{0,64},{32,96},{64,0},{96,32},{1,65},{33,97},{65,1},{97,33},{2,66}... | collective-permute-start | bytes 786440 | tf_op jit(solution)/shard_map/ppermute | solution.py:484
  6.5 11.0 %collective-permute-start.1 = (bf16[2,2,256,128]{3,2,1,0:T(8,128)(2,1)S(1)}, bf16[2,2,256,128]{3,2,1,0:T(8,128)(2,1)S(1)}, u32[]{:S(2)}, u32[]{:S(2)}) collective-permute-start(bf16[2,2,256,128]{3,2,1,0:T(8,128)(2,1)S(1)} %get-tuple-element.30), channel_id=1, source_target_pairs={{0,32},{32,64},{64,96},{96,0},{1,33},{33,65},{65,97},{97,1},{2,34}... | collective-permute-start | bytes 786440 | tf_op jit(solution)/shard_map/ppermute | solution.py:479
  7.0 10.5 %collective-permute-start = (bf16[2,2,256,128]{3,2,1,0:T(8,128)(2,1)S(1)}, bf16[2,2,256,128]{3,2,1,0:T(8,128)(2,1)S(1)}, u32[]{:S(2)}, u32[]{:S(2)}) collective-permute-start(bf16[2,2,256,128]{3,2,1,0:T(8,128)(2,1)S(1)} %get-tuple-element.31), channel_id=1, source_target_pairs={{0,96},{32,0},{64,32},{96,64},{1,97},{33,1},{65,33},{97,65},{2,98}... | collective-permute-start | bytes 786440 | tf_op jit(solution)/shard_map/ppermute | solution.py:479
  9.3 2.9 %copy-start = (f32[4,128]{1,0:T(4,128)S(1)}, f32[4,128]{1,0:T(4,128)}, u32[]{:S(2)}) copy-start(f32[4,128]{1,0:T(4,128)} %refs_2_.3) | copy-start | bytes 6148
  19.3 2.5 %collective-permute-start.3 = (f32[128,128]{1,0:T(8,128)S(1)}, f32[128,128]{1,0:T(8,128)S(1)}, u32[]{:S(2)}, u32[]{:S(2)}) collective-permute-start(f32[128,128]{1,0:T(8,128)S(1)} %get-tuple-element.21), channel_id=1, source_target_pairs={{0,1},{1,0},{2,3},{3,2},{4,5},{5,4},{6,7},{7,6},{8,9},{9,8},{10,11... | collective-permute-start | bytes 196616 | tf_op jit(solution)/shard_map/ppermute | solution.py:492
  21.8 5.5 %collective-permute-start.6 = (f32[128,128]{1,0:T(8,128)S(1)}, f32[128,128]{1,0:T(8,128)S(1)}, u32[]{:S(2)}, u32[]{:S(2)}) collective-permute-start(f32[128,128]{1,0:T(8,128)S(1)} %add.67), channel_id=1, source_target_pairs={{0,4},{1,5},{2,6},{3,7},{4,0},{5,1},{6,2},{7,3},{8,12},{9,13},{10,... | collective-permute-start | bytes 196616 | tf_op jit(solution)/shard_map/ppermute | solution.py:466
  24.7 4.3 %collective-permute-start.5 = (f32[128,128]{1,0:T(8,128)S(1)}, f32[128,128]{1,0:T(8,128)S(1)}, u32[]{:S(2)}, u32[]{:S(2)}) collective-permute-start(f32[128,128]{1,0:T(8,128)S(1)} %add.67), channel_id=1, source_target_pairs={{0,2},{1,3},{2,4},{3,5},{4,6},{5,7},{6,0},{7,1},{8,10},{9,11},{10,... | collective-permute-start | bytes 196616 | tf_op jit(solution)/shard_map/ppermute | solution.py:466
  25.0 4.0 %collective-permute-start.4 = (f32[128,128]{1,0:T(8,128)S(1)}, f32[128,128]{1,0:T(8,128)S(1)}, u32[]{:S(2)}, u32[]{:S(2)}) collective-permute-start(f32[128,128]{1,0:T(8,128)S(1)} %add.67), channel_id=1, source_target_pairs={{0,6},{1,7},{2,0},{3,1},{4,2},{5,3},{6,4},{7,5},{8,14},{9,15},{10,... | collective-permute-start | bytes 196616 | tf_op jit(solution)/shard_map/ppermute | solution.py:466
  29.0 6.4 %collective-permute-start.9 = (f32[128,128]{1,0:T(8,128)S(1)}, f32[128,128]{1,0:T(8,128)S(1)}, u32[]{:S(2)}, u32[]{:S(2)}) collective-permute-start(f32[128,128]{1,0:T(8,128)S(1)} %add_add_fusion.1), channel_id=1, source_target_pairs={{0,16},{1,17},{2,18},{3,19},{4,20},{5,21},{6,22},{7,23},{8,24},{9,... | collective-permute-start | bytes 196616 | tf_op jit(solution)/shard_map/ppermute | solution.py:466
  32.7 4.5 %collective-permute-start.8 = (f32[128,128]{1,0:T(8,128)S(1)}, f32[128,128]{1,0:T(8,128)S(1)}, u32[]{:S(2)}, u32[]{:S(2)}) collective-permute-start(f32[128,128]{1,0:T(8,128)S(1)} %add_add_fusion.1), channel_id=1, source_target_pairs={{0,8},{1,9},{2,10},{3,11},{4,12},{5,13},{6,14},{7,15},{8,16},{9,17... | collective-permute-start | bytes 196616 | tf_op jit(solution)/shard_map/ppermute | solution.py:466
  33.4 3.8 %collective-permute-start.7 = (f32[128,128]{1,0:T(8,128)S(1)}, f32[128,128]{1,0:T(8,128)S(1)}, u32[]{:S(2)}, u32[]{:S(2)}) collective-permute-start(f32[128,128]{1,0:T(8,128)S(1)} %add_add_fusion.1), channel_id=1, source_target_pairs={{0,24},{1,25},{2,26},{3,27},{4,28},{5,29},{6,30},{7,31},{8,0},{9,1... | collective-permute-start | bytes 196616 | tf_op jit(solution)/shard_map/ppermute | solution.py:466
  39.6 4.1 %collective-permute-start.10 = (f32[4,64,128]{2,1,0:T(8,128)S(1)}, f32[4,64,128]{2,1,0:T(8,128)S(1)}, u32[]{:S(2)}, u32[]{:S(2)}) collective-permute-start(f32[4,64,128]{2,1,0:T(8,128)S(1)} %factor.1.refs_0_), channel_id=1, source_target_pairs={{0,1},{1,0},{2,3},{3,2},{4,5},{5,4},{6,7},{7,6},{8,9},{9,8},{10,11... | collective-permute-start | bytes 393224 | tf_op jit(solution)/shard_map/ppermute | solution.py:496

commit v6 on v5

--- a/solution.py
+++ b/solution.py
@@ -156,7 +156,7 @@
             even_ref[s, 3, rows, :] = y0[1] - y2[1]
         return 0
 
-    lax.fori_loop(0, ROWS // 16, step, 0)
+    lax.fori_loop(0, ROWS // 16, step, 0, unroll=4)
 
 
 def send_kernel(near3, near1, weight, even, other_ref, s_ref, send_ref, work, mixed, products):
@@ -196,7 +196,7 @@
             other_ref[q, 1, rows, :] = x0[1] - v[1]
         return 0
 
-    lax.fori_loop(0, ROWS // 16, step, 0)
+    lax.fori_loop(0, ROWS // 16, step, 0, unroll=4)
     pack_gram(work, s_ref, send_ref, mixed, products)
 
 
@@ -447,23 +447,23 @@
     )(factor, s, weights, *outputs)
 
 
-def space_perm(along, shift):
+def space_perm(first, shift):
     pairs = []
     for i in range(32):
         z, x, core = i // 8, i // 2 % 4, i % 2
-        if along == "x":
+        if shift == 0:
+            core = 1 - core
+        elif first == (core == 0):
             x = (x + shift) % 4
-        elif along == "z":
+        else:
             z = (z + shift) % 4
-        else:
-            core = 1 - core
         pairs.append((i, (z * 4 + x) * 2 + core))
     return pairs
 
 
 def sum_over_chips(value):
-    for along in ("x", "z"):
-        far = [lax.ppermute(value, "space", space_perm(along, d)) for d in (3, 1, 2)]
+    for first in (True, False):
+        far = [lax.ppermute(value, "space", space_perm(first, d)) for d in (3, 1, 2)]
         value = ((value + far[0]) + far[1]) + far[2]
     return value
 
@@ -488,7 +488,7 @@
     own = piece(0, last)
     even = run_even(own, near[2], weights)
     other, s_far, send = run_send(near[3], near[1], weights, even)
-    across = space_perm("core", 1)
+    across = space_perm(True, 0)
     arrived = lax.ppermute(send, "space", across)
     s_own, keep = run_keep(other)
     gram = sum_over_chips(keep + arrived)

time: 45.3 us -> 45.2 us (level)
  no operation moved by 1% of the time
where the time goes in v6:
time: 45.2 us; the launch traced here: 45 us
  starting transfers between devices  22.5 us (50%)
  waiting for transfers between devices  10.6 us (23%)
  Pallas kernels  8.17 us (18%)
  local copies, waits for them, and re-layouts  3.01 us (7%)
  between operations  0.74 us (2%)
    ppermute x6, starting transfers between devices, sum_over_chips(): lax.ppermute(value, 'space', space_perm(first, d))  11.7 us
    ppermute x2, waiting for transfers between devices, move(): lax.ppermute(piece(d, source), 'tm', [(i, (i + d) % 4) for i in range(4)])  5.12 us
    ppermute x1, starting transfers between devices, on_device(): near[2] = lax.ppermute(first, 'tm', [(i, (i + 2) % 4) for i in range(4)])  3.82 us
    ppermute x6, waiting for transfers between devices, sum_over_chips(): lax.ppermute(value, 'space', space_perm(first, d))  3.5 us
    squeeze x3, local copies, waits for them, and re-layouts, piece(): return lax.dynamic_index_in_dim(source, (t + d) % 4, 2, keepdims=False)  3.01 us
    ppermute x1, starting transfers between devices, on_device(): far = lax.ppermute(factor, 'space', across)  2.95 us
    ppermute x2, starting transfers between devices, move(): lax.ppermute(piece(d, source), 'tm', [(i, (i + d) % 4) for i in range(4)])  2.75 us
    pallas_call x2, Pallas kernels, run_modes(): pl.pallas_call(functools.partial(modes_kernel, slot), name='modes_far' if...  2.66 us
  transfers between devices with their start and end apart: 11, of which 4 were waited for; matrix products, arithmetic and copies ran while one was open for 5% of the time, Pallas kernels for 6%

profile of v6, /device:TPU:1, one launch (start us, length us, event | category | flops | bytes accessed | tf_op | source)
XLA Modules:
  0.0 45.0 jit_solution(14422999470866629536)
XLA Ops:
  0.6 1.0 %dynamic-slice_bitcast_fusion.3 = bf16[2,2,256,128]{3,2,1,0:T(8,128)(2,1)S(1)} fusion(bf16[2,2,4,256,128]{4,3,2,1,0:T(8,128)(2,1)} %bitcast.17, s32[]{:T(128)S(6)} %select_n.33), kind=kLoop, calls=%fused_computation.3 | loop fusion | bytes 524292 | tf_op jit(solution)/shard_map/jit(dynamic_index_in_dim)/squeeze | solution.py:476
  1.6 3.8 %collective-permute-start.2 = (bf16[2,2,256,128]{3,2,1,0:T(8,128)(2,1)S(1)}, bf16[2,2,256,128]{3,2,1,0:T(8,128)(2,1)S(1)}, u32[]{:S(2)}, u32[]{:S(2)}) collective-permute-start(bf16[2,2,256,128]{3,2,1,0:T(8,128)(2,1)S(1)} %dynamic-slice_bitcast_fusion.3), channel_id=1, source_target_pairs={{0,64},{32,96},{64,0},{96,32},{1,65},{33,97},{65,1},{97,33},{2,66}... | collective-permute-start | bytes 786440 | tf_op jit(solution)/shard_map/ppermute | solution.py:484
  5.5 1.1 %dynamic-slice_bitcast_fusion.1 = (bf16[2,2,256,128]{3,2,1,0:T(8,128)(2,1)S(1)}, bf16[2,2,256,128]{3,2,1,0:T(8,128)(2,1)S(1)}) fusion(s32[]{:T(128)S(6)} %select_n.37, s32[]{:T(128)S(6)} %select_n.35, bf16[2,2,4,256,128]{4,3,2,1,0:T(8,128)(2,1)} %bitcast.18), kind=kLoop, calls=%fused_computation.1 | loop fusion | bytes 1048584 | tf_op jit(solution)/shard_map/jit(dynamic_index_in_dim)/squeeze | solution.py:476
  6.5 0.5 %collective-permute-start.1 = (bf16[2,2,256,128]{3,2,1,0:T(8,128)(2,1)S(1)}, bf16[2,2,256,128]{3,2,1,0:T(8,128)(2,1)S(1)}, u32[]{:S(2)}, u32[]{:S(2)}) collective-permute-start(bf16[2,2,256,128]{3,2,1,0:T(8,128)(2,1)S(1)} %get-tuple-element.30), channel_id=1, source_target_pairs={{0,32},{32,64},{64,96},{96,0},{1,33},{33,65},{65,97},{97,1},{2,34}... | collective-permute-start | bytes 786440 | tf_op jit(solution)/shard_map/ppermute | solution.py:479
  7.0 2.3 %collective-permute-start = (bf16[2,2,256,128]{3,2,1,0:T(8,128)(2,1)S(1)}, bf16[2,2,256,128]{3,2,1,0:T(8,128)(2,1)S(1)}, u32[]{:S(2)}, u32[]{:S(2)}) collective-permute-start(bf16[2,2,256,128]{3,2,1,0:T(8,128)(2,1)S(1)} %get-tuple-element.31), channel_id=1, source_target_pairs={{0,96},{32,0},{64,32},{96,64},{1,97},{33,1},{65,33},{97,65},{2,98}... | collective-permute-start | bytes 786440 | tf_op jit(solution)/shard_map/ppermute | solution.py:479
  9.3 0.0 copy-start
  9.3 1.9 %collective-permute-done.2.near2 = bf16[2,2,256,128]{3,2,1,0:T(8,128)(2,1)S(1)} collective-permute-done((bf16[2,2,256,128]{3,2,1,0:T(8,128)(2,1)S(1)}, bf16[2,2,256,128]{3,2,1,0:T(8,128)(2,1)S(1)}, u32[]{:S(2)}, u32[]{:S(2)}) %collective-permute-start.2) | collective-permute-done | bytes 262176 | tf_op jit(solution)/shard_map/ppermute | solution.py:484
  11.2 1.0 %dynamic-slice_bitcast_fusion.own = bf16[2,2,256,128]{3,2,1,0:T(8,128)(2,1)S(1)} fusion(s32[]{:T(128)S(6)} %select_n.39, bf16[2,2,4,256,128]{4,3,2,1,0:T(8,128)(2,1)} %bitcast.19), kind=kLoop, calls=%fused_computation | loop fusion | bytes 524292 | tf_op jit(solution)/shard_map/jit(dynamic_index_in_dim)/squeeze | solution.py:476
  12.2 0.0 copy-done
  12.2 0.2 even.1
  12.4 5.1 %collective-permute-done.1.near1 = bf16[2,2,256,128]{3,2,1,0:T(8,128)(2,1)S(1)} collective-permute-done((bf16[2,2,256,128]{3,2,1,0:T(8,128)(2,1)S(1)}, bf16[2,2,256,128]{3,2,1,0:T(8,128)(2,1)S(1)}, u32[]{:S(2)}, u32[]{:S(2)}) %collective-permute-start.1) | collective-permute-done | bytes 262176 | tf_op jit(solution)/shard_map/ppermute | solution.py:479
  17.5 0.0 collective-permute-done.near3
  17.5 1.7 %send_gram.1 = (f32[4,2,256,128]{3,2,1,0:T(8,128)S(1)}, bf16[4,256,512]{2,1,0:T(8,128)(2,1)S(1)}, f32[128,128]{1,0:T(8,128)S(1)}) custom-call(bf16[2,2,256,128]{3,2,1,0:T(8,128)(2,1)S(1)} %collective-permute-done.near3, bf16[2,2,256,128]{3,2,1,0:T(8,128)(2,1)S(1)} %collective-permute-done.1.near1, f32[4,128]{1,0:T(4,128)S(1)} %copy-done, ...), custom_call_target="tpu_custom_call" | custom-call | tf_op jit(solution)/shard_map/send_gram/pallas_call | solution.py:375
  19.2 1.3 %collective-permute-start.3 = (f32[128,128]{1,0:T(8,128)S(1)}, f32[128,128]{1,0:T(8,128)S(1)}, u32[]{:S(2)}, u32[]{:S(2)}) collective-permute-start(f32[128,128]{1,0:T(8,128)S(1)} %get-tuple-element.21), channel_id=1, source_target_pairs={{0,1},{1,0},{2,3},{3,2},{4,5},{5,4},{6,7},{7,6},{8,9},{9,8},{10,11... | collective-permute-start | bytes 196616 | tf_op jit(solution)/shard_map/ppermute | solution.py:492
  20.5 1.2 %keep_gram.1 = (bf16[4,256,512]{2,1,0:T(8,128)(2,1)S(1)}, f32[128,128]{1,0:T(8,128)S(1)}) custom-call(f32[4,2,256,128]{3,2,1,0:T(8,128)S(1)} %get-tuple-element.19.work), custom_call_target="tpu_custom_call" | custom-call | flops 300000000 | bytes 2097152 | tf_op jit(solution)/shard_map/keep_gram/pallas_call | solution.py:395
  21.7 0.0 collective-permute-done.3
  21.8 3.7 %collective-permute-start.6 = (f32[128,128]{1,0:T(8,128)S(1)}, f32[128,128]{1,0:T(8,128)S(1)}, u32[]{:S(2)}, u32[]{:S(2)}) collective-permute-start(f32[128,128]{1,0:T(8,128)S(1)} %add.67), channel_id=1, source_target_pairs={{0,4},{1,17},{2,6},{3,19},{4,0},{5,21},{6,2},{7,23},{8,12},{9,25},... | collective-permute-start | bytes 196616 | tf_op jit(solution)/shard_map/ppermute | solution.py:466
  25.4 0.7 %collective-permute-start.5 = (f32[128,128]{1,0:T(8,128)S(1)}, f32[128,128]{1,0:T(8,128)S(1)}, u32[]{:S(2)}, u32[]{:S(2)}) collective-permute-start(f32[128,128]{1,0:T(8,128)S(1)} %add.67), channel_id=1, source_target_pairs={{0,2},{1,9},{2,4},{3,11},{4,6},{5,13},{6,0},{7,15},{8,10},{9,17},{... | collective-permute-start | bytes 196616 | tf_op jit(solution)/shard_map/ppermute | solution.py:466
  26.2 1.9 %collective-permute-start.4 = (f32[128,128]{1,0:T(8,128)S(1)}, f32[128,128]{1,0:T(8,128)S(1)}, u32[]{:S(2)}, u32[]{:S(2)}) collective-permute-start(f32[128,128]{1,0:T(8,128)S(1)} %add.67), channel_id=1, source_target_pairs={{0,6},{1,25},{2,0},{3,27},{4,2},{5,29},{6,4},{7,31},{8,14},{9,1},{... | collective-permute-start | bytes 196616 | tf_op jit(solution)/shard_map/ppermute | solution.py:466
  28.1 0.0 collective-permute-done.6
  28.1 1.8 %collective-permute-done.5 = f32[128,128]{1,0:T(8,128)S(1)} collective-permute-done((f32[128,128]{1,0:T(8,128)S(1)}, f32[128,128]{1,0:T(8,128)S(1)}, u32[]{:S(2)}, u32[]{:S(2)}) %collective-permute-start.5) | collective-permute-done | bytes 65568 | tf_op jit(solution)/shard_map/ppermute | solution.py:466
  30.0 0.0 collective-permute-done.4
  30.0 2.6 %collective-permute-start.9 = (f32[128,128]{1,0:T(8,128)S(1)}, f32[128,128]{1,0:T(8,128)S(1)}, u32[]{:S(2)}, u32[]{:S(2)}) collective-permute-start(f32[128,128]{1,0:T(8,128)S(1)} %add_add_fusion.1), channel_id=1, source_target_pairs={{0,16},{1,5},{2,18},{3,7},{4,20},{5,1},{6,22},{7,3},{8,24},{9,13},... | collective-permute-start | bytes 196616 | tf_op jit(solution)/shard_map/ppermute | solution.py:466
  32.6 0.6 %collective-permute-start.8 = (f32[128,128]{1,0:T(8,128)S(1)}, f32[128,128]{1,0:T(8,128)S(1)}, u32[]{:S(2)}, u32[]{:S(2)}) collective-permute-start(f32[128,128]{1,0:T(8,128)S(1)} %add_add_fusion.1), channel_id=1, source_target_pairs={{0,8},{1,3},{2,10},{3,5},{4,12},{5,7},{6,14},{7,1},{8,16},{9,11},{... | collective-permute-start | bytes 196616 | tf_op jit(solution)/shard_map/ppermute | solution.py:466
  33.2 2.1 %collective-permute-start.7 = (f32[128,128]{1,0:T(8,128)S(1)}, f32[128,128]{1,0:T(8,128)S(1)}, u32[]{:S(2)}, u32[]{:S(2)}) collective-permute-start(f32[128,128]{1,0:T(8,128)S(1)} %add_add_fusion.1), channel_id=1, source_target_pairs={{0,24},{1,7},{2,26},{3,1},{4,28},{5,3},{6,30},{7,5},{8,0},{9,15},{... | collective-permute-start | bytes 196616 | tf_op jit(solution)/shard_map/ppermute | solution.py:466
  35.3 0.0 collective-permute-done.9
  35.3 1.6 %collective-permute-done.8 = f32[128,128]{1,0:T(8,128)S(1)} collective-permute-done((f32[128,128]{1,0:T(8,128)S(1)}, f32[128,128]{1,0:T(8,128)S(1)}, u32[]{:S(2)}, u32[]{:S(2)}) %collective-permute-start.8) | collective-permute-done | bytes 65568 | tf_op jit(solution)/shard_map/ppermute | solution.py:466
  36.9 0.0 collective-permute-done.7
  37.0 2.4 %factor.1.refs_0_ = f32[4,64,128]{2,1,0:T(8,128)S(1)} custom-call(f32[128,128]{1,0:T(8,128)S(1)} %add_add_fusion.gram), custom_call_target="tpu_custom_call" | custom-call | tf_op jit(solution)/shard_map/factor/pallas_call | solution.py:414
  39.4 3.0 %collective-permute-start.10 = (f32[4,64,128]{2,1,0:T(8,128)S(1)}, f32[4,64,128]{2,1,0:T(8,128)S(1)}, u32[]{:S(2)}, u32[]{:S(2)}) collective-permute-start(f32[4,64,128]{2,1,0:T(8,128)S(1)} %factor.1.refs_0_), channel_id=1, source_target_pairs={{0,1},{1,0},{2,3},{3,2},{4,5},{5,4},{6,7},{7,6},{8,9},{9,8},{10,11... | collective-permute-start | bytes 393224 | tf_op jit(solution)/shard_map/ppermute | solution.py:496
  42.3 1.3 %modes_own.1 = (bf16[2,8,256,128]{3,2,1,0:T(8,128)(2,1)}, f32[2,8,64,64]{3,2,1,0:T(8,128)}) custom-call(f32[4,64,128]{2,1,0:T(8,128)S(1)} %factor.1.refs_0_, bf16[4,256,512]{2,1,0:T(8,128)(2,1)S(1)} %get-tuple-element.23.refs_1_, f32[4,128]{1,0:T(4,128)S(1)} %copy-done), custom_call_target="tpu_custom_call" | custom-call | flops 300000000 | bytes 4194304 | tf_op jit(solution)/shard_map/modes_own/pallas_call | solution.py:427
  43.6 0.0 collective-permute-done.10.refs_0_
  43.6 1.3 %modes_far.1 = (bf16[2,8,256,128]{3,2,1,0:T(8,128)(2,1)}, f32[2,8,64,64]{3,2,1,0:T(8,128)}) custom-call(f32[4,64,128]{2,1,0:T(8,128)S(1)} %collective-permute-done.10.refs_0_, bf16[4,256,512]{2,1,0:T(8,128)(2,1)S(1)} %get-tuple-element.22.refs_1_, f32[4,128]{1,0:T(4,128)S(1)} %copy-done, ...), custom_call_target="tpu_custom_call", output_to_operand_aliasing={{0}: (3, {}), {1}: (4, {})} | custom-call | flops 300000000 | bytes 4194304 | tf_op jit(solution)/shard_map/modes_far/pallas_call | solution.py:427
  (3 shorter events, 0.0 us)
Async XLA Ops:
  1.6 9.6 %collective-permute-start.2 = (bf16[2,2,256,128]{3,2,1,0:T(8,128)(2,1)S(1)}, bf16[2,2,256,128]{3,2,1,0:T(8,128)(2,1)S(1)}, u32[]{:S(2)}, u32[]{:S(2)}) collective-permute-start(bf16[2,2,256,128]{3,2,1,0:T(8,128)(2,1)S(1)} %dynamic-slice_bitcast_fusion.3), channel_id=1, source_target_pairs={{0,64},{32,96},{64,0},{96,32},{1,65},{33,97},{65,1},{97,33},{2,66}... | collective-permute-start | bytes 786440 | tf_op jit(solution)/shard_map/ppermute | solution.py:484
  6.5 11.0 %collective-permute-start.1 = (bf16[2,2,256,128]{3,2,1,0:T(8,128)(2,1)S(1)}, bf16[2,2,256,128]{3,2,1,0:T(8,128)(2,1)S(1)}, u32[]{:S(2)}, u32[]{:S(2)}) collective-permute-start(bf16[2,2,256,128]{3,2,1,0:T(8,128)(2,1)S(1)} %get-tuple-element.30), channel_id=1, source_target_pairs={{0,32},{32,64},{64,96},{96,0},{1,33},{33,65},{65,97},{97,1},{2,34}... | collective-permute-start | bytes 786440 | tf_op jit(solution)/shard_map/ppermute | solution.py:479
  7.0 10.5 %collective-permute-start = (bf16[2,2,256,128]{3,2,1,0:T(8,128)(2,1)S(1)}, bf16[2,2,256,128]{3,2,1,0:T(8,128)(2,1)S(1)}, u32[]{:S(2)}, u32[]{:S(2)}) collective-permute-start(bf16[2,2,256,128]{3,2,1,0:T(8,128)(2,1)S(1)} %get-tuple-element.31), channel_id=1, source_target_pairs={{0,96},{32,0},{64,32},{96,64},{1,97},{33,1},{65,33},{97,65},{2,98}... | collective-permute-start | bytes 786440 | tf_op jit(solution)/shard_map/ppermute | solution.py:479
  9.3 2.9 %copy-start = (f32[4,128]{1,0:T(4,128)S(1)}, f32[4,128]{1,0:T(4,128)}, u32[]{:S(2)}) copy-start(f32[4,128]{1,0:T(4,128)} %refs_2_.3) | copy-start | bytes 6148
  19.2 2.5 %collective-permute-start.3 = (f32[128,128]{1,0:T(8,128)S(1)}, f32[128,128]{1,0:T(8,128)S(1)}, u32[]{:S(2)}, u32[]{:S(2)}) collective-permute-start(f32[128,128]{1,0:T(8,128)S(1)} %get-tuple-element.21), channel_id=1, source_target_pairs={{0,1},{1,0},{2,3},{3,2},{4,5},{5,4},{6,7},{7,6},{8,9},{9,8},{10,11... | collective-permute-start | bytes 196616 | tf_op jit(solution)/shard_map/ppermute | solution.py:492
  21.8 6.4 %collective-permute-start.6 = (f32[128,128]{1,0:T(8,128)S(1)}, f32[128,128]{1,0:T(8,128)S(1)}, u32[]{:S(2)}, u32[]{:S(2)}) collective-permute-start(f32[128,128]{1,0:T(8,128)S(1)} %add.67), channel_id=1, source_target_pairs={{0,4},{1,17},{2,6},{3,19},{4,0},{5,21},{6,2},{7,23},{8,12},{9,25},... | collective-permute-start | bytes 196616 | tf_op jit(solution)/shard_map/ppermute | solution.py:466
  25.4 4.5 %collective-permute-start.5 = (f32[128,128]{1,0:T(8,128)S(1)}, f32[128,128]{1,0:T(8,128)S(1)}, u32[]{:S(2)}, u32[]{:S(2)}) collective-permute-start(f32[128,128]{1,0:T(8,128)S(1)} %add.67), channel_id=1, source_target_pairs={{0,2},{1,9},{2,4},{3,11},{4,6},{5,13},{6,0},{7,15},{8,10},{9,17},{... | collective-permute-start | bytes 196616 | tf_op jit(solution)/shard_map/ppermute | solution.py:466
  26.2 3.8 %collective-permute-start.4 = (f32[128,128]{1,0:T(8,128)S(1)}, f32[128,128]{1,0:T(8,128)S(1)}, u32[]{:S(2)}, u32[]{:S(2)}) collective-permute-start(f32[128,128]{1,0:T(8,128)S(1)} %add.67), channel_id=1, source_target_pairs={{0,6},{1,25},{2,0},{3,27},{4,2},{5,29},{6,4},{7,31},{8,14},{9,1},{... | collective-permute-start | bytes 196616 | tf_op jit(solution)/shard_map/ppermute | solution.py:466
  30.0 5.3 %collective-permute-start.9 = (f32[128,128]{1,0:T(8,128)S(1)}, f32[128,128]{1,0:T(8,128)S(1)}, u32[]{:S(2)}, u32[]{:S(2)}) collective-permute-start(f32[128,128]{1,0:T(8,128)S(1)} %add_add_fusion.1), channel_id=1, source_target_pairs={{0,16},{1,5},{2,18},{3,7},{4,20},{5,1},{6,22},{7,3},{8,24},{9,13},... | collective-permute-start | bytes 196616 | tf_op jit(solution)/shard_map/ppermute | solution.py:466
  32.6 4.3 %collective-permute-start.8 = (f32[128,128]{1,0:T(8,128)S(1)}, f32[128,128]{1,0:T(8,128)S(1)}, u32[]{:S(2)}, u32[]{:S(2)}) collective-permute-start(f32[128,128]{1,0:T(8,128)S(1)} %add_add_fusion.1), channel_id=1, source_target_pairs={{0,8},{1,3},{2,10},{3,5},{4,12},{5,7},{6,14},{7,1},{8,16},{9,11},{... | collective-permute-start | bytes 196616 | tf_op jit(solution)/shard_map/ppermute | solution.py:466
  33.2 3.7 %collective-permute-start.7 = (f32[128,128]{1,0:T(8,128)S(1)}, f32[128,128]{1,0:T(8,128)S(1)}, u32[]{:S(2)}, u32[]{:S(2)}) collective-permute-start(f32[128,128]{1,0:T(8,128)S(1)} %add_add_fusion.1), channel_id=1, source_target_pairs={{0,24},{1,7},{2,26},{3,1},{4,28},{5,3},{6,30},{7,5},{8,0},{9,15},{... | collective-permute-start | bytes 196616 | tf_op jit(solution)/shard_map/ppermute | solution.py:466
  39.4 4.3 %collective-permute-start.10 = (f32[4,64,128]{2,1,0:T(8,128)S(1)}, f32[4,64,128]{2,1,0:T(8,128)S(1)}, u32[]{:S(2)}, u32[]{:S(2)}) collective-permute-start(f32[4,64,128]{2,1,0:T(8,128)S(1)} %factor.1.refs_0_), channel_id=1, source_target_pairs={{0,1},{1,0},{2,3},{3,2},{4,5},{5,4},{6,7},{7,6},{8,9},{9,8},{10,11... | collective-permute-start | bytes 393224 | tf_op jit(solution)/shard_map/ppermute | solution.py:496

commit v7 on v5

--- a/solution.py
+++ b/solution.py
@@ -156,7 +156,7 @@
             even_ref[s, 3, rows, :] = y0[1] - y2[1]
         return 0
 
-    lax.fori_loop(0, ROWS // 16, step, 0)
+    lax.fori_loop(0, ROWS // 16, step, 0, unroll=4)
 
 
 def send_kernel(near3, near1, weight, even, other_ref, s_ref, send_ref, work, mixed, products):
@@ -196,7 +196,7 @@
             other_ref[q, 1, rows, :] = x0[1] - v[1]
         return 0
 
-    lax.fori_loop(0, ROWS // 16, step, 0)
+    lax.fori_loop(0, ROWS // 16, step, 0, unroll=4)
     pack_gram(work, s_ref, send_ref, mixed, products)
 
 

time: 45.3 us -> 45.2 us (level)
  no operation moved by 1% of the time
where the time goes in v7:
time: 45.2 us; the launch traced here: 45 us
  starting transfers between devices  22.5 us (50%)
  waiting for transfers between devices  10.5 us (23%)
  Pallas kernels  8.17 us (18%)
  local copies, waits for them, and re-layouts  3.01 us (7%)
  between operations  0.74 us (2%)
    ppermute x6, starting transfers between devices, sum_over_chips(): lax.ppermute(value, 'space', space_perm(along, d))  11.9 us
    ppermute x2, waiting for transfers between devices, move(): lax.ppermute(piece(d, source), 'tm', [(i, (i + d) % 4) for i in range(4)])  5.12 us
    ppermute x1, starting transfers between devices, on_device(): near[2] = lax.ppermute(first, 'tm', [(i, (i + 2) % 4) for i in range(4)])  3.82 us
    ppermute x6, waiting for transfers between devices, sum_over_chips(): lax.ppermute(value, 'space', space_perm(along, d))  3.48 us
    squeeze x3, local copies, waits for them, and re-layouts, piece(): return lax.dynamic_index_in_dim(source, (t + d) % 4, 2, keepdims=False)  3.01 us
    ppermute x1, starting transfers between devices, on_device(): far = lax.ppermute(factor, 'space', across)  2.77 us
    ppermute x2, starting transfers between devices, move(): lax.ppermute(piece(d, source), 'tm', [(i, (i + d) % 4) for i in range(4)])  2.75 us
    pallas_call x2, Pallas kernels, run_modes(): pl.pallas_call(functools.partial(modes_kernel, slot), name='modes_far' if...  2.66 us
  transfers between devices with their start and end apart: 11, of which 4 were waited for; matrix products, arithmetic and copies ran while one was open for 5% of the time, Pallas kernels for 6%

profile of v7, /device:TPU:1, one launch (start us, length us, event | category | flops | bytes accessed | tf_op | source)
XLA Modules:
  0.0 45.0 jit_solution(5190056658841283818)
XLA Ops:
  0.6 1.0 %dynamic-slice_bitcast_fusion.3 = bf16[2,2,256,128]{3,2,1,0:T(8,128)(2,1)S(1)} fusion(bf16[2,2,4,256,128]{4,3,2,1,0:T(8,128)(2,1)} %bitcast.17, s32[]{:T(128)S(6)} %select_n.33), kind=kLoop, calls=%fused_computation.3 | loop fusion | bytes 524292 | tf_op jit(solution)/shard_map/jit(dynamic_index_in_dim)/squeeze | solution.py:476
  1.6 3.8 %collective-permute-start.2 = (bf16[2,2,256,128]{3,2,1,0:T(8,128)(2,1)S(1)}, bf16[2,2,256,128]{3,2,1,0:T(8,128)(2,1)S(1)}, u32[]{:S(2)}, u32[]{:S(2)}) collective-permute-start(bf16[2,2,256,128]{3,2,1,0:T(8,128)(2,1)S(1)} %dynamic-slice_bitcast_fusion.3), channel_id=1, source_target_pairs={{0,64},{32,96},{64,0},{96,32},{1,65},{33,97},{65,1},{97,33},{2,66}... | collective-permute-start | bytes 786440 | tf_op jit(solution)/shard_map/ppermute | solution.py:484
  5.5 1.1 %dynamic-slice_bitcast_fusion.1 = (bf16[2,2,256,128]{3,2,1,0:T(8,128)(2,1)S(1)}, bf16[2,2,256,128]{3,2,1,0:T(8,128)(2,1)S(1)}) fusion(s32[]{:T(128)S(6)} %select_n.37, s32[]{:T(128)S(6)} %select_n.35, bf16[2,2,4,256,128]{4,3,2,1,0:T(8,128)(2,1)} %bitcast.18), kind=kLoop, calls=%fused_computation.1 | loop fusion | bytes 1048584 | tf_op jit(solution)/shard_map/jit(dynamic_index_in_dim)/squeeze | solution.py:476
  6.5 0.5 %collective-permute-start.1 = (bf16[2,2,256,128]{3,2,1,0:T(8,128)(2,1)S(1)}, bf16[2,2,256,128]{3,2,1,0:T(8,128)(2,1)S(1)}, u32[]{:S(2)}, u32[]{:S(2)}) collective-permute-start(bf16[2,2,256,128]{3,2,1,0:T(8,128)(2,1)S(1)} %get-tuple-element.30), channel_id=1, source_target_pairs={{0,32},{32,64},{64,96},{96,0},{1,33},{33,65},{65,97},{97,1},{2,34}... | collective-permute-start | bytes 786440 | tf_op jit(solution)/shard_map/ppermute | solution.py:479
  7.0 2.3 %collective-permute-start = (bf16[2,2,256,128]{3,2,1,0:T(8,128)(2,1)S(1)}, bf16[2,2,256,128]{3,2,1,0:T(8,128)(2,1)S(1)}, u32[]{:S(2)}, u32[]{:S(2)}) collective-permute-start(bf16[2,2,256,128]{3,2,1,0:T(8,128)(2,1)S(1)} %get-tuple-element.31), channel_id=1, source_target_pairs={{0,96},{32,0},{64,32},{96,64},{1,97},{33,1},{65,33},{97,65},{2,98}... | collective-permute-start | bytes 786440 | tf_op jit(solution)/shard_map/ppermute | solution.py:479
  9.3 0.0 copy-start
  9.3 1.9 %collective-permute-done.2.near2 = bf16[2,2,256,128]{3,2,1,0:T(8,128)(2,1)S(1)} collective-permute-done((bf16[2,2,256,128]{3,2,1,0:T(8,128)(2,1)S(1)}, bf16[2,2,256,128]{3,2,1,0:T(8,128)(2,1)S(1)}, u32[]{:S(2)}, u32[]{:S(2)}) %collective-permute-start.2) | collective-permute-done | bytes 262176 | tf_op jit(solution)/shard_map/ppermute | solution.py:484
  11.2 1.0 %dynamic-slice_bitcast_fusion.own = bf16[2,2,256,128]{3,2,1,0:T(8,128)(2,1)S(1)} fusion(s32[]{:T(128)S(6)} %select_n.39, bf16[2,2,4,256,128]{4,3,2,1,0:T(8,128)(2,1)} %bitcast.19), kind=kLoop, calls=%fused_computation | loop fusion | bytes 524292 | tf_op jit(solution)/shard_map/jit(dynamic_index_in_dim)/squeeze | solution.py:476
  12.2 0.0 copy-done
  12.2 0.2 even.1
  12.4 5.1 %collective-permute-done.1.near1 = bf16[2,2,256,128]{3,2,1,0:T(8,128)(2,1)S(1)} collective-permute-done((bf16[2,2,256,128]{3,2,1,0:T(8,128)(2,1)S(1)}, bf16[2,2,256,128]{3,2,1,0:T(8,128)(2,1)S(1)}, u32[]{:S(2)}, u32[]{:S(2)}) %collective-permute-start.1) | collective-permute-done | bytes 262176 | tf_op jit(solution)/shard_map/ppermute | solution.py:479
  17.5 0.0 collective-permute-done.near3
  17.5 1.7 %send_gram.1 = (f32[4,2,256,128]{3,2,1,0:T(8,128)S(1)}, bf16[4,256,512]{2,1,0:T(8,128)(2,1)S(1)}, f32[128,128]{1,0:T(8,128)S(1)}) custom-call(bf16[2,2,256,128]{3,2,1,0:T(8,128)(2,1)S(1)} %collective-permute-done.near3, bf16[2,2,256,128]{3,2,1,0:T(8,128)(2,1)S(1)} %collective-permute-done.1.near1, f32[4,128]{1,0:T(4,128)S(1)} %copy-done, ...), custom_call_target="tpu_custom_call" | custom-call | tf_op jit(solution)/shard_map/send_gram/pallas_call | solution.py:375
  19.2 1.3 %collective-permute-start.3 = (f32[128,128]{1,0:T(8,128)S(1)}, f32[128,128]{1,0:T(8,128)S(1)}, u32[]{:S(2)}, u32[]{:S(2)}) collective-permute-start(f32[128,128]{1,0:T(8,128)S(1)} %get-tuple-element.21), channel_id=1, source_target_pairs={{0,1},{1,0},{2,3},{3,2},{4,5},{5,4},{6,7},{7,6},{8,9},{9,8},{10,11... | collective-permute-start | bytes 196616 | tf_op jit(solution)/shard_map/ppermute | solution.py:492
  20.5 1.2 %keep_gram.1 = (bf16[4,256,512]{2,1,0:T(8,128)(2,1)S(1)}, f32[128,128]{1,0:T(8,128)S(1)}) custom-call(f32[4,2,256,128]{3,2,1,0:T(8,128)S(1)} %get-tuple-element.19.work), custom_call_target="tpu_custom_call" | custom-call | flops 300000000 | bytes 2097152 | tf_op jit(solution)/shard_map/keep_gram/pallas_call | solution.py:395
  21.7 0.0 collective-permute-done.3
  21.8 2.8 %collective-permute-start.6 = (f32[128,128]{1,0:T(8,128)S(1)}, f32[128,128]{1,0:T(8,128)S(1)}, u32[]{:S(2)}, u32[]{:S(2)}) collective-permute-start(f32[128,128]{1,0:T(8,128)S(1)} %add.67), channel_id=1, source_target_pairs={{0,4},{1,5},{2,6},{3,7},{4,0},{5,1},{6,2},{7,3},{8,12},{9,13},{10,... | collective-permute-start | bytes 196616 | tf_op jit(solution)/shard_map/ppermute | solution.py:466
  24.6 0.3 collective-permute-start.5
  24.9 2.4 %collective-permute-start.4 = (f32[128,128]{1,0:T(8,128)S(1)}, f32[128,128]{1,0:T(8,128)S(1)}, u32[]{:S(2)}, u32[]{:S(2)}) collective-permute-start(f32[128,128]{1,0:T(8,128)S(1)} %add.67), channel_id=1, source_target_pairs={{0,6},{1,7},{2,0},{3,1},{4,2},{5,3},{6,4},{7,5},{8,14},{9,15},{10,... | collective-permute-start | bytes 196616 | tf_op jit(solution)/shard_map/ppermute | solution.py:466
  27.3 0.0 collective-permute-done.6
  27.3 1.6 %collective-permute-done.5 = f32[128,128]{1,0:T(8,128)S(1)} collective-permute-done((f32[128,128]{1,0:T(8,128)S(1)}, f32[128,128]{1,0:T(8,128)S(1)}, u32[]{:S(2)}, u32[]{:S(2)}) %collective-permute-start.5) | collective-permute-done | bytes 65568 | tf_op jit(solution)/shard_map/ppermute | solution.py:466
  28.9 0.0 collective-permute-done.4
  28.9 3.7 %collective-permute-start.9 = (f32[128,128]{1,0:T(8,128)S(1)}, f32[128,128]{1,0:T(8,128)S(1)}, u32[]{:S(2)}, u32[]{:S(2)}) collective-permute-start(f32[128,128]{1,0:T(8,128)S(1)} %add_add_fusion.1), channel_id=1, source_target_pairs={{0,16},{1,17},{2,18},{3,19},{4,20},{5,21},{6,22},{7,23},{8,24},{9,... | collective-permute-start | bytes 196616 | tf_op jit(solution)/shard_map/ppermute | solution.py:466
  32.6 0.7 %collective-permute-start.8 = (f32[128,128]{1,0:T(8,128)S(1)}, f32[128,128]{1,0:T(8,128)S(1)}, u32[]{:S(2)}, u32[]{:S(2)}) collective-permute-start(f32[128,128]{1,0:T(8,128)S(1)} %add_add_fusion.1), channel_id=1, source_target_pairs={{0,8},{1,9},{2,10},{3,11},{4,12},{5,13},{6,14},{7,15},{8,16},{9,17... | collective-permute-start | bytes 196616 | tf_op jit(solution)/shard_map/ppermute | solution.py:466
  33.4 1.9 %collective-permute-start.7 = (f32[128,128]{1,0:T(8,128)S(1)}, f32[128,128]{1,0:T(8,128)S(1)}, u32[]{:S(2)}, u32[]{:S(2)}) collective-permute-start(f32[128,128]{1,0:T(8,128)S(1)} %add_add_fusion.1), channel_id=1, source_target_pairs={{0,24},{1,25},{2,26},{3,27},{4,28},{5,29},{6,30},{7,31},{8,0},{9,1... | collective-permute-start | bytes 196616 | tf_op jit(solution)/shard_map/ppermute | solution.py:466
  35.3 0.0 collective-permute-done.9
  35.3 1.8 %collective-permute-done.8 = f32[128,128]{1,0:T(8,128)S(1)} collective-permute-done((f32[128,128]{1,0:T(8,128)S(1)}, f32[128,128]{1,0:T(8,128)S(1)}, u32[]{:S(2)}, u32[]{:S(2)}) %collective-permute-start.8) | collective-permute-done | bytes 65568 | tf_op jit(solution)/shard_map/ppermute | solution.py:466
  37.1 0.0 collective-permute-done.7
  37.1 2.4 %factor.1.refs_0_ = f32[4,64,128]{2,1,0:T(8,128)S(1)} custom-call(f32[128,128]{1,0:T(8,128)S(1)} %add_add_fusion.gram), custom_call_target="tpu_custom_call" | custom-call | tf_op jit(solution)/shard_map/factor/pallas_call | solution.py:414
  39.5 2.8 %collective-permute-start.10 = (f32[4,64,128]{2,1,0:T(8,128)S(1)}, f32[4,64,128]{2,1,0:T(8,128)S(1)}, u32[]{:S(2)}, u32[]{:S(2)}) collective-permute-start(f32[4,64,128]{2,1,0:T(8,128)S(1)} %factor.1.refs_0_), channel_id=1, source_target_pairs={{0,1},{1,0},{2,3},{3,2},{4,5},{5,4},{6,7},{7,6},{8,9},{9,8},{10,11... | collective-permute-start | bytes 393224 | tf_op jit(solution)/shard_map/ppermute | solution.py:496
  42.3 1.3 %modes_own.1 = (bf16[2,8,256,128]{3,2,1,0:T(8,128)(2,1)}, f32[2,8,64,64]{3,2,1,0:T(8,128)}) custom-call(f32[4,64,128]{2,1,0:T(8,128)S(1)} %factor.1.refs_0_, bf16[4,256,512]{2,1,0:T(8,128)(2,1)S(1)} %get-tuple-element.23.refs_1_, f32[4,128]{1,0:T(4,128)S(1)} %copy-done), custom_call_target="tpu_custom_call" | custom-call | flops 300000000 | bytes 4194304 | tf_op jit(solution)/shard_map/modes_own/pallas_call | solution.py:427
  43.6 0.0 collective-permute-done.10.refs_0_
  43.6 1.3 %modes_far.1 = (bf16[2,8,256,128]{3,2,1,0:T(8,128)(2,1)}, f32[2,8,64,64]{3,2,1,0:T(8,128)}) custom-call(f32[4,64,128]{2,1,0:T(8,128)S(1)} %collective-permute-done.10.refs_0_, bf16[4,256,512]{2,1,0:T(8,128)(2,1)S(1)} %get-tuple-element.22.refs_1_, f32[4,128]{1,0:T(4,128)S(1)} %copy-done, ...), custom_call_target="tpu_custom_call", output_to_operand_aliasing={{0}: (3, {}), {1}: (4, {})} | custom-call | flops 300000000 | bytes 4194304 | tf_op jit(solution)/shard_map/modes_far/pallas_call | solution.py:427
  (3 shorter events, 0.0 us)
Async XLA Ops:
  1.6 9.6 %collective-permute-start.2 = (bf16[2,2,256,128]{3,2,1,0:T(8,128)(2,1)S(1)}, bf16[2,2,256,128]{3,2,1,0:T(8,128)(2,1)S(1)}, u32[]{:S(2)}, u32[]{:S(2)}) collective-permute-start(bf16[2,2,256,128]{3,2,1,0:T(8,128)(2,1)S(1)} %dynamic-slice_bitcast_fusion.3), channel_id=1, source_target_pairs={{0,64},{32,96},{64,0},{96,32},{1,65},{33,97},{65,1},{97,33},{2,66}... | collective-permute-start | bytes 786440 | tf_op jit(solution)/shard_map/ppermute | solution.py:484
  6.5 11.0 %collective-permute-start.1 = (bf16[2,2,256,128]{3,2,1,0:T(8,128)(2,1)S(1)}, bf16[2,2,256,128]{3,2,1,0:T(8,128)(2,1)S(1)}, u32[]{:S(2)}, u32[]{:S(2)}) collective-permute-start(bf16[2,2,256,128]{3,2,1,0:T(8,128)(2,1)S(1)} %get-tuple-element.30), channel_id=1, source_target_pairs={{0,32},{32,64},{64,96},{96,0},{1,33},{33,65},{65,97},{97,1},{2,34}... | collective-permute-start | bytes 786440 | tf_op jit(solution)/shard_map/ppermute | solution.py:479
  7.0 10.5 %collective-permute-start = (bf16[2,2,256,128]{3,2,1,0:T(8,128)(2,1)S(1)}, bf16[2,2,256,128]{3,2,1,0:T(8,128)(2,1)S(1)}, u32[]{:S(2)}, u32[]{:S(2)}) collective-permute-start(bf16[2,2,256,128]{3,2,1,0:T(8,128)(2,1)S(1)} %get-tuple-element.31), channel_id=1, source_target_pairs={{0,96},{32,0},{64,32},{96,64},{1,97},{33,1},{65,33},{97,65},{2,98}... | collective-permute-start | bytes 786440 | tf_op jit(solution)/shard_map/ppermute | solution.py:479
  9.3 2.9 %copy-start = (f32[4,128]{1,0:T(4,128)S(1)}, f32[4,128]{1,0:T(4,128)}, u32[]{:S(2)}) copy-start(f32[4,128]{1,0:T(4,128)} %refs_2_.3) | copy-start | bytes 6148
  19.2 2.5 %collective-permute-start.3 = (f32[128,128]{1,0:T(8,128)S(1)}, f32[128,128]{1,0:T(8,128)S(1)}, u32[]{:S(2)}, u32[]{:S(2)}) collective-permute-start(f32[128,128]{1,0:T(8,128)S(1)} %get-tuple-element.21), channel_id=1, source_target_pairs={{0,1},{1,0},{2,3},{3,2},{4,5},{5,4},{6,7},{7,6},{8,9},{9,8},{10,11... | collective-permute-start | bytes 196616 | tf_op jit(solution)/shard_map/ppermute | solution.py:492
  21.8 5.5 %collective-permute-start.6 = (f32[128,128]{1,0:T(8,128)S(1)}, f32[128,128]{1,0:T(8,128)S(1)}, u32[]{:S(2)}, u32[]{:S(2)}) collective-permute-start(f32[128,128]{1,0:T(8,128)S(1)} %add.67), channel_id=1, source_target_pairs={{0,4},{1,5},{2,6},{3,7},{4,0},{5,1},{6,2},{7,3},{8,12},{9,13},{10,... | collective-permute-start | bytes 196616 | tf_op jit(solution)/shard_map/ppermute | solution.py:466
  24.6 4.3 %collective-permute-start.5 = (f32[128,128]{1,0:T(8,128)S(1)}, f32[128,128]{1,0:T(8,128)S(1)}, u32[]{:S(2)}, u32[]{:S(2)}) collective-permute-start(f32[128,128]{1,0:T(8,128)S(1)} %add.67), channel_id=1, source_target_pairs={{0,2},{1,3},{2,4},{3,5},{4,6},{5,7},{6,0},{7,1},{8,10},{9,11},{10,... | collective-permute-start | bytes 196616 | tf_op jit(solution)/shard_map/ppermute | solution.py:466
  24.9 4.0 %collective-permute-start.4 = (f32[128,128]{1,0:T(8,128)S(1)}, f32[128,128]{1,0:T(8,128)S(1)}, u32[]{:S(2)}, u32[]{:S(2)}) collective-permute-start(f32[128,128]{1,0:T(8,128)S(1)} %add.67), channel_id=1, source_target_pairs={{0,6},{1,7},{2,0},{3,1},{4,2},{5,3},{6,4},{7,5},{8,14},{9,15},{10,... | collective-permute-start | bytes 196616 | tf_op jit(solution)/shard_map/ppermute | solution.py:466
  28.9 6.4 %collective-permute-start.9 = (f32[128,128]{1,0:T(8,128)S(1)}, f32[128,128]{1,0:T(8,128)S(1)}, u32[]{:S(2)}, u32[]{:S(2)}) collective-permute-start(f32[128,128]{1,0:T(8,128)S(1)} %add_add_fusion.1), channel_id=1, source_target_pairs={{0,16},{1,17},{2,18},{3,19},{4,20},{5,21},{6,22},{7,23},{8,24},{9,... | collective-permute-start | bytes 196616 | tf_op jit(solution)/shard_map/ppermute | solution.py:466
  32.6 4.5 %collective-permute-start.8 = (f32[128,128]{1,0:T(8,128)S(1)}, f32[128,128]{1,0:T(8,128)S(1)}, u32[]{:S(2)}, u32[]{:S(2)}) collective-permute-start(f32[128,128]{1,0:T(8,128)S(1)} %add_add_fusion.1), channel_id=1, source_target_pairs={{0,8},{1,9},{2,10},{3,11},{4,12},{5,13},{6,14},{7,15},{8,16},{9,17... | collective-permute-start | bytes 196616 | tf_op jit(solution)/shard_map/ppermute | solution.py:466
  33.4 3.8 %collective-permute-start.7 = (f32[128,128]{1,0:T(8,128)S(1)}, f32[128,128]{1,0:T(8,128)S(1)}, u32[]{:S(2)}, u32[]{:S(2)}) collective-permute-start(f32[128,128]{1,0:T(8,128)S(1)} %add_add_fusion.1), channel_id=1, source_target_pairs={{0,24},{1,25},{2,26},{3,27},{4,28},{5,29},{6,30},{7,31},{8,0},{9,1... | collective-permute-start | bytes 196616 | tf_op jit(solution)/shard_map/ppermute | solution.py:466
  39.5 4.1 %collective-permute-start.10 = (f32[4,64,128]{2,1,0:T(8,128)S(1)}, f32[4,64,128]{2,1,0:T(8,128)S(1)}, u32[]{:S(2)}, u32[]{:S(2)}) collective-permute-start(f32[4,64,128]{2,1,0:T(8,128)S(1)} %factor.1.refs_0_), channel_id=1, source_target_pairs={{0,1},{1,0},{2,3},{3,2},{4,5},{5,4},{6,7},{7,6},{8,9},{9,8},{10,11... | collective-permute-start | bytes 393224 | tf_op jit(solution)/shard_map/ppermute | solution.py:496

commit v8 on v6

--- a/solution.py
+++ b/solution.py
@@ -156,7 +156,7 @@
             even_ref[s, 3, rows, :] = y0[1] - y2[1]
         return 0
 
-    lax.fori_loop(0, ROWS // 16, step, 0, unroll=4)
+    lax.fori_loop(0, ROWS // 16, step, 0)
 
 
 def send_kernel(near3, near1, weight, even, other_ref, s_ref, send_ref, work, mixed, products):
@@ -196,7 +196,7 @@
             other_ref[q, 1, rows, :] = x0[1] - v[1]
         return 0
 
-    lax.fori_loop(0, ROWS // 16, step, 0, unroll=4)
+    lax.fori_loop(0, ROWS // 16, step, 0)
     pack_gram(work, s_ref, send_ref, mixed, products)
 
 

time: 45.2 us -> 45.3 us (level)
  no operation moved by 1% of the time
where the time goes in v8:
time: 45.3 us; the launch traced here: 45.1 us
  starting transfers between devices  22.5 us (50%)
  waiting for transfers between devices  10.5 us (23%)
  Pallas kernels  8.31 us (18%)
  local copies, waits for them, and re-layouts  3.01 us (7%)
  between operations  0.74 us (2%)
    ppermute x6, starting transfers between devices, sum_over_chips(): lax.ppermute(value, 'space', space_perm(first, d))  11.7 us
    ppermute x2, waiting for transfers between devices, move(): lax.ppermute(piece(d, source), 'tm', [(i, (i + d) % 4) for i in range(4)])  5.05 us
    ppermute x1, starting transfers between devices, on_device(): near[2] = lax.ppermute(first, 'tm', [(i, (i + 2) % 4) for i in range(4)])  3.82 us
    ppermute x6, waiting for transfers between devices, sum_over_chips(): lax.ppermute(value, 'space', space_perm(first, d))  3.5 us
    squeeze x3, local copies, waits for them, and re-layouts, piece(): return lax.dynamic_index_in_dim(source, (t + d) % 4, 2, keepdims=False)  3.01 us
    ppermute x1, starting transfers between devices, on_device(): far = lax.ppermute(factor, 'space', across)  2.95 us
    ppermute x2, starting transfers between devices, move(): lax.ppermute(piece(d, source), 'tm', [(i, (i + d) % 4) for i in range(4)])  2.75 us
    pallas_call x2, Pallas kernels, run_modes(): pl.pallas_call(functools.partial(modes_kernel, slot), name='modes_far' if...  2.66 us
  transfers between devices with their start and end apart: 11, of which 4 were waited for; matrix products, arithmetic and copies ran while one was open for 5% of the time, Pallas kernels for 6%

profile of v8, /device:TPU:1, one launch (start us, length us, event | category | flops | bytes accessed | tf_op | source)
XLA Modules:
  0.0 45.1 jit_solution(18388240999044371026)
XLA Ops:
  0.6 1.0 %dynamic-slice_bitcast_fusion.3 = bf16[2,2,256,128]{3,2,1,0:T(8,128)(2,1)S(1)} fusion(bf16[2,2,4,256,128]{4,3,2,1,0:T(8,128)(2,1)} %bitcast.17, s32[]{:T(128)S(6)} %select_n.33), kind=kLoop, calls=%fused_computation.3 | loop fusion | bytes 524292 | tf_op jit(solution)/shard_map/jit(dynamic_index_in_dim)/squeeze | solution.py:476
  1.6 3.8 %collective-permute-start.2 = (bf16[2,2,256,128]{3,2,1,0:T(8,128)(2,1)S(1)}, bf16[2,2,256,128]{3,2,1,0:T(8,128)(2,1)S(1)}, u32[]{:S(2)}, u32[]{:S(2)}) collective-permute-start(bf16[2,2,256,128]{3,2,1,0:T(8,128)(2,1)S(1)} %dynamic-slice_bitcast_fusion.3), channel_id=1, source_target_pairs={{0,64},{32,96},{64,0},{96,32},{1,65},{33,97},{65,1},{97,33},{2,66}... | collective-permute-start | bytes 786440 | tf_op jit(solution)/shard_map/ppermute | solution.py:484
  5.5 1.1 %dynamic-slice_bitcast_fusion.1 = (bf16[2,2,256,128]{3,2,1,0:T(8,128)(2,1)S(1)}, bf16[2,2,256,128]{3,2,1,0:T(8,128)(2,1)S(1)}) fusion(s32[]{:T(128)S(6)} %select_n.37, s32[]{:T(128)S(6)} %select_n.35, bf16[2,2,4,256,128]{4,3,2,1,0:T(8,128)(2,1)} %bitcast.18), kind=kLoop, calls=%fused_computation.1 | loop fusion | bytes 1048584 | tf_op jit(solution)/shard_map/jit(dynamic_index_in_dim)/squeeze | solution.py:476
  6.5 0.5 %collective-permute-start.1 = (bf16[2,2,256,128]{3,2,1,0:T(8,128)(2,1)S(1)}, bf16[2,2,256,128]{3,2,1,0:T(8,128)(2,1)S(1)}, u32[]{:S(2)}, u32[]{:S(2)}) collective-permute-start(bf16[2,2,256,128]{3,2,1,0:T(8,128)(2,1)S(1)} %get-tuple-element.30), channel_id=1, source_target_pairs={{0,32},{32,64},{64,96},{96,0},{1,33},{33,65},{65,97},{97,1},{2,34}... | collective-permute-start | bytes 786440 | tf_op jit(solution)/shard_map/ppermute | solution.py:479
  7.0 2.3 %collective-permute-start = (bf16[2,2,256,128]{3,2,1,0:T(8,128)(2,1)S(1)}, bf16[2,2,256,128]{3,2,1,0:T(8,128)(2,1)S(1)}, u32[]{:S(2)}, u32[]{:S(2)}) collective-permute-start(bf16[2,2,256,128]{3,2,1,0:T(8,128)(2,1)S(1)} %get-tuple-element.31), channel_id=1, source_target_pairs={{0,96},{32,0},{64,32},{96,64},{1,97},{33,1},{65,33},{97,65},{2,98}... | collective-permute-start | bytes 786440 | tf_op jit(solution)/shard_map/ppermute | solution.py:479
  9.3 0.0 copy-start
  9.3 1.9 %collective-permute-done.2.near2 = bf16[2,2,256,128]{3,2,1,0:T(8,128)(2,1)S(1)} collective-permute-done((bf16[2,2,256,128]{3,2,1,0:T(8,128)(2,1)S(1)}, bf16[2,2,256,128]{3,2,1,0:T(8,128)(2,1)S(1)}, u32[]{:S(2)}, u32[]{:S(2)}) %collective-permute-start.2) | collective-permute-done | bytes 262176 | tf_op jit(solution)/shard_map/ppermute | solution.py:484
  11.2 1.0 %dynamic-slice_bitcast_fusion.own = bf16[2,2,256,128]{3,2,1,0:T(8,128)(2,1)S(1)} fusion(s32[]{:T(128)S(6)} %select_n.39, bf16[2,2,4,256,128]{4,3,2,1,0:T(8,128)(2,1)} %bitcast.19), kind=kLoop, calls=%fused_computation | loop fusion | bytes 524292 | tf_op jit(solution)/shard_map/jit(dynamic_index_in_dim)/squeeze | solution.py:476
  12.2 0.0 copy-done
  12.2 0.3 even.1
  12.5 5.1 %collective-permute-done.1.near1 = bf16[2,2,256,128]{3,2,1,0:T(8,128)(2,1)S(1)} collective-permute-done((bf16[2,2,256,128]{3,2,1,0:T(8,128)(2,1)S(1)}, bf16[2,2,256,128]{3,2,1,0:T(8,128)(2,1)S(1)}, u32[]{:S(2)}, u32[]{:S(2)}) %collective-permute-start.1) | collective-permute-done | bytes 262176 | tf_op jit(solution)/shard_map/ppermute | solution.py:479
  17.5 0.0 collective-permute-done.near3
  17.5 1.8 %send_gram.1 = (f32[4,2,256,128]{3,2,1,0:T(8,128)S(1)}, bf16[4,256,512]{2,1,0:T(8,128)(2,1)S(1)}, f32[128,128]{1,0:T(8,128)S(1)}) custom-call(bf16[2,2,256,128]{3,2,1,0:T(8,128)(2,1)S(1)} %collective-permute-done.near3, bf16[2,2,256,128]{3,2,1,0:T(8,128)(2,1)S(1)} %collective-permute-done.1.near1, f32[4,128]{1,0:T(4,128)S(1)} %copy-done, ...), custom_call_target="tpu_custom_call" | custom-call | tf_op jit(solution)/shard_map/send_gram/pallas_call | solution.py:375
  19.3 1.3 %collective-permute-start.3 = (f32[128,128]{1,0:T(8,128)S(1)}, f32[128,128]{1,0:T(8,128)S(1)}, u32[]{:S(2)}, u32[]{:S(2)}) collective-permute-start(f32[128,128]{1,0:T(8,128)S(1)} %get-tuple-element.21), channel_id=1, source_target_pairs={{0,1},{1,0},{2,3},{3,2},{4,5},{5,4},{6,7},{7,6},{8,9},{9,8},{10,11... | collective-permute-start | bytes 196616 | tf_op jit(solution)/shard_map/ppermute | solution.py:492
  20.6 1.2 %keep_gram.1 = (bf16[4,256,512]{2,1,0:T(8,128)(2,1)S(1)}, f32[128,128]{1,0:T(8,128)S(1)}) custom-call(f32[4,2,256,128]{3,2,1,0:T(8,128)S(1)} %get-tuple-element.19.work), custom_call_target="tpu_custom_call" | custom-call | flops 300000000 | bytes 2097152 | tf_op jit(solution)/shard_map/keep_gram/pallas_call | solution.py:395
  21.8 0.0 collective-permute-done.3
  21.8 3.7 %collective-permute-start.6 = (f32[128,128]{1,0:T(8,128)S(1)}, f32[128,128]{1,0:T(8,128)S(1)}, u32[]{:S(2)}, u32[]{:S(2)}) collective-permute-start(f32[128,128]{1,0:T(8,128)S(1)} %add.67), channel_id=1, source_target_pairs={{0,4},{1,17},{2,6},{3,19},{4,0},{5,21},{6,2},{7,23},{8,12},{9,25},... | collective-permute-start | bytes 196616 | tf_op jit(solution)/shard_map/ppermute | solution.py:466
  25.5 0.7 %collective-permute-start.5 = (f32[128,128]{1,0:T(8,128)S(1)}, f32[128,128]{1,0:T(8,128)S(1)}, u32[]{:S(2)}, u32[]{:S(2)}) collective-permute-start(f32[128,128]{1,0:T(8,128)S(1)} %add.67), channel_id=1, source_target_pairs={{0,2},{1,9},{2,4},{3,11},{4,6},{5,13},{6,0},{7,15},{8,10},{9,17},{... | collective-permute-start | bytes 196616 | tf_op jit(solution)/shard_map/ppermute | solution.py:466
  26.3 1.9 %collective-permute-start.4 = (f32[128,128]{1,0:T(8,128)S(1)}, f32[128,128]{1,0:T(8,128)S(1)}, u32[]{:S(2)}, u32[]{:S(2)}) collective-permute-start(f32[128,128]{1,0:T(8,128)S(1)} %add.67), channel_id=1, source_target_pairs={{0,6},{1,25},{2,0},{3,27},{4,2},{5,29},{6,4},{7,31},{8,14},{9,1},{... | collective-permute-start | bytes 196616 | tf_op jit(solution)/shard_map/ppermute | solution.py:466
  28.2 0.0 collective-permute-done.6
  28.2 1.8 %collective-permute-done.5 = f32[128,128]{1,0:T(8,128)S(1)} collective-permute-done((f32[128,128]{1,0:T(8,128)S(1)}, f32[128,128]{1,0:T(8,128)S(1)}, u32[]{:S(2)}, u32[]{:S(2)}) %collective-permute-start.5) | collective-permute-done | bytes 65568 | tf_op jit(solution)/shard_map/ppermute | solution.py:466
  30.0 0.0 collective-permute-done.4
  30.1 2.6 %collective-permute-start.9 = (f32[128,128]{1,0:T(8,128)S(1)}, f32[128,128]{1,0:T(8,128)S(1)}, u32[]{:S(2)}, u32[]{:S(2)}) collective-permute-start(f32[128,128]{1,0:T(8,128)S(1)} %add_add_fusion.1), channel_id=1, source_target_pairs={{0,16},{1,5},{2,18},{3,7},{4,20},{5,1},{6,22},{7,3},{8,24},{9,13},... | collective-permute-start | bytes 196616 | tf_op jit(solution)/shard_map/ppermute | solution.py:466
  32.7 0.6 %collective-permute-start.8 = (f32[128,128]{1,0:T(8,128)S(1)}, f32[128,128]{1,0:T(8,128)S(1)}, u32[]{:S(2)}, u32[]{:S(2)}) collective-permute-start(f32[128,128]{1,0:T(8,128)S(1)} %add_add_fusion.1), channel_id=1, source_target_pairs={{0,8},{1,3},{2,10},{3,5},{4,12},{5,7},{6,14},{7,1},{8,16},{9,11},{... | collective-permute-start | bytes 196616 | tf_op jit(solution)/shard_map/ppermute | solution.py:466
  33.3 2.1 %collective-permute-start.7 = (f32[128,128]{1,0:T(8,128)S(1)}, f32[128,128]{1,0:T(8,128)S(1)}, u32[]{:S(2)}, u32[]{:S(2)}) collective-permute-start(f32[128,128]{1,0:T(8,128)S(1)} %add_add_fusion.1), channel_id=1, source_target_pairs={{0,24},{1,7},{2,26},{3,1},{4,28},{5,3},{6,30},{7,5},{8,0},{9,15},{... | collective-permute-start | bytes 196616 | tf_op jit(solution)/shard_map/ppermute | solution.py:466
  35.4 0.0 collective-permute-done.9
  35.4 1.6 %collective-permute-done.8 = f32[128,128]{1,0:T(8,128)S(1)} collective-permute-done((f32[128,128]{1,0:T(8,128)S(1)}, f32[128,128]{1,0:T(8,128)S(1)}, u32[]{:S(2)}, u32[]{:S(2)}) %collective-permute-start.8) | collective-permute-done | bytes 65568 | tf_op jit(solution)/shard_map/ppermute | solution.py:466
  37.0 0.0 collective-permute-done.7
  37.0 2.4 %factor.1.refs_0_ = f32[4,64,128]{2,1,0:T(8,128)S(1)} custom-call(f32[128,128]{1,0:T(8,128)S(1)} %add_add_fusion.gram), custom_call_target="tpu_custom_call" | custom-call | tf_op jit(solution)/shard_map/factor/pallas_call | solution.py:414
  39.4 3.0 %collective-permute-start.10 = (f32[4,64,128]{2,1,0:T(8,128)S(1)}, f32[4,64,128]{2,1,0:T(8,128)S(1)}, u32[]{:S(2)}, u32[]{:S(2)}) collective-permute-start(f32[4,64,128]{2,1,0:T(8,128)S(1)} %factor.1.refs_0_), channel_id=1, source_target_pairs={{0,1},{1,0},{2,3},{3,2},{4,5},{5,4},{6,7},{7,6},{8,9},{9,8},{10,11... | collective-permute-start | bytes 393224 | tf_op jit(solution)/shard_map/ppermute | solution.py:496
  42.4 1.3 %modes_own.1 = (bf16[2,8,256,128]{3,2,1,0:T(8,128)(2,1)}, f32[2,8,64,64]{3,2,1,0:T(8,128)}) custom-call(f32[4,64,128]{2,1,0:T(8,128)S(1)} %factor.1.refs_0_, bf16[4,256,512]{2,1,0:T(8,128)(2,1)S(1)} %get-tuple-element.23.refs_1_, f32[4,128]{1,0:T(4,128)S(1)} %copy-done), custom_call_target="tpu_custom_call" | custom-call | flops 300000000 | bytes 4194304 | tf_op jit(solution)/shard_map/modes_own/pallas_call | solution.py:427
  43.7 0.0 collective-permute-done.10.refs_0_
  43.7 1.3 %modes_far.1 = (bf16[2,8,256,128]{3,2,1,0:T(8,128)(2,1)}, f32[2,8,64,64]{3,2,1,0:T(8,128)}) custom-call(f32[4,64,128]{2,1,0:T(8,128)S(1)} %collective-permute-done.10.refs_0_, bf16[4,256,512]{2,1,0:T(8,128)(2,1)S(1)} %get-tuple-element.22.refs_1_, f32[4,128]{1,0:T(4,128)S(1)} %copy-done, ...), custom_call_target="tpu_custom_call", output_to_operand_aliasing={{0}: (3, {}), {1}: (4, {})} | custom-call | flops 300000000 | bytes 4194304 | tf_op jit(solution)/shard_map/modes_far/pallas_call | solution.py:427
  (3 shorter events, 0.0 us)
Async XLA Ops:
  1.6 9.6 %collective-permute-start.2 = (bf16[2,2,256,128]{3,2,1,0:T(8,128)(2,1)S(1)}, bf16[2,2,256,128]{3,2,1,0:T(8,128)(2,1)S(1)}, u32[]{:S(2)}, u32[]{:S(2)}) collective-permute-start(bf16[2,2,256,128]{3,2,1,0:T(8,128)(2,1)S(1)} %dynamic-slice_bitcast_fusion.3), channel_id=1, source_target_pairs={{0,64},{32,96},{64,0},{96,32},{1,65},{33,97},{65,1},{97,33},{2,66}... | collective-permute-start | bytes 786440 | tf_op jit(solution)/shard_map/ppermute | solution.py:484
  6.5 11.0 %collective-permute-start.1 = (bf16[2,2,256,128]{3,2,1,0:T(8,128)(2,1)S(1)}, bf16[2,2,256,128]{3,2,1,0:T(8,128)(2,1)S(1)}, u32[]{:S(2)}, u32[]{:S(2)}) collective-permute-start(bf16[2,2,256,128]{3,2,1,0:T(8,128)(2,1)S(1)} %get-tuple-element.30), channel_id=1, source_target_pairs={{0,32},{32,64},{64,96},{96,0},{1,33},{33,65},{65,97},{97,1},{2,34}... | collective-permute-start | bytes 786440 | tf_op jit(solution)/shard_map/ppermute | solution.py:479
  7.0 10.5 %collective-permute-start = (bf16[2,2,256,128]{3,2,1,0:T(8,128)(2,1)S(1)}, bf16[2,2,256,128]{3,2,1,0:T(8,128)(2,1)S(1)}, u32[]{:S(2)}, u32[]{:S(2)}) collective-permute-start(bf16[2,2,256,128]{3,2,1,0:T(8,128)(2,1)S(1)} %get-tuple-element.31), channel_id=1, source_target_pairs={{0,96},{32,0},{64,32},{96,64},{1,97},{33,1},{65,33},{97,65},{2,98}... | collective-permute-start | bytes 786440 | tf_op jit(solution)/shard_map/ppermute | solution.py:479
  9.3 2.9 %copy-start = (f32[4,128]{1,0:T(4,128)S(1)}, f32[4,128]{1,0:T(4,128)}, u32[]{:S(2)}) copy-start(f32[4,128]{1,0:T(4,128)} %refs_2_.3) | copy-start | bytes 6148
  19.3 2.5 %collective-permute-start.3 = (f32[128,128]{1,0:T(8,128)S(1)}, f32[128,128]{1,0:T(8,128)S(1)}, u32[]{:S(2)}, u32[]{:S(2)}) collective-permute-start(f32[128,128]{1,0:T(8,128)S(1)} %get-tuple-element.21), channel_id=1, source_target_pairs={{0,1},{1,0},{2,3},{3,2},{4,5},{5,4},{6,7},{7,6},{8,9},{9,8},{10,11... | collective-permute-start | bytes 196616 | tf_op jit(solution)/shard_map/ppermute | solution.py:492
  21.8 6.4 %collective-permute-start.6 = (f32[128,128]{1,0:T(8,128)S(1)}, f32[128,128]{1,0:T(8,128)S(1)}, u32[]{:S(2)}, u32[]{:S(2)}) collective-permute-start(f32[128,128]{1,0:T(8,128)S(1)} %add.67), channel_id=1, source_target_pairs={{0,4},{1,17},{2,6},{3,19},{4,0},{5,21},{6,2},{7,23},{8,12},{9,25},... | collective-permute-start | bytes 196616 | tf_op jit(solution)/shard_map/ppermute | solution.py:466
  25.5 4.5 %collective-permute-start.5 = (f32[128,128]{1,0:T(8,128)S(1)}, f32[128,128]{1,0:T(8,128)S(1)}, u32[]{:S(2)}, u32[]{:S(2)}) collective-permute-start(f32[128,128]{1,0:T(8,128)S(1)} %add.67), channel_id=1, source_target_pairs={{0,2},{1,9},{2,4},{3,11},{4,6},{5,13},{6,0},{7,15},{8,10},{9,17},{... | collective-permute-start | bytes 196616 | tf_op jit(solution)/shard_map/ppermute | solution.py:466
  26.3 3.8 %collective-permute-start.4 = (f32[128,128]{1,0:T(8,128)S(1)}, f32[128,128]{1,0:T(8,128)S(1)}, u32[]{:S(2)}, u32[]{:S(2)}) collective-permute-start(f32[128,128]{1,0:T(8,128)S(1)} %add.67), channel_id=1, source_target_pairs={{0,6},{1,25},{2,0},{3,27},{4,2},{5,29},{6,4},{7,31},{8,14},{9,1},{... | collective-permute-start | bytes 196616 | tf_op jit(solution)/shard_map/ppermute | solution.py:466
  30.1 5.3 %collective-permute-start.9 = (f32[128,128]{1,0:T(8,128)S(1)}, f32[128,128]{1,0:T(8,128)S(1)}, u32[]{:S(2)}, u32[]{:S(2)}) collective-permute-start(f32[128,128]{1,0:T(8,128)S(1)} %add_add_fusion.1), channel_id=1, source_target_pairs={{0,16},{1,5},{2,18},{3,7},{4,20},{5,1},{6,22},{7,3},{8,24},{9,13},... | collective-permute-start | bytes 196616 | tf_op jit(solution)/shard_map/ppermute | solution.py:466
  32.7 4.3 %collective-permute-start.8 = (f32[128,128]{1,0:T(8,128)S(1)}, f32[128,128]{1,0:T(8,128)S(1)}, u32[]{:S(2)}, u32[]{:S(2)}) collective-permute-start(f32[128,128]{1,0:T(8,128)S(1)} %add_add_fusion.1), channel_id=1, source_target_pairs={{0,8},{1,3},{2,10},{3,5},{4,12},{5,7},{6,14},{7,1},{8,16},{9,11},{... | collective-permute-start | bytes 196616 | tf_op jit(solution)/shard_map/ppermute | solution.py:466
  33.3 3.7 %collective-permute-start.7 = (f32[128,128]{1,0:T(8,128)S(1)}, f32[128,128]{1,0:T(8,128)S(1)}, u32[]{:S(2)}, u32[]{:S(2)}) collective-permute-start(f32[128,128]{1,0:T(8,128)S(1)} %add_add_fusion.1), channel_id=1, source_target_pairs={{0,24},{1,7},{2,26},{3,1},{4,28},{5,3},{6,30},{7,5},{8,0},{9,15},{... | collective-permute-start | bytes 196616 | tf_op jit(solution)/shard_map/ppermute | solution.py:466
  39.4 4.3 %collective-permute-start.10 = (f32[4,64,128]{2,1,0:T(8,128)S(1)}, f32[4,64,128]{2,1,0:T(8,128)S(1)}, u32[]{:S(2)}, u32[]{:S(2)}) collective-permute-start(f32[4,64,128]{2,1,0:T(8,128)S(1)} %factor.1.refs_0_), channel_id=1, source_target_pairs={{0,1},{1,0},{2,3},{3,2},{4,5},{5,4},{6,7},{7,6},{8,9},{9,8},{10,11... | collective-permute-start | bytes 393224 | tf_op jit(solution)/shard_map/ppermute | solution.py:496
